TPU v7x, 128 devices: a whole 4x4x4 slice. The times are simulated.
128 devices in a mesh: leaf: 128 (over x, z, y, core).
Axes of the slice: x: 4, y: 4, z: 4, core: 2. Of those that a mesh axis runs over, the one named last changes fastest.
Arguments:
- points: bfloat16 [1048576, 128], P('leaf'), may hold values from -6 to 6
- leaf_basis: bfloat16 [16384, 64, 32], P('leaf'), may hold values from -0.75 to 0.75
- local_transfer: bfloat16 [32640, 32, 32], P('leaf'), may hold values from -0.75 to 0.75
- top_transfer: bfloat16 [128, 32, 32], replicated, may hold values from -0.75 to 0.75
- local_coupling: bfloat16 [32640, 8, 32, 32], P('leaf'), may hold values from -0.375 to 0.375
- local_lists: int32 [32640, 8], P('leaf'), may hold values from -1 to 16383, as said below
- top_coupling: bfloat16 [128, 8, 32, 32], replicated, may hold values from -0.375 to 0.375
- top_lists: int32 [128, 8], replicated, may hold values from -1 to 127, as said below
- near_blocks: bfloat16 [16384, 6, 64, 64], P('leaf'), may hold values from -0.3125 to 0.3125
- near_lists: int32 [16384, 6], P('leaf'), may hold values from -1 to 16383, as said below
Outputs:
- product: bfloat16 [1048576, 128], P('leaf')
Inputs may be any that keep to these rules, and one draw needn't show every extreme that they name: `local_lists`: space is cut into 128 slabs one leaf box thick, subtree d being slab d; inside a slab the tree halves the cross-section alternately along its two directions, and a node at depth TD + k is a cell of that level's grid. Partners are children of the node's parent's neighbouring cells (in slabs d - 1, d, d + 1) that are not adjacent to the node; they are distinct within a row, and rows at depths TD to TD + 2 are empty. `top_lists`: rows of nodes at depths 0 and 1 are empty; other partners are distinct nodes of the same depth, two or more positions away from the node. `near_lists`: slot 0 is the leaf itself; the others are distinct leaves whose boxes touch the leaf's box, in the leaf's own slab or the slabs beside it.
All inputs are finite; a program needn't handle non-finite values.
Results may differ from a plain program's by a relative error of at most 0.028.
Values may be sent and summed in bfloat16 or wider, within the bound.
No kernel may reach another device: no remote copies, remote signals or barrier semaphores. Data moves between devices by JAX's collectives and lax.ppermute only.
A program may use at most 192 MiB of HBM per device.

v0:
```python
import jax
import jax.numpy as jnp
from jax import lax
from jax.sharding import PartitionSpec as P


def with_halo(shard, sides, width):
    for axis, dim in sides:
        count, length = (lax.axis_size(axis), shard.shape[dim])
        up = [(i, (i + 1) % count) for i in range(count - 1)]
        down = [(j, i) for i, j in up]
        last = lax.slice_in_dim(shard, length - width, length, axis=dim)
        first = lax.slice_in_dim(shard, 0, width, axis=dim)
        before = lax.ppermute(last, axis, up)
        after = lax.ppermute(first, axis, down)
        shard = jnp.concatenate([before, shard, after], axis=dim)
    return shard


def couple(window, blocks, partner_ids, first_node):
    is_valid = partner_ids >= 0
    positions = jnp.where(is_valid, partner_ids - first_node, 0)
    total = jnp.zeros((blocks.shape[0], blocks.shape[2], window.shape[2]), jnp.float32)
    for slot_idx in range(partner_ids.shape[1]):
        picked = window[positions[:, slot_idx]]
        picked = jnp.where(is_valid[:, slot_idx, None, None], picked, jnp.zeros((), window.dtype))
        total = total + jnp.einsum(
            "mrs,msv->mrv", blocks[:, slot_idx], picked, preferred_element_type=jnp.float32
        )
    return total


def shards(
    points,
    leaf_basis,
    local_transfer,
    top_transfer,
    local_coupling,
    local_lists,
    top_coupling,
    top_lists,
    near_blocks,
    near_lists,
):
    leaf_dev, leaf_size, rank_size = leaf_basis.shape
    vec_count = points.shape[1]
    levels_dev = leaf_dev.bit_length() - 1
    device_count = lax.axis_size("leaf")
    top_depth = device_count.bit_length() - 1
    own_index = lax.axis_index("leaf")
    leaf_rows = points.reshape(leaf_dev, leaf_size, vec_count)
    coeffs = [None] * (levels_dev + 1)
    coeffs[levels_dev] = jnp.einsum(
        "lpr,lpv->lrv", leaf_basis, leaf_rows, preferred_element_type=jnp.float32
    ).astype(jnp.bfloat16)
    for depth_now in range(levels_dev - 1, -1, -1):
        lower = 2 ** (depth_now + 1) - 1
        up_terms = jnp.einsum(
            "crs,crv->csv",
            local_transfer[lower : 2 * lower + 1],
            coeffs[depth_now + 1],
            preferred_element_type=jnp.float32,
        )
        coeffs[depth_now] = (
            up_terms.reshape(-1, 2, rank_size, vec_count).sum(axis=1).astype(jnp.bfloat16)
        )
    windows = [None] * (levels_dev + 1)
    for depth_now in range(levels_dev, 2, -1):
        windows[depth_now] = with_halo(
            coeffs[depth_now], (("leaf", 0),), coeffs[depth_now].shape[0]
        )
    root_term = jnp.einsum(
        "rs,rv->sv", local_transfer[0], coeffs[0][0], preferred_element_type=jnp.float32
    )
    gathered = lax.all_gather(root_term[None], "leaf", axis=0, tiled=True)
    top_coeffs = {}
    up_terms = gathered
    for depth_now in range(top_depth - 1, 1, -1):
        level_coeff = up_terms.reshape(-1, 2, rank_size, vec_count).sum(axis=1).astype(jnp.bfloat16)
        top_coeffs[depth_now] = level_coeff
        if depth_now > 2:
            transfers = top_transfer[2**depth_now : 2 ** (depth_now + 1)]
            up_terms = jnp.einsum(
                "crs,crv->csv", transfers, level_coeff, preferred_element_type=jnp.float32
            )
    carried = None
    for depth_now in range(2, top_depth):
        ancestor = (device_count + own_index) // 2 ** (top_depth - depth_now)
        far_now = couple(
            top_coeffs[depth_now],
            top_coupling[ancestor][None],
            top_lists[ancestor][None],
            2**depth_now,
        )[0]
        if carried is None:
            carried = far_now
        else:
            carried = far_now + jnp.dot(
                top_transfer[ancestor],
                carried.astype(jnp.bfloat16),
                preferred_element_type=jnp.float32,
            )
    near_window = with_halo(leaf_rows, (("leaf", 0),), leaf_dev)
    for depth_now in range(levels_dev + 1):
        lower = 2**depth_now - 1
        parents = jnp.repeat(
            carried.astype(jnp.bfloat16).reshape(-1, rank_size, vec_count), 2, axis=0
        )
        if depth_now == 0:
            parents = parents[:1]
        carried = jnp.einsum(
            "crs,csv->crv",
            local_transfer[lower : 2 * lower + 1],
            parents,
            preferred_element_type=jnp.float32,
        )
        if depth_now >= 3:
            first_node = (own_index - 1) * (lower + 1)
            carried = carried + couple(
                windows[depth_now],
                local_coupling[lower : 2 * lower + 1],
                local_lists[lower : 2 * lower + 1],
                first_node,
            )
    far_rows = jnp.einsum(
        "lpr,lrv->lpv", leaf_basis, carried.astype(jnp.bfloat16), preferred_element_type=jnp.float32
    )
    first_leaf = (own_index - 1) * leaf_dev
    near_rows = couple(near_window, near_blocks, near_lists, first_leaf)
    return (far_rows + near_rows).astype(jnp.bfloat16).reshape(leaf_dev * leaf_size, vec_count)


def solution(mesh):
    return jax.shard_map(
        shards,
        mesh=mesh,
        in_specs=(
            P("leaf", None),
            P("leaf", None, None),
            P("leaf", None, None),
            P(),
            P("leaf", None, None, None),
            P("leaf", None),
            P(),
            P(),
            P("leaf", None, None, None),
            P("leaf", None),
        ),
        out_specs=P("leaf", None),
        check_vma=False,
    )
```

profile of v0, /device:TPU:6, one launch (start us, length us, event | category | flops | bytes accessed | tf_op | source)
XLA Modules:
  0.0 633.1 jit_solution(14000777045308287244)
XLA Ops:
  26.8 8.1 %collective-permute-start.1 = (bf16[8,32,128]{2,1,0:T(8,128)(2,1)}, bf16[8,32,128]{2,1,0:T(8,128)(2,1)}, u32[]{:S(2)}, u32[]{:S(2)}) collective-permute-start(bf16[8,32,128]{2,1,0:T(8,128)(2,1)} %bitcast_reduce_fusion.6), channel_id=1, source_target_pairs={{1,0},{2,1},{3,2},{4,3},{5,4},{6,5},{7,6},{8,7},{9,8},{10,9},{11,1... | collective-permute-start | bytes 196616 | tf_op jit(solution)/shard_map/ppermute | solution.py:15
  36.8 7.9 %collective-permute-start.3 = (bf16[16,32,128]{2,1,0:T(8,128)(2,1)}, bf16[16,32,128]{2,1,0:T(8,128)(2,1)}, u32[]{:S(2)}, u32[]{:S(2)}) collective-permute-start(bf16[16,32,128]{2,1,0:T(8,128)(2,1)} %bitcast_reduce_fusion.4), channel_id=1, source_target_pairs={{1,0},{2,1},{3,2},{4,3},{5,4},{6,5},{7,6},{8,7},{9,8},{10,9},{11,1... | collective-permute-start | bytes 393224 | tf_op jit(solution)/shard_map/ppermute | solution.py:15
  120.9 7.0 %constant_dynamic-slice_fusion.76 = (bf16[1,1,32,32]{0,3,2,1:T(8,128)(2,1)}, bf16[1,1,32,32]{0,3,2,1:T(8,128)(2,1)}, bf16[1,1,32,32]{0,3,2,1:T(8,128)(2,1)}, bf1...) fusion(bf16[128,8,32,32]{0,3,2,1:T(8,128)(2,1)S(1)} %copy-done,, ...), kind=kLoop, calls=%fused_computation.444 | loop fusion | bytes 163888 | tf_op jit(solution)/shard_map/slice | solution.py:28
  278.5 6.5 %fusion.639 = (bf16[128,1,64,64]{0,3,2,1:T(8,128)(2,1)S(1)}, bf16[128,1,64,64]{0,3,2,1:T(8,128)(2,1)}, bf16[128,1,64,64]{0,3,2,1:T(8,128)(2,1)}, bf16[128,1,64,6...) fusion(bf16[128,6,64,64]{0,3,2,1:T(8,128)(2,1)} %param.18), kind=kLoop, calls=%fused_computation.962 | loop fusion | bytes 12582912 | tf_op jit(solution)/shard_map/slice | solution.py:28
  285.0 4.6 copy.243
  292.4 4.7 copy.242
  298.3 4.7 copy.241
  304.2 4.7 copy.240
  310.1 3.8 copy.239
  314.0 3.8 copy.244
  358.2 7.9 %collective-permute-start.5 = (bf16[32,32,128]{2,1,0:T(8,128)(2,1)S(1)}, bf16[32,32,128]{2,1,0:T(8,128)(2,1)}, u32[]{:S(2)}, u32[]{:S(2)}) collective-permute-start(bf16[32,32,128]{2,1,0:T(8,128)(2,1)S(1)} %bitcast_reduce_fusion.2), channel_id=1, source_target_pairs={{1,0},{2,1},{3,2},{4,3},{5,4},{6,5},{7,6},{8,7},{9,8},{10,9},{11,1... | collective-permute-start | bytes 786440 | tf_op jit(solution)/shard_map/ppermute | solution.py:15
  377.7 8.0 %collective-permute-start.7 = (bf16[64,32,128]{2,1,0:T(8,128)(2,1)S(1)}, bf16[64,32,128]{2,1,0:T(8,128)(2,1)}, u32[]{:S(2)}, u32[]{:S(2)}) collective-permute-start(bf16[64,32,128]{2,1,0:T(8,128)(2,1)S(1)} %copy-done.21), channel_id=1, source_target_pairs={{1,0},{2,1},{3,2},{4,3},{5,4},{6,5},{7,6},{8,7},{9,8},{10,9},{11,1... | collective-permute-start | bytes 1572872 | tf_op jit(solution)/shard_map/ppermute | solution.py:15
  405.0 7.9 %collective-permute-start.9 = (bf16[128,32,128]{2,1,0:T(8,128)(2,1)S(1)}, bf16[128,32,128]{2,1,0:T(8,128)(2,1)}, u32[]{:S(2)}, u32[]{:S(2)}) collective-permute-start(bf16[128,32,128]{2,1,0:T(8,128)(2,1)S(1)} %convolution_convert_fusion), channel_id=1, source_target_pairs={{1,0},{2,1},{3,2},{4,3},{5,4},{6,5},{7,6},{8,7},{9,8},{10,9},{11,1... | collective-permute-start | bytes 3145736 | tf_op jit(solution)/shard_map/ppermute | solution.py:15
  430.2 7.9 %collective-permute-start.11 = (bf16[128,64,128]{2,1,0:T(8,128)(2,1)}, bf16[128,64,128]{2,1,0:T(8,128)(2,1)}, u32[]{:S(2)}, u32[]{:S(2)}) collective-permute-start(bf16[128,64,128]{2,1,0:T(8,128)(2,1)} %bitcast.2), channel_id=1, source_target_pairs={{1,0},{2,1},{3,2},{4,3},{5,4},{6,5},{7,6},{8,7},{9,8},{10,9},{11,1... | collective-permute-start | bytes 6291464 | tf_op jit(solution)/shard_map/ppermute | solution.py:15
  496.5 6.3 %pad_maximum_fusion = bf16[384,64,128]{2,1,0:T(8,128)(2,1)} fusion(bf16[128,64,128]{2,1,0:T(8,128)(2,1)} %collective-permute-done.11, bf16[128,64,128]{2,1,0:T(8,128)(2,1)} %bitcast.2, bf16[128,64,128]{2,1,0:T(8,128)(2,1)} %collective-permute-done.10), kind=kLoop, calls=%fused_computation.46 | loop fusion | flops 6291456 | bytes 12582912 | tf_op jit(solution)/shard_map/concatenate | solution.py:16
  502.8 5.1 gather_fusion.44
  507.9 5.0 gather_fusion.43
  512.9 5.0 gather_fusion.42
  518.0 5.1 gather_fusion.41
  523.0 5.0 gather_fusion.40
  528.0 5.2 gather_fusion.45
  533.3 4.5 fusion.1
  604.0 10.4 %fusion.23 = f32[128,128,64]{1,2,0:T(8,128)} fusion(bf16[128,64,32]{1,2,0:T(8,128)(2,1)S(1)} %copy-done.8, f32[128,128,32]{1,2,0:T(8,128)} %fusion.658, f32[128,128,32]{1,2,0:T(8,128)} %fusion.61, f32[128,128,32]{1,2,0:T(8,128)} %fusion.63, f32[128,128,32]{1,2,0:T(8,128)} %fusion.65, f32[128,128,32]{1,2,0:T(8,128)} %fusion.67, f32[128,128,32]{1,2,0:T(8,128)} %fusion.69, ...), kind=kOutput, calls=%fused_computation.74 | convolution fusion | flops 105906176 | bytes 22806656 | tf_op jit(solution)/shard_map/lpr,lrv->lpv/dot_general | solution.py:125
  614.3 11.7 %add_convert_fusion = bf16[128,128,64]{1,2,0:T(8,128)(2,1)} fusion(f32[128,128,64]{1,2,0:T(8,128)} %fusion.23, f32[128,128,64]{1,2,0:T(8,128)} %fusion.1, f32[128,128,64]{1,2,0:T(8,128)} %fusion.3, f32[128,128,64]{1,2,0:T(8,128)} %fusion.5, f32[128,128,64]{1,2,0:T(8,128)} %fusion.9, f32[128,128,64]{1,2,0:T(8,128)} %fusion.7, ...), kind=kOutput, calls=%fused_computation.47 | convolution fusion | flops 142606336 | bytes 30408832 | tf_op jit(solution)/shard_map/mrs,msv->mrv/dot_general | solution.py:27
  (816 shorter events, 389.9 us)
Async XLA Ops:
  6.5 544.1 %all-gather.3.cloned.1.call-start = ((), (), s32[]{:S(2)}) async-start(), calls=%async_computation | async-start | bytes 2113536 | tf_op jit(solution)/shard_map/all_gather | solution.py:75
  20.0 385.0 %copy-start.5 = (bf16[128,32,128]{2,1,0:T(8,128)(2,1)}, bf16[128,32,128]{2,1,0:T(8,128)(2,1)S(1)}, u32[]{:S(2)}) copy-start(bf16[128,32,128]{2,1,0:T(8,128)(2,1)S(1)} %convolution_convert_fusion) | copy-start | bytes 3145732
  24.9 333.3 %collective-permute-start = (bf16[8,32,128]{2,1,0:T(8,128)(2,1)}, bf16[8,32,128]{2,1,0:T(8,128)(2,1)}, u32[]{:S(2)}, u32[]{:S(2)}) collective-permute-start(bf16[8,32,128]{2,1,0:T(8,128)(2,1)} %bitcast_reduce_fusion.6), channel_id=1, source_target_pairs={{0,1},{1,2},{2,3},{3,4},{4,5},{5,6},{6,7},{7,8},{8,9},{9,10},{10,1... | collective-permute-start | bytes 196616 | tf_op jit(solution)/shard_map/ppermute | solution.py:14
  26.8 339.3 %collective-permute-start.1 = (bf16[8,32,128]{2,1,0:T(8,128)(2,1)}, bf16[8,32,128]{2,1,0:T(8,128)(2,1)}, u32[]{:S(2)}, u32[]{:S(2)}) collective-permute-start(bf16[8,32,128]{2,1,0:T(8,128)(2,1)} %bitcast_reduce_fusion.6), channel_id=1, source_target_pairs={{1,0},{2,1},{3,2},{4,3},{5,4},{6,5},{7,6},{8,7},{9,8},{10,9},{11,1... | collective-permute-start | bytes 196616 | tf_op jit(solution)/shard_map/ppermute | solution.py:15
  34.9 342.8 %collective-permute-start.2 = (bf16[16,32,128]{2,1,0:T(8,128)(2,1)}, bf16[16,32,128]{2,1,0:T(8,128)(2,1)}, u32[]{:S(2)}, u32[]{:S(2)}) collective-permute-start(bf16[16,32,128]{2,1,0:T(8,128)(2,1)} %bitcast_reduce_fusion.4), channel_id=1, source_target_pairs={{0,1},{1,2},{2,3},{3,4},{4,5},{5,6},{6,7},{7,8},{8,9},{9,10},{10,1... | collective-permute-start | bytes 393224 | tf_op jit(solution)/shard_map/ppermute | solution.py:14
  36.8 348.8 %collective-permute-start.3 = (bf16[16,32,128]{2,1,0:T(8,128)(2,1)}, bf16[16,32,128]{2,1,0:T(8,128)(2,1)}, u32[]{:S(2)}, u32[]{:S(2)}) collective-permute-start(bf16[16,32,128]{2,1,0:T(8,128)(2,1)} %bitcast_reduce_fusion.4), channel_id=1, source_target_pairs={{1,0},{2,1},{3,2},{4,3},{5,4},{6,5},{7,6},{8,7},{9,8},{10,9},{11,1... | collective-permute-start | bytes 393224 | tf_op jit(solution)/shard_map/ppermute | solution.py:15
  44.7 360.3 %collective-permute-start.4 = (bf16[32,32,128]{2,1,0:T(8,128)(2,1)S(1)}, bf16[32,32,128]{2,1,0:T(8,128)(2,1)}, u32[]{:S(2)}, u32[]{:S(2)}) collective-permute-start(bf16[32,32,128]{2,1,0:T(8,128)(2,1)S(1)} %bitcast_reduce_fusion.2), channel_id=1, source_target_pairs={{0,1},{1,2},{2,3},{3,4},{4,5},{5,6},{6,7},{7,8},{8,9},{9,10},{10,1... | collective-permute-start | bytes 786440 | tf_op jit(solution)/shard_map/ppermute | solution.py:14
  314.0 60.1 %copy-start.149 = (bf16[8,1,32,32]{3,2,0,1:T(8,128)(2,1)S(1)}, bf16[8,1,32,32]{3,2,0,1:T(8,128)(2,1)}, u32[]{:S(2)}) copy-start(bf16[8,1,32,32]{3,2,0,1:T(8,128)(2,1)} %copy.208) | copy-start | bytes 49156
  314.0 60.9 %copy-start.148 = (bf16[8,1,32,32]{3,2,0,1:T(8,128)(2,1)S(1)}, bf16[8,1,32,32]{3,2,0,1:T(8,128)(2,1)}, u32[]{:S(2)}) copy-start(bf16[8,1,32,32]{3,2,0,1:T(8,128)(2,1)} %copy.207) | copy-start | bytes 49156
  314.0 61.8 %copy-start.147 = (bf16[8,1,32,32]{3,2,0,1:T(8,128)(2,1)S(1)}, bf16[8,1,32,32]{3,2,0,1:T(8,128)(2,1)}, u32[]{:S(2)}) copy-start(bf16[8,1,32,32]{3,2,0,1:T(8,128)(2,1)} %copy.209) | copy-start | bytes 49156
  317.8 58.3 %copy-start.219 = (pred[8]{0:T(512)(128)(4,1)S(1)}, pred[8]{0:T(512)(128)(4,1)}, u32[]{:S(2)}) copy-start(pred[8]{0:T(512)(128)(4,1)} %get-tuple-element.691) | copy-start | bytes 28
  317.8 58.5 %copy-start.145 = (bf16[8,1,32,32]{3,2,0,1:T(8,128)(2,1)S(1)}, bf16[8,1,32,32]{3,2,0,1:T(8,128)(2,1)}, u32[]{:S(2)}) copy-start(bf16[8,1,32,32]{3,2,0,1:T(8,128)(2,1)} %copy.211) | copy-start | bytes 49156
  317.8 58.5 %copy-start.218 = (pred[8]{0:T(512)(128)(4,1)S(1)}, pred[8]{0:T(512)(128)(4,1)}, u32[]{:S(2)}) copy-start(pred[8]{0:T(512)(128)(4,1)} %get-tuple-element.690) | copy-start | bytes 28
  317.8 58.7 %copy-start.144 = (bf16[8,1,32,32]{3,2,0,1:T(8,128)(2,1)S(1)}, bf16[8,1,32,32]{3,2,0,1:T(8,128)(2,1)}, u32[]{:S(2)}) copy-start(bf16[8,1,32,32]{3,2,0,1:T(8,128)(2,1)} %copy.212) | copy-start | bytes 49156
  317.8 58.7 %copy-start.217 = (pred[8]{0:T(512)(128)(4,1)S(1)}, pred[8]{0:T(512)(128)(4,1)}, u32[]{:S(2)}) copy-start(pred[8]{0:T(512)(128)(4,1)} %get-tuple-element.689) | copy-start | bytes 28
  317.8 59.0 %copy-start.143 = (bf16[8,1,32,32]{3,2,0,1:T(8,128)(2,1)S(1)}, bf16[8,1,32,32]{3,2,0,1:T(8,128)(2,1)}, u32[]{:S(2)}) copy-start(bf16[8,1,32,32]{3,2,0,1:T(8,128)(2,1)} %copy.213) | copy-start | bytes 49156
  317.8 59.0 %copy-start.216 = (pred[8]{0:T(512)(128)(4,1)S(1)}, pred[8]{0:T(512)(128)(4,1)}, u32[]{:S(2)}) copy-start(pred[8]{0:T(512)(128)(4,1)} %get-tuple-element.688) | copy-start | bytes 28
  358.2 54.7 %collective-permute-start.5 = (bf16[32,32,128]{2,1,0:T(8,128)(2,1)S(1)}, bf16[32,32,128]{2,1,0:T(8,128)(2,1)}, u32[]{:S(2)}, u32[]{:S(2)}) collective-permute-start(bf16[32,32,128]{2,1,0:T(8,128)(2,1)S(1)} %bitcast_reduce_fusion.2), channel_id=1, source_target_pairs={{1,0},{2,1},{3,2},{4,3},{5,4},{6,5},{7,6},{8,7},{9,8},{10,9},{11,1... | collective-permute-start | bytes 786440 | tf_op jit(solution)/shard_map/ppermute | solution.py:15
  366.1 64.1 %collective-permute-start.6 = (bf16[64,32,128]{2,1,0:T(8,128)(2,1)S(1)}, bf16[64,32,128]{2,1,0:T(8,128)(2,1)}, u32[]{:S(2)}, u32[]{:S(2)}) collective-permute-start(bf16[64,32,128]{2,1,0:T(8,128)(2,1)S(1)} %copy-done.21), channel_id=1, source_target_pairs={{0,1},{1,2},{2,3},{3,4},{4,5},{5,6},{6,7},{7,8},{8,9},{9,10},{10,1... | collective-permute-start | bytes 1572872 | tf_op jit(solution)/shard_map/ppermute | solution.py:14
  377.7 60.4 %collective-permute-start.7 = (bf16[64,32,128]{2,1,0:T(8,128)(2,1)S(1)}, bf16[64,32,128]{2,1,0:T(8,128)(2,1)}, u32[]{:S(2)}, u32[]{:S(2)}) collective-permute-start(bf16[64,32,128]{2,1,0:T(8,128)(2,1)S(1)} %copy-done.21), channel_id=1, source_target_pairs={{1,0},{2,1},{3,2},{4,3},{5,4},{6,5},{7,6},{8,7},{9,8},{10,9},{11,1... | collective-permute-start | bytes 1572872 | tf_op jit(solution)/shard_map/ppermute | solution.py:15
  385.7 77.3 %collective-permute-start.8 = (bf16[128,32,128]{2,1,0:T(8,128)(2,1)S(1)}, bf16[128,32,128]{2,1,0:T(8,128)(2,1)}, u32[]{:S(2)}, u32[]{:S(2)}) collective-permute-start(bf16[128,32,128]{2,1,0:T(8,128)(2,1)S(1)} %convolution_convert_fusion), channel_id=1, source_target_pairs={{0,1},{1,2},{2,3},{3,4},{4,5},{5,6},{6,7},{7,8},{8,9},{9,10},{10,1... | collective-permute-start | bytes 3145736 | tf_op jit(solution)/shard_map/ppermute | solution.py:14
  405.0 57.9 %collective-permute-start.9 = (bf16[128,32,128]{2,1,0:T(8,128)(2,1)S(1)}, bf16[128,32,128]{2,1,0:T(8,128)(2,1)}, u32[]{:S(2)}, u32[]{:S(2)}) collective-permute-start(bf16[128,32,128]{2,1,0:T(8,128)(2,1)S(1)} %convolution_convert_fusion), channel_id=1, source_target_pairs={{1,0},{2,1},{3,2},{4,3},{5,4},{6,5},{7,6},{8,7},{9,8},{10,9},{11,1... | collective-permute-start | bytes 3145736 | tf_op jit(solution)/shard_map/ppermute | solution.py:15
  412.9 83.6 %collective-permute-start.10 = (bf16[128,64,128]{2,1,0:T(8,128)(2,1)}, bf16[128,64,128]{2,1,0:T(8,128)(2,1)}, u32[]{:S(2)}, u32[]{:S(2)}) collective-permute-start(bf16[128,64,128]{2,1,0:T(8,128)(2,1)} %bitcast.2), channel_id=1, source_target_pairs={{0,1},{1,2},{2,3},{3,4},{4,5},{5,6},{6,7},{7,8},{8,9},{9,10},{10,1... | collective-permute-start | bytes 6291464 | tf_op jit(solution)/shard_map/ppermute | solution.py:14
  430.2 66.3 %collective-permute-start.11 = (bf16[128,64,128]{2,1,0:T(8,128)(2,1)}, bf16[128,64,128]{2,1,0:T(8,128)(2,1)}, u32[]{:S(2)}, u32[]{:S(2)}) collective-permute-start(bf16[128,64,128]{2,1,0:T(8,128)(2,1)} %bitcast.2), channel_id=1, source_target_pairs={{1,0},{2,1},{3,2},{4,3},{5,4},{6,5},{7,6},{8,7},{9,8},{10,9},{11,1... | collective-permute-start | bytes 6291464 | tf_op jit(solution)/shard_map/ppermute | solution.py:15
  (224 other events, 3307.1 us)
Sparse Core Ops, SparseCore 0:
  50.8 64.8 all-gather.2
where the time goes:
time: 644 us; the launch traced here: 633 us
  local copies, waits for them, and re-layouts  297 us (46%)
  matrix products  137 us (21%)
  between operations  92.6 us (14%)
  starting transfers between devices  59.6 us (9%)
  other arithmetic  47.3 us (7%)
    unnamed x563, local copies, waits for them, and re-layouts  152 us
    dot_general x84, matrix products, couple(): jnp.einsum('mrs,msv->mrv', blocks[:, slot_idx], picked, preferred_element...  111 us
    gather x46, local copies, waits for them, and re-layouts, couple(): picked = window[positions[:, slot_idx]]  79.6 us
    ppermute x6, starting transfers between devices, with_halo(): after = lax.ppermute(first, axis, down)  47.5 us
    gather x30, other arithmetic, couple(): picked = window[positions[:, slot_idx]]  23.6 us
    slice x6, local copies, waits for them, and re-layouts, couple(): blocks[:, slot_idx]  23.2 us
    squeeze x9, local copies, waits for them, and re-layouts, couple(): blocks[:, slot_idx]  23.1 us
  transfers between devices with their start and end apart: 13, of which 0 were waited for; matrix products, arithmetic and copies ran while one was open for 61% of the time, Pallas kernels for 0%

commit v1 on v0

v1 whole, which is shorter than its diff:
```python
import jax
import jax.numpy as jnp
import numpy as np
from jax import lax
from jax.experimental import pallas as pl
from jax.experimental.pallas import tpu as pltpu
from jax.sharding import PartitionSpec as P

BF = jnp.bfloat16
F32 = jnp.float32
NT = (((1,), (1,)), ((), ()))
NN = (((1,), (0,)), ((), ()))
TN = (((0,), (0,)), ((), ()))


def dot(a, b, dims=NN):
    return lax.dot_general(a, b, dims, preferred_element_type=F32)


def eye(rows, cols):
    return (lax.broadcasted_iota(jnp.int32, (rows, cols), 0)
            == lax.broadcasted_iota(jnp.int32, (rows, cols), 1)).astype(BF)


def steps(count, width, body):
    def trip(t, carry):
        for u in range(width):
            body(t * width + u)
        return carry
    lax.fori_loop(0, count // width, trip, 0)


def near_prep_kernel(blocks, out, wide):
    slots, rows, cols, leaves = blocks.shape
    ident = eye(leaves, leaves)
    chunks = slots * cols // 128

    def turn(r):
        both = blocks[:, r].reshape(slots * cols, leaves)
        turned = dot(ident, both, NT)
        for j in range(chunks):
            wide[j, pl.ds(pl.multiple_of(r * leaves, leaves), leaves), :] = turned[:, j * 128:(j + 1) * 128]

    steps(rows, 4, turn)

    def pick(leaf):
        parts = [wide[j, pl.ds(leaf, rows, stride=leaves), :].astype(BF) for j in range(chunks)]
        for j in range(chunks):
            out[leaf, :, j * 128:(j + 1) * 128] = parts[j]

    steps(leaves, 8, pick)


def near_prep(blocks_t, part=16):
    slots, rows, cols, leaves = blocks_t.shape
    width = slots * cols
    return pl.pallas_call(
        near_prep_kernel,
        grid=(rows // part,),
        in_specs=[pl.BlockSpec((slots, part, cols, leaves), lambda i: (0, i, 0, 0))],
        out_specs=pl.BlockSpec((leaves, part, width), lambda i: (0, i, 0)),
        out_shape=jax.ShapeDtypeStruct((leaves, rows, width), BF),
        scratch_shapes=[pltpu.VMEM((width // 128, part * leaves, 128), F32)],
        compiler_params=pltpu.CompilerParams(vmem_limit_bytes=40 << 20),
        name="near_prep",
    )(blocks_t)


def coup_prep_kernel(blocks, out, wide):
    slots, rows, cols, nodes = blocks.shape
    padded = out.shape[0]
    ident = eye(padded, nodes)
    chunks = slots * cols // 128

    def turn(r):
        both = blocks[:, r].reshape(slots * cols, nodes)
        turned = dot(ident, both, NT)
        for j in range(chunks):
            wide[j, pl.ds(pl.multiple_of(r * padded, padded), padded), :] = turned[:, j * 128:(j + 1) * 128]

    steps(rows, 4, turn)

    def pick(node):
        for j in range(chunks):
            out[node, :, j * 128:(j + 1) * 128] = wide[j, pl.ds(node, rows, stride=padded), :].astype(BF)

    steps(padded, 8, pick)


def coup_prep(blocks_t, part=16):
    slots, rows, cols, nodes = blocks_t.shape
    width = slots * cols
    padded = (nodes + 7) // 8 * 8
    return pl.pallas_call(
        coup_prep_kernel,
        grid=(rows // part,),
        in_specs=[pl.BlockSpec((slots, part, cols, nodes), lambda i: (0, i, 0, 0))],
        out_specs=pl.BlockSpec((padded, part, width), lambda i: (0, i, 0)),
        out_shape=jax.ShapeDtypeStruct((padded, rows, width), BF),
        scratch_shapes=[pltpu.VMEM((width // 128, part * padded, 128), F32)],
        compiler_params=pltpu.CompilerParams(vmem_limit_bytes=40 << 20),
        name="coup_prep",
    )(blocks_t)


def upward_kernel(points, basis, transfer, coeff, root, basis_out, transfer_out, wide_b, wide_e):
    size, rank, leaves = basis.shape
    nodes = transfer.shape[2]
    padded = nodes + 1
    ident = eye(leaves, leaves)
    ident_e = eye(padded, nodes)

    def turn_b(p):
        wide_b[pl.ds(pl.multiple_of(p * leaves, leaves), leaves), 0:rank] = dot(ident, basis[p], NT)

    steps(size, 8, turn_b)

    def turn_e(r):
        wide_e[pl.ds(pl.multiple_of(r * padded, padded), padded), 0:rank] = dot(ident_e, transfer[r], NT)

    steps(rank, 4, turn_e)

    def leaf_step(leaf):
        mine = wide_b[pl.ds(leaf, size, stride=leaves), :].astype(BF)[:, 0:rank]
        basis_out[leaf] = mine
        x = points[pl.ds(pl.multiple_of(leaf * size, size), size), :]
        at = pl.multiple_of((leaves - 1 + leaf) * rank, rank)
        coeff[pl.ds(at, rank), :] = dot(mine, x, TN).astype(BF)

    steps(leaves, 8, leaf_step)

    def e_of(node):
        mine = wide_e[pl.ds(node, rank, stride=padded), :].astype(BF)[:, 0:rank]
        transfer_out[node] = mine
        return mine

    count = leaves // 2
    while count >= 1:
        def node_step(p, count=count):
            left = 2 * count - 1 + 2 * p
            both = jnp.concatenate([e_of(left), e_of(left + 1)], axis=0)
            kids = coeff[pl.ds(pl.multiple_of(left * rank, rank), 2 * rank), :]
            at = pl.multiple_of((count - 1 + p) * rank, rank)
            coeff[pl.ds(at, rank), :] = dot(both, kids, TN).astype(BF)
        steps(count, min(count, 8), node_step)
        count //= 2
    root[...] = dot(e_of(0), coeff[0:rank, :], TN)
    coeff[pl.ds(nodes * rank, rank), :] = jnp.zeros((rank, coeff.shape[1]), BF)


def upward(points, basis_t, transfer_t):
    size, rank, leaves = basis_t.shape
    padded = transfer_t.shape[2] + 1
    vecs = points.shape[1]
    return pl.pallas_call(
        upward_kernel,
        out_shape=(
            jax.ShapeDtypeStruct((padded * rank, vecs), BF),
            jax.ShapeDtypeStruct((rank, vecs), F32),
            jax.ShapeDtypeStruct((leaves, size, rank), BF),
            jax.ShapeDtypeStruct((padded, rank, rank), BF),
        ),
        scratch_shapes=[pltpu.VMEM((size * leaves, 128), F32), pltpu.VMEM((rank * padded, 128), F32)],
        compiler_params=pltpu.CompilerParams(vmem_limit_bytes=48 << 20),
        name="upward",
    )(points, basis_t, transfer_t)


def near_kernel(pos, lhs, own, mate, other, out, window, sems):
    i = pl.program_id(0)
    part, size, width = lhs.shape
    slots = width // size
    rows = own.shape[0]

    @pl.when(i == 0)
    def _():
        copies = [pltpu.make_async_copy(src, window.at[pl.ds(n * rows, rows)], sems.at[n])
                  for n, src in enumerate((own, mate, other))]
        for c in copies:
            c.start()
        window[3 * rows:3 * rows + size, :] = jnp.zeros((size, window.shape[1]), BF)
        for c in copies:
            c.wait()

    def leaf_step(l):
        leaf = i * part + l
        rhs = jnp.concatenate(
            [window[pl.ds(pl.multiple_of(pos[s, leaf] * size, size), size), :] for s in range(slots)], axis=0)
        out[pl.ds(pl.multiple_of(l * size, size), size), :] = dot(lhs[l], rhs)

    steps(part, 8, leaf_step)


def near(pos, lhs, own, mate, other, part=32):
    leaves, size, width = lhs.shape
    rows, vecs = own.shape
    any_ = pl.BlockSpec(memory_space=pl.ANY)
    return pl.pallas_call(
        near_kernel,
        grid_spec=pltpu.PrefetchScalarGridSpec(
            num_scalar_prefetch=1,
            grid=(leaves // part,),
            in_specs=[pl.BlockSpec((part, size, width), lambda i, p: (i, 0, 0)), any_, any_, any_],
            out_specs=pl.BlockSpec((part * size, vecs), lambda i, p: (i, 0)),
            scratch_shapes=[pltpu.VMEM((3 * rows + size, vecs), BF), pltpu.SemaphoreType.DMA((3,))],
        ),
        out_shape=jax.ShapeDtypeStruct((rows, vecs), F32),
        compiler_params=pltpu.CompilerParams(vmem_limit_bytes=40 << 20),
        name="near",
    )(pos, lhs, own, mate, other)


def final_kernel(pos, lhs, own, mate, other, transfer, basis, above, near_rows, out, window, far, down, sems):
    rank = transfer.shape[1]
    leaves, size, _ = basis.shape
    slots = lhs.shape[2] // rank
    first = 7
    rows = (2 * leaves - 1 - first) * rank
    copies = [pltpu.make_async_copy(src.at[pl.ds(first * rank, rows)], window.at[pl.ds(n * rows, rows)], sems.at[n])
              for n, src in enumerate((own, mate, other))]
    for c in copies:
        c.start()
    window[3 * rows:3 * rows + rank, :] = jnp.zeros((rank, window.shape[1]), BF)
    for c in copies:
        c.wait()

    def couple(n):
        node = n + first
        rhs = jnp.concatenate(
            [window[pl.ds(pl.multiple_of(pos[s, node] * rank, rank), rank), :] for s in range(slots)], axis=0)
        far[pl.ds(pl.multiple_of(n * rank, rank), rank), :] = dot(lhs[node], rhs)

    steps(2 * leaves - 1 - first, 8, couple)

    down[0:rank, :] = dot(transfer[0], above[...].astype(BF)).astype(BF)
    count = 2
    while count < leaves:
        def node_step(p, count=count):
            node = count - 1 + p
            parent = (node - 1) // 2 if isinstance(node, int) else lax.shift_right_logical(node - 1, 1)
            got = dot(transfer[node], down[pl.ds(pl.multiple_of(parent * rank, rank), rank), :])
            if count >= 8:
                got = got + far[pl.ds(pl.multiple_of((node - first) * rank, rank), rank), :]
            down[pl.ds(pl.multiple_of(node * rank, rank), rank), :] = got.astype(BF)
        steps(count, min(count, 8), node_step)
        count *= 2

    def leaf_step(leaf):
        node = leaves - 1 + leaf
        parent = lax.shift_right_logical(node - 1, 1)
        got = dot(transfer[node], down[pl.ds(pl.multiple_of(parent * rank, rank), rank), :])
        got = got + far[pl.ds(pl.multiple_of((node - first) * rank, rank), rank), :]
        at = pl.ds(pl.multiple_of(leaf * size, size), size)
        out[at, :] = (dot(basis[leaf], got.astype(BF)) + near_rows[at, :]).astype(BF)

    steps(leaves, 8, leaf_step)


def final(pos, lhs, own, mate, other, transfer, basis, above, near_rows):
    leaves, size, rank = basis.shape
    vecs = own.shape[1]
    any_ = pl.BlockSpec(memory_space=pl.ANY)
    vm = pl.BlockSpec(memory_space=pltpu.VMEM)
    rows = (2 * leaves - 8) * rank
    return pl.pallas_call(
        final_kernel,
        in_specs=[pl.BlockSpec(memory_space=pltpu.SMEM), vm, any_, any_, any_, vm, vm, vm, vm],
        out_shape=jax.ShapeDtypeStruct((leaves * size, vecs), BF),
        scratch_shapes=[
            pltpu.VMEM((3 * rows + rank, vecs), BF),
            pltpu.VMEM((rows, vecs), F32),
            pltpu.VMEM(((leaves - 1) * rank, vecs), BF),
            pltpu.SemaphoreType.DMA((3,)),
        ],
        compiler_params=pltpu.CompilerParams(vmem_limit_bytes=56 << 20),
        name="final",
    )(pos, lhs, own, mate, other, transfer, basis, above, near_rows)


def top_kernel(where_am_i, lists, gathered, transfer, coupling, out, wide_e, wide_c, coeff):
    rank, _, nodes = transfer.shape
    slots = coupling.shape[0]
    chips = nodes // 2
    me = where_am_i[0]
    depths = nodes.bit_length() - 1
    ident = eye(nodes, nodes)
    row = lax.broadcasted_iota(jnp.int32, (8, nodes), 0)
    lane = lax.broadcasted_iota(jnp.int32, (8, nodes), 1)
    ancestor = lax.shift_right_logical(nodes + me, jnp.maximum(depths - 2 - row, 0))
    picks = ((lane == ancestor) & (row < depths - 2)).astype(BF)

    def turn(r):
        wide_e[pl.ds(pl.multiple_of(r * nodes, nodes), nodes), 0:rank] = dot(ident, transfer[r], NT)
        both = coupling[:, r].reshape(slots * rank, nodes)
        turned = dot(picks, both, NT)
        for j in range(2):
            wide_c[j, pl.ds(pl.multiple_of(r * 8, 8), 8), :] = turned[:, j * 128:(j + 1) * 128]

    steps(rank, 4, turn)
    coeff[0:rank, :] = jnp.zeros((rank, coeff.shape[1]), BF)

    def place(q):
        seen = q ^ lax.shift_right_logical(me, 1)
        coeff[pl.ds(pl.multiple_of((chips + q) * rank, rank), rank), :] = (
            gathered[pl.ds(pl.multiple_of(seen * rank, rank), rank), :])

    steps(chips, 8, place)

    def e_of(node):
        return wide_e[pl.ds(node, rank, stride=nodes), :].astype(BF)[:, 0:rank]

    count = chips // 2
    while count >= 4:
        def node_step(p, count=count):
            node = count + p
            both = jnp.concatenate([e_of(2 * node), e_of(2 * node + 1)], axis=0)
            kids = coeff[pl.ds(pl.multiple_of(2 * node * rank, rank), 2 * rank), :]
            coeff[pl.ds(pl.multiple_of(node * rank, rank), rank), :] = dot(both, kids, TN).astype(BF)
        steps(count, min(count, 8), node_step)
        count //= 2

    down = None
    for depth in range(2, depths):
        node = lax.shift_right_logical(nodes + me, depths - depth)
        rhs = jnp.concatenate([
            coeff[pl.ds(pl.multiple_of(jnp.maximum(lists[s, node], 0) * rank, rank), rank), :]
            for s in range(slots)], axis=0)
        lhs = jnp.concatenate(
            [wide_c[j, pl.ds(depth - 2, rank, stride=8), :].astype(BF) for j in range(2)], axis=1)
        far = dot(lhs, rhs)
        down = far if down is None else far + dot(e_of(node), down.astype(BF))
    out[...] = down


def top(me, lists_t, gathered, transfer_t, coupling_t):
    rank, _, nodes = transfer_t.shape
    vecs = gathered.shape[1]
    sm = pl.BlockSpec(memory_space=pltpu.SMEM)
    vm = pl.BlockSpec(memory_space=pltpu.VMEM)
    return pl.pallas_call(
        top_kernel,
        in_specs=[sm, sm, vm, vm, vm],
        out_shape=jax.ShapeDtypeStruct((rank, vecs), F32),
        scratch_shapes=[pltpu.VMEM((rank * nodes, 128), F32), pltpu.VMEM((2, rank * 8, 128), F32),
                        pltpu.VMEM((nodes * rank, vecs), BF)],
        compiler_params=pltpu.CompilerParams(vmem_limit_bytes=32 << 20),
        name="top",
    )(me, lists_t, gathered, transfer_t, coupling_t)


def slots_of(ids, size_log, own, base, per_slab):
    slab = lax.shift_right_arithmetic(ids, size_log)
    inside = ids & (lax.shift_left(jnp.ones_like(size_log), size_log) - 1)
    block = jnp.where(slab == own, 0, jnp.where(slab == (own ^ 1), 1, 2))
    return jnp.where(ids >= 0, block * per_slab + base + inside, 3 * per_slab)


def shards(points, leaf_basis, local_transfer, top_transfer, local_coupling, local_lists,
           top_coupling, top_lists, near_blocks, near_lists):
    leaf_dev, leaf_size, rank = leaf_basis.shape
    nodes = local_transfer.shape[0]
    count = lax.axis_size("leaf")
    own = lax.axis_index("leaf")
    mates = [(i, i ^ 1) for i in range(count)]
    others = [(i, i + 1) for i in range(1, count - 1, 2)]
    others = others + [(j, i) for i, j in others]

    basis_t = jnp.transpose(leaf_basis, (1, 2, 0))
    transfer_t = jnp.transpose(local_transfer, (1, 2, 0))
    points_other = lax.ppermute(points, "leaf", others)
    points_mate = lax.ppermute(points, "leaf", mates)
    coeff, root, basis_rows, transfer_rows = upward(points, basis_t, transfer_t)
    coeff_other = lax.ppermute(coeff, "leaf", others)
    coeff_mate = lax.ppermute(coeff, "leaf", mates)
    gathered = (root + lax.ppermute(root, "leaf", mates)).astype(BF)
    step = 2
    while step < count:
        came = lax.ppermute(gathered, "leaf", [(i, i ^ step) for i in range(count)])
        gathered = jnp.concatenate([gathered, came], axis=0)
        step *= 2
    lhs_near = near_prep(jnp.transpose(near_blocks, (1, 2, 3, 0)))
    lhs_coup = coup_prep(jnp.transpose(local_coupling, (1, 2, 3, 0)))
    above = top(own[None], top_lists.T, gathered, jnp.transpose(top_transfer, (1, 2, 0)),
                jnp.transpose(top_coupling, (1, 2, 3, 0)))
    leaf_log = leaf_dev.bit_length() - 1
    near_pos = slots_of(near_lists.T, jnp.full((1, leaf_dev), leaf_log, jnp.int32), own, 0, leaf_dev)
    near_rows = near(near_pos, lhs_near, points, points_mate, points_other)
    level = np.array([[(n + 1).bit_length() - 1 for n in range(nodes)]], np.int32)
    coup_pos = slots_of(local_lists.T, jnp.asarray(level), own, jnp.asarray(2 ** level - 8), nodes - 7)
    return final(coup_pos, lhs_coup, coeff, coeff_mate, coeff_other, transfer_rows, basis_rows, above, near_rows)


def solution(mesh):
    leaf, whole = P("leaf"), P()
    return jax.shard_map(
        shards,
        mesh=mesh,
        in_specs=(leaf, leaf, leaf, whole, leaf, leaf, whole, whole, leaf, leaf),
        out_specs=leaf,
        check_vma=False,
    )
```

time: 644 us -> 182 us (0.28); the launches traced: 633 us -> 180 us
  local copies, waits for them, and re-layouts: 297 us -> 13.1 us
  matrix products: 137 us -> 0 us
  Pallas kernels: 0 us -> 111 us
  between operations: 92.6 us -> 0.23 us
  other arithmetic: 47.3 us -> 0.63 us
  starting transfers between devices: 59.6 us -> 23 us
  waiting for transfers between devices: 0.05 us -> 31.6 us
    unnamed x563 -> x43, local copies, waits for them, and re-layouts: 152 us -> 13 us
    dot_general x107 -> x0, matrix products: 137 us -> none  [the longest x84 111 us: couple(): jnp.einsum('mrs,msv->mrv', blocks[:, slot_idx], picked, preferred_element...]
    pallas_call x0 -> x6, Pallas kernels: none -> 111 us  [the longest x1 41.1 us: final(): pl.pallas_call(final_kernel, in_specs=[pl.BlockSpec(memory_space=pltpu.SM...]
    gather x46 -> x0, local copies, waits for them, and re-layouts: 79.6 us -> none  [couple(): picked = window[positions[:, slot_idx]]]
    ppermute x12 -> x11, starting transfers between devices: 59.6 us -> 23 us  [the longest x6 11.7 us: shards(): came = lax.ppermute(gathered, 'leaf', [(i, i ^ step) for i in range(count)])]
    slice x25 -> x0, local copies, waits for them, and re-layouts: 36.3 us -> none  [the longest x6 23.2 us: couple(): blocks[:, slot_idx]]
    ppermute x12 -> x11, waiting for transfers between devices: 0.03 us -> 31.6 us  [the longest x6 28.3 us: shards(): came = lax.ppermute(gathered, 'leaf', [(i, i ^ step) for i in range(count)])]
    gather x30 -> x0, other arithmetic: 23.6 us -> none  [couple(): picked = window[positions[:, slot_idx]]]
  transfers between devices with their start and end apart: 13 -> 11, of which waited for: 0 -> 6; matrix products, arithmetic and copies ran while one was open for 61% -> 0% of each run, Pallas kernels for 0% -> 39%
where the time goes in v1:
time: 182 us; the launch traced here: 180 us
  Pallas kernels  111 us (61%)
  waiting for transfers between devices  31.6 us (17%)
  starting transfers between devices  23 us (13%)
  local copies, waits for them, and re-layouts  13.1 us (7%)
    pallas_call x1, Pallas kernels, final(): pl.pallas_call(final_kernel, in_specs=[pl.BlockSpec(memory_space=pltpu.SM...  41.1 us
    ppermute x6, waiting for transfers between devices, shards(): came = lax.ppermute(gathered, 'leaf', [(i, i ^ step) for i in range(count)])  28.3 us
    pallas_call x1, Pallas kernels, upward(): pl.pallas_call(upward_kernel, out_shape=(jax.ShapeDtypeStruct((padded * r...  28.3 us
    pallas_call x1, Pallas kernels, near_prep(): pl.pallas_call(near_prep_kernel, grid=(rows // part,), in_specs=[pl.Block...  13.8 us
    unnamed x43, local copies, waits for them, and re-layouts  13 us
    ppermute x6, starting transfers between devices, shards(): came = lax.ppermute(gathered, 'leaf', [(i, i ^ step) for i in range(count)])  11.7 us
    pallas_call x1, Pallas kernels, top(): pl.pallas_call(top_kernel, in_specs=[sm, sm, vm, vm, vm], out_shape=jax.S...  10.1 us
    pallas_call x1, Pallas kernels, near(): pl.pallas_call(near_kernel, grid_spec=pltpu.PrefetchScalarGridSpec(num_sc...  9.44 us
  transfers between devices with their start and end apart: 11, of which 6 were waited for; matrix products, arithmetic and copies ran while one was open for 0% of the time, Pallas kernels for 39%

profile of v1, /device:TPU:6, one launch (start us, length us, event | category | flops | bytes accessed | tf_op | source)
XLA Modules:
  0.0 179.8 jit_solution(12724465223754603795)
XLA Ops:
  0.0 8.8 %collective-permute-start.10 = (bf16[8192,128]{1,0:T(8,128)(2,1)}, bf16[8192,128]{1,0:T(8,128)(2,1)}, u32[]{:S(2)}, u32[]{:S(2)}) collective-permute-start(bf16[8192,128]{1,0:T(8,128)(2,1)} %own.1), channel_id=1, source_target_pairs={{1,2},{3,4},{5,6},{7,8},{9,10},{11,12},{13,14},{15,16},{17,18},{19... | collective-permute-start | bytes 6291464 | tf_op jit(solution)/shard_map/ppermute | solution.py:370
  9.8 1.0 copy-done.8
  10.9 28.3 %upward.1 = (bf16[8192,128]{1,0:T(8,128)(2,1)}, f32[32,128]{1,0:T(8,128)S(1)}, bf16[128,64,32]{2,1,0:T(8,128)(2,1)S(1)}, bf16[256,32,32]{2,1,0:T(8,128)(2,1)}) custom-call(bf16[8192,128]{1,0:T(8,128)(2,1)} %own.1, bf16[64,32,128]{2,1,0:T(8,128)(2,1)S(1)} %bitcast.17, bf16[32,32,255]{2,1,0:T(8,128)(2,1)S(1)} %bitcast.18), custom_call_target="tpu_custom_call" | custom-call | tf_op jit(solution)/shard_map/upward/pallas_call | solution.py:155
  39.1 1.3 copy-done.6
  40.5 1.9 %collective-permute-start.1 = (bf16[8192,128]{1,0:T(8,128)(2,1)}, bf16[8192,128]{1,0:T(8,128)(2,1)}, u32[]{:S(2)}, u32[]{:S(2)}) collective-permute-start(bf16[8192,128]{1,0:T(8,128)(2,1)} %get-tuple-element.9.own), channel_id=1, source_target_pairs={{1,2},{3,4},{5,6},{7,8},{9,10},{11,12},{13,14},{15,16},{17,18},{19... | collective-permute-start | bytes 6291464 | tf_op jit(solution)/shard_map/ppermute | solution.py:373
  43.0 3.3 %collective-permute-done.2 = f32[32,128]{1,0:T(8,128)S(1)} collective-permute-done((f32[32,128]{1,0:T(8,128)S(1)}, f32[32,128]{1,0:T(8,128)S(1)}, u32[]{:S(2)}, u32[]{:S(2)}) %collective-permute-start.2) | collective-permute-done | bytes 16416 | tf_op jit(solution)/shard_map/ppermute | solution.py:375
  46.3 16.9 %collective-permute-done.3 = bf16[32,128]{1,0:T(8,128)(2,1)S(1)} collective-permute-done((bf16[32,128]{1,0:T(8,128)(2,1)S(1)}, bf16[32,128]{1,0:T(8,128)(2,1)S(1)}, u32[]{:S(2)}, u32[]{:S(2)}) %collective-permute-start.3) | collective-permute-done | bytes 8224 | tf_op jit(solution)/shard_map/ppermute | solution.py:378
  63.2 2.9 %collective-permute-start.4 = (bf16[64,128]{1,0:T(8,128)(2,1)S(1)}, bf16[64,128]{1,0:T(8,128)(2,1)S(1)}, u32[]{:S(2)}, u32[]{:S(2)}) collective-permute-start(bf16[64,128]{1,0:T(8,128)(2,1)S(1)} %pad_maximum_fusion.2), channel_id=1, source_target_pairs={{0,4},{1,5},{2,6},{3,7},{4,0},{5,1},{6,2},{7,3},{8,12},{9,13},{10,... | collective-permute-start | bytes 49160 | tf_op jit(solution)/shard_map/ppermute | solution.py:378
  66.1 2.3 %collective-permute-done.4 = bf16[64,128]{1,0:T(8,128)(2,1)S(1)} collective-permute-done((bf16[64,128]{1,0:T(8,128)(2,1)S(1)}, bf16[64,128]{1,0:T(8,128)(2,1)S(1)}, u32[]{:S(2)}, u32[]{:S(2)}) %collective-permute-start.4) | collective-permute-done | bytes 16416 | tf_op jit(solution)/shard_map/ppermute | solution.py:378
  68.4 1.9 %collective-permute-start.5 = (bf16[128,128]{1,0:T(8,128)(2,1)S(1)}, bf16[128,128]{1,0:T(8,128)(2,1)S(1)}, u32[]{:S(2)}, u32[]{:S(2)}) collective-permute-start(bf16[128,128]{1,0:T(8,128)(2,1)S(1)} %pad_maximum_fusion.1), channel_id=1, source_target_pairs={{0,8},{1,9},{2,10},{3,11},{4,12},{5,13},{6,14},{7,15},{8,0},{9,1},... | collective-permute-start | bytes 98312 | tf_op jit(solution)/shard_map/ppermute | solution.py:378
  70.4 2.0 %collective-permute-done.5 = bf16[128,128]{1,0:T(8,128)(2,1)S(1)} collective-permute-done((bf16[128,128]{1,0:T(8,128)(2,1)S(1)}, bf16[128,128]{1,0:T(8,128)(2,1)S(1)}, u32[]{:S(2)}, u32[]{:S(2)}) %collective-permute-start.5) | collective-permute-done | bytes 32800 | tf_op jit(solution)/shard_map/ppermute | solution.py:378
  72.3 3.9 %collective-permute-start.6 = (bf16[256,128]{1,0:T(8,128)(2,1)S(1)}, bf16[256,128]{1,0:T(8,128)(2,1)S(1)}, u32[]{:S(2)}, u32[]{:S(2)}) collective-permute-start(bf16[256,128]{1,0:T(8,128)(2,1)S(1)} %pad_maximum_fusion), channel_id=1, source_target_pairs={{0,16},{1,17},{2,18},{3,19},{4,20},{5,21},{6,22},{7,23},{8,24},{9,... | collective-permute-start | bytes 196616 | tf_op jit(solution)/shard_map/ppermute | solution.py:378
  76.3 2.2 %collective-permute-done.6 = bf16[256,128]{1,0:T(8,128)(2,1)S(1)} collective-permute-done((bf16[256,128]{1,0:T(8,128)(2,1)S(1)}, bf16[256,128]{1,0:T(8,128)(2,1)S(1)}, u32[]{:S(2)}, u32[]{:S(2)}) %collective-permute-start.6) | collective-permute-done | bytes 65568 | tf_op jit(solution)/shard_map/ppermute | solution.py:378
  79.4 4.9 %collective-permute-done.7 = bf16[512,128]{1,0:T(8,128)(2,1)S(1)} collective-permute-done((bf16[512,128]{1,0:T(8,128)(2,1)S(1)}, bf16[512,128]{1,0:T(8,128)(2,1)S(1)}, u32[]{:S(2)}, u32[]{:S(2)}) %collective-permute-start.7) | collective-permute-done | bytes 131104 | tf_op jit(solution)/shard_map/ppermute | solution.py:378
  84.3 2.1 %collective-permute-start.8 = (bf16[1024,128]{1,0:T(8,128)(2,1)S(1)}, bf16[1024,128]{1,0:T(8,128)(2,1)S(1)}, u32[]{:S(2)}, u32[]{:S(2)}) collective-permute-start(bf16[1024,128]{1,0:T(8,128)(2,1)S(1)} %get-tuple-element.15), channel_id=1, source_target_pairs={{0,64},{1,65},{2,66},{3,67},{4,68},{5,69},{6,70},{7,71},{8,72},{9,... | collective-permute-start | bytes 786440 | tf_op jit(solution)/shard_map/ppermute | solution.py:378
  86.4 2.2 %copy-done.4 = bf16[255,8,32,32]{0,3,2,1:T(8,128)(2,1)S(1)} copy-done((bf16[255,8,32,32]{0,3,2,1:T(8,128)(2,1)S(1)}, bf16[255,8,32,32]{0,3,2,1:T(8,128)(2,1)}, u32[]{:S(2)}) %copy-start.4) | copy-done | bytes 4177944
  88.6 8.7 %coup_prep.1.lhs = bf16[256,32,256]{2,1,0:T(8,128)(2,1)S(1)} custom-call(bf16[8,32,32,255]{3,2,1,0:T(8,128)(2,1)S(1)} %bitcast.15), custom_call_target="tpu_custom_call" | custom-call | tf_op jit(solution)/shard_map/coup_prep/pallas_call | solution.py:94
  97.3 2.1 %copy-done.2 = bf16[256,32,256]{2,1,0:T(8,128)(2,1)} copy-done((bf16[256,32,256]{2,1,0:T(8,128)(2,1)}, bf16[256,32,256]{2,1,0:T(8,128)(2,1)S(1)}, u32[]{:S(2)}) %copy-start.2) | copy-done | bytes 4194328
  99.4 13.8 %near_prep.1.lhs = bf16[128,64,384]{2,1,0:T(8,128)(2,1)S(1)} custom-call(bf16[6,64,64,128]{3,2,1,0:T(8,128)(2,1)S(1)} %bitcast.14), custom_call_target="tpu_custom_call" | custom-call | tf_op jit(solution)/shard_map/near_prep/pallas_call | solution.py:57
  113.2 2.6 %copy-done = bf16[128,64,384]{2,1,0:T(8,128)(2,1)} copy-done((bf16[128,64,384]{2,1,0:T(8,128)(2,1)}, bf16[128,64,384]{2,1,0:T(8,128)(2,1)S(1)}, u32[]{:S(2)}) %copy-start) | copy-done | bytes 6291480
  116.6 10.1 %top.1.above = f32[32,128]{1,0:T(8,128)S(1)} custom-call(s32[1]{0:T(128)} %bitcast.4.where_am_i, s32[8,128]{1,0:T(8,128)S(1)} %bitcast.20, bf16[2048,128]{1,0:T(8,128)(2,1)S(1)} %constant_dynamic-update-slice_fusion.11.gathered, bf16[32,32,128]{2,1,0:T(8,128)(2,1)S(1)} %bitcast.19, bf16[8,32,32,128]{3,2,1,0:T(8,128)(2,1)S(1)} %bitcast.16), custom_call_target="tpu_custom_call" | custom-call | tf_op jit(solution)/shard_map/top/pallas_call | solution.py:340
  127.3 9.4 %near.1.near_rows = f32[8192,128]{1,0:T(8,128)S(1)} custom-call(s32[6,128]{1,0:T(8,128)S(1)} %select_bitcast_fusion.1.pos, bf16[128,64,384]{2,1,0:T(8,128)(2,1)} %copy-done, bf16[8192,128]{1,0:T(8,128)(2,1)S(1)} %copy-done.3, bf16[8192,128]{1,0:T(8,128)(2,1)} %collective-permute-done.9.mate, bf16[8192,128]{1,0:T(8,128)(2,1)} %collective-permute-done.10.other), custom_call_target="tpu_custom_call" | custom-call | tf_op jit(solution)/shard_map/near/pallas_call | solution.py:198
  136.7 2.0 %copy-done.1 = f32[8192,128]{1,0:T(8,128)} copy-done((f32[8192,128]{1,0:T(8,128)}, f32[8192,128]{1,0:T(8,128)S(1)}, u32[]{:S(2)}) %copy-start.1) | copy-done | bytes 4194328
  138.7 41.1 %final.1 = bf16[8192,128]{1,0:T(8,128)(2,1)} custom-call(s32[8,255]{1,0:T(8,128)} %select_bitcast_fusion.pos, bf16[256,32,256]{2,1,0:T(8,128)(2,1)} %copy-done.2, bf16[8192,128]{1,0:T(8,128)(2,1)} %get-tuple-element.9.own, bf16[8192,128]{1,0:T(8,128)(2,1)} %collective-permute-done.mate, bf16[8192,128]{1,0:T(8,128)(2,1)} %collective-permute-done.1.other, ...), custom_call_target="tpu_custom_call" | custom-call | tf_op jit(solution)/shard_map/final/pallas_call | solution.py:265
  (56 shorter events, 4.0 us)
Async XLA Ops:
  0.0 127.3 %collective-permute-start.9 = (bf16[8192,128]{1,0:T(8,128)(2,1)}, bf16[8192,128]{1,0:T(8,128)(2,1)}, u32[]{:S(2)}, u32[]{:S(2)}) collective-permute-start(bf16[8192,128]{1,0:T(8,128)(2,1)} %own.1), channel_id=1, source_target_pairs={{0,1},{1,0},{2,3},{3,2},{4,5},{5,4},{6,7},{7,6},{8,9},{9,8},{10,11... | collective-permute-start | bytes 6291464 | tf_op jit(solution)/shard_map/ppermute | solution.py:371
  0.0 127.3 %collective-permute-start.10 = (bf16[8192,128]{1,0:T(8,128)(2,1)}, bf16[8192,128]{1,0:T(8,128)(2,1)}, u32[]{:S(2)}, u32[]{:S(2)}) collective-permute-start(bf16[8192,128]{1,0:T(8,128)(2,1)} %own.1), channel_id=1, source_target_pairs={{1,2},{3,4},{5,6},{7,8},{9,10},{11,12},{13,14},{15,16},{17,18},{19... | collective-permute-start | bytes 6291464 | tf_op jit(solution)/shard_map/ppermute | solution.py:370
  10.9 75.5 %copy-start.13 = (s32[128,6]{0,1:T(8,128)S(1)}, s32[128,6]{0,1:T(8,128)}, u32[]{:S(2)}) copy-start(s32[128,6]{0,1:T(8,128)} %param.21) | copy-start | bytes 9220
  10.9 88.5 %slice-start = ((s8[6291456]{0:T(1024)(128)(4,1)}), s8[2097152]{0:T(1024)(128)(4,1)S(1)}, s32[]{:S(2)}) async-start(s8[6291456]{0:T(1024)(128)(4,1)} %bitcast.12), calls=%async_computation | async-start | bytes 4194304
  40.5 98.3 %collective-permute-start.1 = (bf16[8192,128]{1,0:T(8,128)(2,1)}, bf16[8192,128]{1,0:T(8,128)(2,1)}, u32[]{:S(2)}, u32[]{:S(2)}) collective-permute-start(bf16[8192,128]{1,0:T(8,128)(2,1)} %get-tuple-element.9.own), channel_id=1, source_target_pairs={{1,2},{3,4},{5,6},{7,8},{9,10},{11,12},{13,14},{15,16},{17,18},{19... | collective-permute-start | bytes 6291464 | tf_op jit(solution)/shard_map/ppermute | solution.py:373
  42.4 96.4 %collective-permute-start = (bf16[8192,128]{1,0:T(8,128)(2,1)}, bf16[8192,128]{1,0:T(8,128)(2,1)}, u32[]{:S(2)}, u32[]{:S(2)}) collective-permute-start(bf16[8192,128]{1,0:T(8,128)(2,1)} %get-tuple-element.9.own), channel_id=1, source_target_pairs={{0,1},{1,0},{2,3},{3,2},{4,5},{5,4},{6,7},{7,6},{8,9},{9,8},{10,11... | collective-permute-start | bytes 6291464 | tf_op jit(solution)/shard_map/ppermute | solution.py:374
  42.5 3.8 %collective-permute-start.2 = (f32[32,128]{1,0:T(8,128)S(1)}, f32[32,128]{1,0:T(8,128)S(1)}, u32[]{:S(2)}, u32[]{:S(2)}) collective-permute-start(f32[32,128]{1,0:T(8,128)S(1)} %get-tuple-element.12), channel_id=1, source_target_pairs={{0,1},{1,0},{2,3},{3,2},{4,5},{5,4},{6,7},{7,6},{8,9},{9,8},{10,11... | collective-permute-start | bytes 49160 | tf_op jit(solution)/shard_map/ppermute | solution.py:375
  46.3 16.9 %collective-permute-start.3 = (bf16[32,128]{1,0:T(8,128)(2,1)S(1)}, bf16[32,128]{1,0:T(8,128)(2,1)S(1)}, u32[]{:S(2)}, u32[]{:S(2)}) collective-permute-start(bf16[32,128]{1,0:T(8,128)(2,1)S(1)} %get-tuple-element.14), channel_id=1, source_target_pairs={{0,2},{1,3},{2,0},{3,1},{4,6},{5,7},{6,4},{7,5},{8,10},{9,11},{10,... | collective-permute-start | bytes 24584 | tf_op jit(solution)/shard_map/ppermute | solution.py:378
  63.2 5.2 %collective-permute-start.4 = (bf16[64,128]{1,0:T(8,128)(2,1)S(1)}, bf16[64,128]{1,0:T(8,128)(2,1)S(1)}, u32[]{:S(2)}, u32[]{:S(2)}) collective-permute-start(bf16[64,128]{1,0:T(8,128)(2,1)S(1)} %pad_maximum_fusion.2), channel_id=1, source_target_pairs={{0,4},{1,5},{2,6},{3,7},{4,0},{5,1},{6,2},{7,3},{8,12},{9,13},{10,... | collective-permute-start | bytes 49160 | tf_op jit(solution)/shard_map/ppermute | solution.py:378
  68.4 3.9 %collective-permute-start.5 = (bf16[128,128]{1,0:T(8,128)(2,1)S(1)}, bf16[128,128]{1,0:T(8,128)(2,1)S(1)}, u32[]{:S(2)}, u32[]{:S(2)}) collective-permute-start(bf16[128,128]{1,0:T(8,128)(2,1)S(1)} %pad_maximum_fusion.1), channel_id=1, source_target_pairs={{0,8},{1,9},{2,10},{3,11},{4,12},{5,13},{6,14},{7,15},{8,0},{9,1},... | collective-permute-start | bytes 98312 | tf_op jit(solution)/shard_map/ppermute | solution.py:378
  72.3 6.1 %collective-permute-start.6 = (bf16[256,128]{1,0:T(8,128)(2,1)S(1)}, bf16[256,128]{1,0:T(8,128)(2,1)S(1)}, u32[]{:S(2)}, u32[]{:S(2)}) collective-permute-start(bf16[256,128]{1,0:T(8,128)(2,1)S(1)} %pad_maximum_fusion), channel_id=1, source_target_pairs={{0,16},{1,17},{2,18},{3,19},{4,20},{5,21},{6,22},{7,23},{8,24},{9,... | collective-permute-start | bytes 196616 | tf_op jit(solution)/shard_map/ppermute | solution.py:378
  78.5 5.8 %collective-permute-start.7 = (bf16[512,128]{1,0:T(8,128)(2,1)S(1)}, bf16[512,128]{1,0:T(8,128)(2,1)S(1)}, u32[]{:S(2)}, u32[]{:S(2)}) collective-permute-start(bf16[512,128]{1,0:T(8,128)(2,1)S(1)} %get-tuple-element.19), channel_id=1, source_target_pairs={{0,32},{1,33},{2,34},{3,35},{4,36},{5,37},{6,38},{7,39},{8,40},{9,... | collective-permute-start | bytes 393224 | tf_op jit(solution)/shard_map/ppermute | solution.py:378
  84.3 32.2 %collective-permute-start.8 = (bf16[1024,128]{1,0:T(8,128)(2,1)S(1)}, bf16[1024,128]{1,0:T(8,128)(2,1)S(1)}, u32[]{:S(2)}, u32[]{:S(2)}) collective-permute-start(bf16[1024,128]{1,0:T(8,128)(2,1)S(1)} %get-tuple-element.15), channel_id=1, source_target_pairs={{0,64},{1,65},{2,66},{3,67},{4,68},{5,69},{6,70},{7,71},{8,72},{9,... | collective-permute-start | bytes 786440 | tf_op jit(solution)/shard_map/ppermute | solution.py:378
  86.4 2.2 %copy-start.4 = (bf16[255,8,32,32]{0,3,2,1:T(8,128)(2,1)S(1)}, bf16[255,8,32,32]{0,3,2,1:T(8,128)(2,1)}, u32[]{:S(2)}) copy-start(bf16[255,8,32,32]{0,3,2,1:T(8,128)(2,1)} %param.16) | copy-start | bytes 12533764
  88.6 10.8 %slice-start.1 = ((s8[6291456]{0:T(1024)(128)(4,1)}), s8[4194304]{0:T(1024)(128)(4,1)S(1)}, s32[]{:S(2)}) async-start(s8[6291456]{0:T(1024)(128)(4,1)} %bitcast.12), calls=%async_computation.1 | async-start | bytes 8388608
  99.4 16.5 %copy-start.12 = (s32[255,8]{0,1:T(8,128)S(1)}, s32[255,8]{0,1:T(8,128)}, u32[]{:S(2)}) copy-start(s32[255,8]{0,1:T(8,128)} %param.17) | copy-start | bytes 24484
  99.4 16.5 %copy-start.14 = (s32[255]{0:T(256)S(1)}, s32[255]{0:T(256)}, u32[]{:S(2)}) copy-start(s32[255]{0:T(256)} %constant.44) | copy-start | bytes 3064
  99.4 16.5 %copy-start.15 = (s32[255]{0:T(256)S(1)}, s32[255]{0:T(256)}, u32[]{:S(2)}) copy-start(s32[255]{0:T(256)} %constant.41) | copy-start | bytes 3064
  99.4 16.5 %copy-start.16 = (s32[255]{0:T(256)S(1)}, s32[255]{0:T(256)}, u32[]{:S(2)}) copy-start(s32[255]{0:T(256)} %constant.40) | copy-start | bytes 3064
  99.4 17.1 %copy-start.5 = (bf16[128,8,32,32]{0,3,2,1:T(8,128)(2,1)S(1)}, bf16[128,8,32,32]{0,3,2,1:T(8,128)(2,1)}, u32[]{:S(2)}) copy-start(bf16[128,8,32,32]{0,3,2,1:T(8,128)(2,1)} %param.18) | copy-start | bytes 6291460
  99.4 17.1 %copy-start.9 = (bf16[128,32,32]{0,2,1:T(8,128)(2,1)S(1)}, bf16[128,32,32]{0,2,1:T(8,128)(2,1)}, u32[]{:S(2)}) copy-start(bf16[128,32,32]{0,2,1:T(8,128)(2,1)} %param.15) | copy-start | bytes 786436
  99.4 17.1 %copy-start.11 = (s32[128,8]{0,1:T(8,128)S(1)}, s32[128,8]{0,1:T(8,128)}, u32[]{:S(2)}) copy-start(s32[128,8]{0,1:T(8,128)} %param.19) | copy-start | bytes 12292
  113.2 2.6 %copy-start = (bf16[128,64,384]{2,1,0:T(8,128)(2,1)}, bf16[128,64,384]{2,1,0:T(8,128)(2,1)S(1)}, u32[]{:S(2)}) copy-start(bf16[128,64,384]{2,1,0:T(8,128)(2,1)S(1)} %near_prep.1.lhs) | copy-start | bytes 18874372
  115.9 11.4 %copy-start.3 = (bf16[8192,128]{1,0:T(8,128)(2,1)S(1)}, bf16[8192,128]{1,0:T(8,128)(2,1)}, u32[]{:S(2)}) copy-start(bf16[8192,128]{1,0:T(8,128)(2,1)} %own.1) | copy-start | bytes 6291460
  (6 other events, 8.1 us)

commit v2 on v0

v2 whole, which is shorter than its diff:
```python
import jax
import jax.numpy as jnp
import numpy as np
from jax import lax
from jax.experimental import pallas as pl
from jax.experimental.pallas import tpu as pltpu
from jax.sharding import PartitionSpec as P

BF = jnp.bfloat16
F32 = jnp.float32
NT = (((1,), (1,)), ((), ()))
NN = (((1,), (0,)), ((), ()))
TN = (((0,), (0,)), ((), ()))
PAD = 8
FIRST = 7
SCALE = 40000
VMEM = 28 << 20
ANY = pl.BlockSpec(memory_space=pl.ANY)


def dot(a, b, dims=NN):
    return lax.dot_general(a, b, dims, preferred_element_type=F32)


def cost(us):
    return pl.CostEstimate(flops=0, bytes_accessed=us * SCALE, transcendentals=0)


def eye(rows, cols):
    return (lax.broadcasted_iota(jnp.int32, (rows, cols), 0)
            == lax.broadcasted_iota(jnp.int32, (rows, cols), 1)).astype(BF)


def batch(count, width, load, work, store):
    width = min(width, count)

    def trip(t, carry):
        at = [t * width + u for u in range(width)]
        got = [load(i) for i in at]
        done = [work(*g) for g in got]
        for i, d in zip(at, done):
            store(i, d)
        return carry

    if count == width:
        trip(0, 0)
    else:
        lax.fori_loop(0, count // width, trip, 0)


def rows_at(index, height, many=1):
    start = index * height
    return pl.ds(start if isinstance(start, int) else pl.multiple_of(start, height), many * height)


def put(wide, at, value):
    width = value.shape[1]
    for j in range(wide.shape[0]):
        piece = value[:, j * 128:min(width, (j + 1) * 128)]
        wide[j, pl.ds(at if isinstance(at, int) else pl.multiple_of(at, 8), value.shape[0]), 0:piece.shape[1]] = piece


def turn_kernel(blocks, extra, out, wide):
    slots, rows, cols, lanes = blocks.shape
    count, _, width = out.shape
    ident = eye(count, lanes)
    step = count + PAD
    chunks = wide.shape[0]

    batch(rows, 8,
          lambda r: (jnp.concatenate([blocks[:, r].reshape(slots * cols, lanes), extra[r]], axis=0),),
          lambda both: dot(ident, both, NT),
          lambda r, turned: put(wide, r * step, turned))

    def store(i, parts):
        for j in range(chunks):
            end = min(width, (j + 1) * 128)
            out[i, :, j * 128:end] = parts[j][:, 0:end - j * 128]

    batch(count, 16,
          lambda i: [wide[j, pl.ds(i, rows, stride=step), :] for j in range(chunks)],
          lambda *parts: [p.astype(BF) for p in parts], store)


def turn(blocks_t, extra_t, name, first, rows, part=16):
    slots, _, cols, lanes = blocks_t.shape
    skip = first // part
    width = slots * cols + extra_t.shape[1]
    count = (lanes + 7) // 8 * 8
    chunks = (width + 127) // 128
    return pl.pallas_call(
        turn_kernel,
        grid=(rows // part,),
        in_specs=[pl.BlockSpec((slots, part, cols, lanes), lambda i: (0, i + skip, 0, 0)),
                  pl.BlockSpec((part,) + extra_t.shape[1:], lambda i: (i + skip, 0, 0))],
        out_specs=pl.BlockSpec((count, part, width), lambda i: (0, i, 0)),
        out_shape=jax.ShapeDtypeStruct((count, rows, width), BF),
        scratch_shapes=[pltpu.VMEM((chunks, part * (count + PAD), 128), F32)],
        compiler_params=pltpu.CompilerParams(vmem_limit_bytes=VMEM),
        cost_estimate=cost(max(1, rows * count // 1024)),
        name=name,
    )(blocks_t, extra_t)


def upward_kernel(me, points_in, basis_in, transfer_in, coeff, keep, give, points, basis, transfer, wide_b, wide_e, sems):
    size, rank, leaves = basis.shape
    copies = [pltpu.make_async_copy(src, dst, sems.at[n])
              for n, (src, dst) in enumerate(((basis_in, basis), (transfer_in, transfer), (points_in, points)))]
    for c in copies:
        c.start()
    nodes = transfer.shape[2]
    padded = nodes + 1
    ident = eye(leaves, leaves)
    ident_e = eye(padded, nodes)
    step_b, step_e = leaves + PAD, padded + PAD

    copies[0].wait()
    batch(size, 16, lambda p: (basis[p],), lambda b: dot(ident, b, NT), lambda p, v: put(wide_b, p * step_b, v))
    copies[1].wait()
    batch(rank, 16, lambda r: (transfer[r],), lambda b: dot(ident_e, b, NT), lambda r, v: put(wide_e, r * step_e, v))

    copies[2].wait()

    def store_leaf(leaf, got):
        coeff[rows_at(leaves - 1 + leaf, rank), :] = got

    batch(leaves, 32,
          lambda leaf: (wide_b[0, pl.ds(leaf, size, stride=step_b), :], points[rows_at(leaf, size), :]),
          lambda mine, x: dot(mine.astype(BF)[:, 0:rank], x, TN).astype(BF), store_leaf)

    def e_of(node):
        return wide_e[0, pl.ds(node, rank, stride=step_e), :]

    def pair_work(left, right, kids):
        both = jnp.concatenate([left, right], axis=0).astype(BF)[:, 0:rank]
        return dot(both, kids, TN).astype(BF)

    count = leaves // 2
    while count >= 1:
        def load(p, count=count):
            left = 2 * count - 1 + 2 * p
            return e_of(left), e_of(left + 1), coeff[rows_at(left, rank, 2), :]

        def store(p, got, count=count):
            coeff[rows_at(count - 1 + p, rank), :] = got

        batch(count, 32, load, pair_work, store)
        count //= 2
    root = dot(e_of(0).astype(BF)[:, 0:rank], coeff[0:rank, :], TN)
    low, high = root[0:rank // 2], root[rank // 2:]
    odd = (me[0] & 1) == 1
    keep[...] = jnp.where(odd, high, low)
    give[...] = jnp.where(odd, low, high)
    coeff[pl.ds(nodes * rank, rank), :] = jnp.zeros((rank, coeff.shape[1]), BF)


def upward(me, points, basis_t, transfer_t):
    size, rank, leaves = basis_t.shape
    padded = transfer_t.shape[2] + 1
    vecs = points.shape[1]
    return pl.pallas_call(
        upward_kernel,
        in_specs=[pl.BlockSpec(memory_space=pltpu.SMEM)] + [pl.BlockSpec(memory_space=pltpu.HBM)] * 3,
        out_shape=(jax.ShapeDtypeStruct((padded * rank, vecs), BF),)
        + (jax.ShapeDtypeStruct((rank // 2, vecs), F32),) * 2,
        scratch_shapes=[pltpu.VMEM(points.shape, BF), pltpu.VMEM(basis_t.shape, BF), pltpu.VMEM(transfer_t.shape, BF),
                        pltpu.VMEM((1, size * (leaves + PAD), 128), F32),
                        pltpu.VMEM((1, rank * (padded + PAD), 128), F32), pltpu.SemaphoreType.DMA((3,))],
        compiler_params=pltpu.CompilerParams(vmem_limit_bytes=VMEM),
        cost_estimate=cost(7),
        name="upward",
    )(me, points, basis_t, transfer_t)


def top_kernel(where_am_i, lists, mine_in, mate_in, transfer_in, coupling_in, out, mine, mate, transfer, coupling,
               wide_e, wide_c, coeff, sems):
    rank, _, nodes = transfer.shape
    copies = [pltpu.make_async_copy(src, dst, sems.at[n]) for n, (src, dst) in enumerate(
        ((transfer_in, transfer), (mine_in, mine), (mate_in, mate), (coupling_in, coupling)))]
    for c in copies:
        c.start()
    slots = coupling.shape[0]
    chips = nodes // 2
    me = where_am_i[0]
    depths = nodes.bit_length() - 1
    step = nodes + PAD
    ident = eye(nodes, nodes)
    row = lax.broadcasted_iota(jnp.int32, (8, nodes), 0)
    lane = lax.broadcasted_iota(jnp.int32, (8, nodes), 1)
    ancestor = lax.shift_right_logical(nodes + me, jnp.maximum(depths - 2 - row, 0))
    picks = ((lane == ancestor) & (row < depths - 2)).astype(BF)

    copies[0].wait()
    batch(rank, 16, lambda r: (transfer[r],), lambda e: dot(ident, e, NT), lambda r, v: put(wide_e, r * step, v))
    coeff[0:rank, :] = jnp.zeros((rank, coeff.shape[1]), BF)

    chip = lax.shift_right_logical(me, 1)
    half = rank // 2
    copies[1].wait()
    copies[2].wait()
    for held, core in ((mine, me & 1), (mate, 1 - (me & 1))):
        def place(q, got, core=core):
            seen = chip ^ q ^ (lax.shift_right_logical(q, 1) & 0b010101)
            coeff[pl.ds(pl.multiple_of((chips + seen) * rank + core * half, half), half), :] = got

        batch(chips, 16, lambda q, held=held: (held[rows_at(q, half), :],), lambda v: v, place)

    def e_of(node):
        return wide_e[0, pl.ds(node, rank, stride=step), :]

    def pair_work(left, right, kids):
        both = jnp.concatenate([left, right], axis=0).astype(BF)[:, 0:rank]
        return dot(both, kids, TN).astype(BF)

    count = chips // 2
    while count >= 4:
        def load(p, count=count):
            left = 2 * (count + p)
            return e_of(left), e_of(left + 1), coeff[rows_at(left, rank, 2), :]

        def store(p, got, count=count):
            coeff[rows_at(count + p, rank), :] = got

        batch(count, 32, load, pair_work, store)
        count //= 2

    copies[3].wait()
    batch(rank, 16, lambda r: (coupling[:, r].reshape(slots * rank, nodes),), lambda c: dot(picks, c, NT),
          lambda r, v: put(wide_c, r * 8, v))
    fars = []
    for depth in range(2, depths):
        node = lax.shift_right_logical(nodes + me, depths - depth)
        rhs = jnp.concatenate([coeff[rows_at(jnp.maximum(lists[s, node], 0), rank), :] for s in range(slots)], axis=0)
        lhs = jnp.concatenate(
            [wide_c[j, pl.ds(depth - 2, rank, stride=8), :].astype(BF) for j in range(wide_c.shape[0])], axis=1)
        fars.append((node, dot(lhs, rhs)))
    down = None
    for node, far in fars:
        down = far if down is None else far + dot(e_of(node).astype(BF)[:, 0:rank], down.astype(BF))
    out[...] = down.astype(BF)


def top(me, lists_t, mine, mate, transfer_t, coupling_t):
    rank, _, nodes = transfer_t.shape
    vecs = mine.shape[1]
    chunks = coupling_t.shape[0] * rank // 128
    sm = pl.BlockSpec(memory_space=pltpu.SMEM)
    hbm = pl.BlockSpec(memory_space=pltpu.HBM)
    return pl.pallas_call(
        top_kernel,
        in_specs=[sm, sm, ANY, ANY, hbm, hbm],
        out_shape=jax.ShapeDtypeStruct((rank, vecs), BF),
        scratch_shapes=[pltpu.VMEM(mine.shape, BF), pltpu.VMEM(mine.shape, BF), pltpu.VMEM(transfer_t.shape, BF), pltpu.VMEM(coupling_t.shape, BF),
                        pltpu.VMEM((1, rank * (nodes + PAD), 128), F32), pltpu.VMEM((chunks, rank * 8, 128), F32),
                        pltpu.VMEM((nodes * rank, vecs), BF), pltpu.SemaphoreType.DMA((4,))],
        compiler_params=pltpu.CompilerParams(vmem_limit_bytes=VMEM),
        cost_estimate=cost(4),
        name="top",
    )(me, lists_t, mine, mate, transfer_t, coupling_t)


def down_kernel(parts, pos, own, mate, other, above, *refs):
    lhs_in, (out, *lhs), (window, down, sems) = refs[:parts], refs[parts:2 * parts + 1], refs[2 * parts + 1:]
    nodes, _, width = lhs[0].shape
    rank = above.shape[0]

    def lhs_of(node):
        return jnp.concatenate([a[node] for a in lhs], axis=0)

    nodes = nodes - 1
    leaves = (nodes + 1) // 2
    slots = width // rank - 1
    rows = (nodes - FIRST) * rank
    half = nodes // 2
    lhs_copies = [[pltpu.make_async_copy(src.at[pl.ds(at, size)], dst.at[pl.ds(at, size)], sems.at[3 + 2 * n + k])
                   for n, (src, dst) in enumerate(zip(lhs_in, lhs))]
                  for k, (at, size) in enumerate(((0, half), (half, nodes + 1 - half)))]
    copies = [pltpu.make_async_copy(src.at[pl.ds(FIRST * rank, rows)], window.at[pl.ds(n * rows, rows)], sems.at[n])
              for n, src in enumerate((own, mate, other))]
    for c in lhs_copies[0] + copies + lhs_copies[1]:
        c.start()
    window[3 * rows:3 * rows + rank, :] = jnp.zeros((rank, window.shape[1]), BF)
    for c in lhs_copies[0]:
        c.wait()

    def parent_of(node):
        if isinstance(node, int):
            return down[rows_at((node - 1) // 2, rank), :] if node else above[...]
        return down[rows_at(lax.shift_right_logical(node - 1, 1), rank), :]

    for node in range(FIRST):
        down[rows_at(node, rank), :] = dot(lhs_of(node)[:, slots * rank:], parent_of(node)).astype(BF)
    for c in copies:
        c.wait()

    count = FIRST + 1
    while count <= leaves:
        def load(p, count=count):
            node = count - 1 + p
            return lhs_of(node), jnp.concatenate(
                [window[rows_at(pos[s, node], rank), :] for s in range(slots)] + [parent_of(node)], axis=0)

        def store(p, got, count=count):
            if count == leaves:
                out[rows_at(p, rank), :] = got
            else:
                down[rows_at(count - 1 + p, rank), :] = got

        if count == leaves:
            for c in lhs_copies[1]:
                c.wait()
        batch(count, DB, load, lambda a, b: dot(a, b).astype(BF), store)
        count *= 2


DB = 32


def downward(pos, lhs, own, mate, other, above):
    nodes = lhs[0].shape[0]
    rank = above.shape[0]
    leaves = nodes // 2
    vecs = own.shape[1]
    any_ = pl.BlockSpec(memory_space=pltpu.HBM)
    vm = pl.BlockSpec(memory_space=pltpu.VMEM)
    rows = (nodes - 1 - FIRST) * rank
    return pl.pallas_call(
        lambda *refs: down_kernel(len(lhs), *refs),
        in_specs=[pl.BlockSpec(memory_space=pltpu.SMEM), any_, any_, any_, vm] + [any_] * len(lhs),
        out_shape=jax.ShapeDtypeStruct((leaves * rank, vecs), BF),
        scratch_shapes=[pltpu.VMEM(a.shape, BF) for a in lhs]
        + [pltpu.VMEM((3 * rows + rank, vecs), BF), pltpu.VMEM((leaves * rank, vecs), BF),
           pltpu.SemaphoreType.DMA((3 + 2 * len(lhs),))],
        compiler_params=pltpu.CompilerParams(vmem_limit_bytes=VMEM),
        cost_estimate=cost(9),
        name="downward",
    )(pos, own, mate, other, above, *lhs)


def rows_kernel(parts, count, pos, down, *refs):
    lhs, pieces, (out, window, sems) = refs[:parts], refs[parts:parts + count], refs[parts + count:]
    i = pl.program_id(0)
    part, _, width = lhs[0].shape
    size = sum(a.shape[1] for a in lhs)
    rank = down.shape[0] // part
    slots = (width - rank) // size

    @pl.when(i == 0)
    def _():
        copies, at = [], 0
        for n, src in enumerate(pieces):
            copies.append(pltpu.make_async_copy(src, window.at[pl.ds(at, src.shape[0])], sems.at[n]))
            at += src.shape[0]
        for c in copies:
            c.start()
        window[at:at + size, :] = jnp.zeros((size, window.shape[1]), BF)
        for c in copies:
            c.wait()

    def load(l):
        return jnp.concatenate([a[l] for a in lhs], axis=0), jnp.concatenate(
            [window[rows_at(pos[s, i * part + l], size), :] for s in range(slots)] + [down[rows_at(l, rank), :]], axis=0)

    def store(l, got):
        out[rows_at(l, size), :] = got

    batch(part, 16, load, lambda a, b: dot(a, b).astype(BF), store)


def leaf_rows(pos, lhs, down, *pieces):
    leaves, _, width = lhs[0].shape
    size = sum(a.shape[1] for a in lhs)
    rows, vecs = pieces[0].shape
    rank = down.shape[0] // leaves
    part = 32
    any_ = pl.BlockSpec(memory_space=pltpu.HBM)
    return pl.pallas_call(
        lambda *refs: rows_kernel(len(lhs), len(pieces), *refs),
        grid_spec=pltpu.PrefetchScalarGridSpec(
            num_scalar_prefetch=1,
            grid=(leaves // part,),
            in_specs=[pl.BlockSpec((part * rank, vecs), lambda i, p: (i, 0))]
            + [pl.BlockSpec((part,) + a.shape[1:], lambda i, p: (i, 0, 0)) for a in lhs] + [any_] * len(pieces),
            out_specs=pl.BlockSpec((part * size, vecs), lambda i, p: (i, 0)),
            scratch_shapes=[pltpu.VMEM((3 * rows + size, vecs), BF), pltpu.SemaphoreType.DMA((len(pieces),))],
        ),
        out_shape=jax.ShapeDtypeStruct((rows, vecs), BF),
        compiler_params=pltpu.CompilerParams(vmem_limit_bytes=VMEM),
        cost_estimate=cost(6),
        name="leaf_rows",
    )(pos, down, *lhs, *pieces)


def split_kernel(src, early, late, held, sems):
    jobs, at = [], 0
    for dst in (early, late):
        for start in range(0, dst.shape[0], 1536):
            size = min(1536, dst.shape[0] - start)
            jobs.append((at + start, size, dst, start))
        at += dst.shape[0]
    into = [pltpu.make_async_copy(src.at[pl.ds(a, size)], held.at[pl.ds(a, size)], sems.at[0, n])
            for n, (a, size, _, _) in enumerate(jobs)]
    back = [pltpu.make_async_copy(held.at[pl.ds(a, size)], dst.at[pl.ds(b, size)], sems.at[1, n])
            for n, (a, size, dst, b) in enumerate(jobs)]
    for c in into:
        c.start()
    for c, d in zip(into, back):
        c.wait()
        d.start()
    for d in back:
        d.wait()


def split(value, cut):
    rows, vecs = value.shape
    hbm = pl.BlockSpec(memory_space=pltpu.HBM)
    return pl.pallas_call(
        split_kernel,
        in_specs=[hbm],
        out_specs=[hbm, hbm],
        out_shape=[jax.ShapeDtypeStruct((cut, vecs), BF), jax.ShapeDtypeStruct((rows - cut, vecs), BF)],
        scratch_shapes=[pltpu.VMEM((rows, vecs), BF), pltpu.SemaphoreType.DMA((2, rows // 1536 + 3))],
        compiler_params=pltpu.CompilerParams(vmem_limit_bytes=VMEM),
        cost_estimate=cost(2),
        name="split",
    )(value)


def slots_of(ids, level, own, base, per_slab):
    slab = lax.shift_right_arithmetic(ids, level)
    inside = ids & (lax.shift_left(jnp.ones_like(level), level) - 1)
    block = jnp.where(slab == own, 0, jnp.where(slab == (own ^ 1), 1, 2))
    return jnp.where(ids >= 0, block * per_slab + base + inside, 3 * per_slab)


def after(value, *marks):
    return lax.optimization_barrier((value,) + marks)[0]


def shards(points, leaf_basis, local_transfer, top_transfer, local_coupling, local_lists,
           top_coupling, top_lists, near_blocks, near_lists):
    leaf_dev, leaf_size, rank = leaf_basis.shape
    nodes = local_transfer.shape[0]
    count = lax.axis_size("leaf")
    own = lax.axis_index("leaf")
    mates = [(i, i ^ 1) for i in range(count)]
    others = [(i, i + 1) for i in range(1, count - 1, 2)]
    others = others + [(j, i) for i, j in others]

    def swap(value, pairs):
        return lax.ppermute(value, "leaf", pairs)

    def by_xor(value, bits):
        return swap(value, [(i, i ^ bits) for i in range(count)])

    basis_t = jnp.transpose(leaf_basis, (1, 2, 0))
    transfer_t = jnp.transpose(local_transfer, (1, 2, 0))
    near_t = jnp.transpose(near_blocks, (1, 2, 3, 0))
    coup_t = jnp.transpose(local_coupling, (1, 2, 3, 0))
    near_t = jnp.transpose(near_blocks, (1, 2, 3, 0))
    coup_t = jnp.transpose(local_coupling, (1, 2, 3, 0))
    early, late = split(points, CUT * leaf_size)
    early_other = swap(early, others)
    coeff, keep, give = upward(own[None], after(points, early), basis_t, transfer_t)
    gathered = (keep + swap(give, mates)).astype(BF)
    step = 2
    while step < count:
        gathered = jnp.concatenate([gathered, by_xor(gathered, step)], axis=0)
        if step == 2:
            gathered = after(gathered, early_other)
        gathered = jnp.concatenate([gathered, by_xor(gathered, 3 * step)], axis=0)
        step *= 4
    gathered_mate = swap(gathered, mates)
    coeff_other = swap(after(coeff, gathered), others)
    coeff_mate = swap(after(coeff, gathered), mates)
    late = after(late, gathered)
    above = top(own[None], top_lists.T, gathered, gathered_mate, jnp.transpose(top_transfer, (1, 2, 0)),
                jnp.transpose(top_coupling, (1, 2, 3, 0)))
    late_other = swap(late, others)
    points_mate = swap(after(points, gathered), mates)
    lhs_coup = [turn(after(coup_t, above), transfer_t, "coupling_turn", 0, rank)]
    lhs_near = [turn(after(near_t, lhs_coup[0]), basis_t, "near_turn", 0, leaf_size)]
    above = after(above, lhs_near[0])
    leaf_log = leaf_dev.bit_length() - 1
    near_pos = slots_of(near_lists.T, jnp.full((1, leaf_dev), leaf_log, jnp.int32), own, 0, leaf_dev)
    level = np.array([[(n + 1).bit_length() - 1 for n in range(nodes)]], np.int32)
    coup_pos = slots_of(local_lists.T, jnp.asarray(level), own, jnp.asarray(2 ** level - 1 - FIRST), nodes - FIRST)
    down = downward(coup_pos, lhs_coup, coeff, coeff_mate, coeff_other, above)
    return leaf_rows(near_pos, lhs_near, down, points, points_mate, early_other, late_other)


CUT = 56


def solution(mesh):
    leaf, whole = P("leaf"), P()
    return jax.shard_map(
        shards,
        mesh=mesh,
        in_specs=(leaf, leaf, leaf, whole, leaf, leaf, whole, whole, leaf, leaf),
        out_specs=leaf,
        check_vma=False,
    )
```

time: 644 us -> 106 us (0.16); the launches traced: 633 us -> 105 us
  local copies, waits for them, and re-layouts: 297 us -> 10.1 us
  matrix products: 137 us -> 0 us
  between operations: 92.6 us -> 0.31 us
  other arithmetic: 47.3 us -> 0.76 us
  Pallas kernels: 0 us -> 45.5 us
  starting transfers between devices: 59.6 us -> 19 us
  waiting for transfers between devices: 0.05 us -> 29.2 us
    unnamed x563 -> x36, local copies, waits for them, and re-layouts: 152 us -> 10 us
    dot_general x107 -> x0, matrix products: 137 us -> none  [the longest x84 111 us: couple(): jnp.einsum('mrs,msv->mrv', blocks[:, slot_idx], picked, preferred_element...]
    gather x46 -> x0, local copies, waits for them, and re-layouts: 79.6 us -> none  [couple(): picked = window[positions[:, slot_idx]]]
    pallas_call x0 -> x7, Pallas kernels: none -> 45.5 us  [the longest x2 14.1 us: turn(): pl.pallas_call(turn_kernel, grid=(rows // part,), in_specs=[pl.BlockSpec(...]
    ppermute x12 -> x13, starting transfers between devices: 59.6 us -> 19 us  [swap(): return lax.ppermute(value, 'leaf', pairs)]
    slice x25 -> x0, local copies, waits for them, and re-layouts: 36.3 us -> none  [the longest x6 23.2 us: couple(): blocks[:, slot_idx]]
    ppermute x12 -> x13, waiting for transfers between devices: 0.03 us -> 29.2 us  [swap(): return lax.ppermute(value, 'leaf', pairs)]
    gather x30 -> x0, other arithmetic: 23.6 us -> none  [couple(): picked = window[positions[:, slot_idx]]]
  transfers between devices with their start and end apart: 13 -> 13, of which waited for: 0 -> 8; matrix products, arithmetic and copies ran while one was open for 61% -> 1% of each run, Pallas kernels for 0% -> 33%
where the time goes in v2:
time: 106 us; the launch traced here: 105 us
  Pallas kernels  45.5 us (43%)
  waiting for transfers between devices  29.2 us (28%)
  starting transfers between devices  19 us (18%)
  local copies, waits for them, and re-layouts  10.1 us (10%)
    ppermute x13, waiting for transfers between devices, swap(): return lax.ppermute(value, 'leaf', pairs)  29.2 us
    ppermute x13, starting transfers between devices, swap(): return lax.ppermute(value, 'leaf', pairs)  19 us
    pallas_call x2, Pallas kernels, turn(): pl.pallas_call(turn_kernel, grid=(rows // part,), in_specs=[pl.BlockSpec(...  14.1 us
    unnamed x36, local copies, waits for them, and re-layouts  10 us
    pallas_call x1, Pallas kernels, downward(): pl.pallas_call(lambda *refs: down_kernel(len(lhs), *refs), in_specs=[pl.B...  9.61 us
    pallas_call x1, Pallas kernels, leaf_rows(): pl.pallas_call(lambda *refs: rows_kernel(len(lhs), len(pieces), *refs), g...  7.79 us
    pallas_call x1, Pallas kernels, upward(): pl.pallas_call(upward_kernel, in_specs=[pl.BlockSpec(memory_space=pltpu.S...  7.19 us
    pallas_call x1, Pallas kernels, top(): pl.pallas_call(top_kernel, in_specs=[sm, sm, ANY, ANY, hbm, hbm], out_sha...  4.18 us
  transfers between devices with their start and end apart: 13, of which 8 were waited for; matrix products, arithmetic and copies ran while one was open for 1% of the time, Pallas kernels for 33%

profile of v2, /device:TPU:6, one launch (start us, length us, event | category | flops | bytes accessed | tf_op | source)
XLA Modules:
  0.0 104.8 jit_solution(900341065314168012)
XLA Ops:
  0.0 1.6 %copy-done = bf16[8192,128]{1,0:T(8,128)(2,1)S(1)} copy-done((bf16[8192,128]{1,0:T(8,128)(2,1)S(1)}, bf16[8192,128]{1,0:T(8,128)(2,1)}, u32[]{:S(2)}) %copy-start) | copy-done | bytes 2097176
  1.6 2.6 %split.1 = (bf16[3584,128]{1,0:T(8,128)(2,1)}, bf16[4608,128]{1,0:T(8,128)(2,1)}) custom-call(bf16[8192,128]{1,0:T(8,128)(2,1)S(1)} %copy-done), custom_call_target="tpu_custom_call" | custom-call | bytes 80000 | tf_op jit(solution)/shard_map/split/pallas_call | solution.py:417
  4.2 8.1 %collective-permute-start.2 = (bf16[3584,128]{1,0:T(8,128)(2,1)}, bf16[3584,128]{1,0:T(8,128)(2,1)S(1)}, u32[]{:S(2)}, u32[]{:S(2)}) collective-permute-start(bf16[3584,128]{1,0:T(8,128)(2,1)} %get-tuple-element.18), channel_id=1, source_target_pairs={{1,2},{3,4},{5,6},{7,8},{9,10},{11,12},{13,14},{15,16},{17,18},{19... | collective-permute-start | bytes 2752520 | tf_op jit(solution)/shard_map/ppermute | solution.py:451
  12.4 1.0 copy-done.4
  13.4 1.0 copy-done.6
  14.4 7.2 %upward.1 = (bf16[8192,128]{1,0:T(8,128)(2,1)}, f32[16,128]{1,0:T(8,128)S(1)}, f32[16,128]{1,0:T(8,128)S(1)}) custom-call(s32[1]{0:T(128)} %bitcast.2.me.where_am_i, bf16[8192,128]{1,0:T(8,128)(2,1)S(1)} %copy-done.1, bf16[64,32,128]{2,1,0:T(8,128)(2,1)S(1)} %bitcast.19, bf16[32,32,255]{2,1,0:T(8,128)(2,1)S(1)} %bitcast.17), custom_call_target="tpu_custom_call" | custom-call | bytes 280000 | tf_op jit(solution)/shard_map/upward/pallas_call | solution.py:161
  21.8 1.2 %collective-permute-done = f32[16,128]{1,0:T(8,128)S(1)} collective-permute-done((f32[16,128]{1,0:T(8,128)S(1)}, f32[16,128]{1,0:T(8,128)S(1)}, u32[]{:S(2)}, u32[]{:S(2)}) %collective-permute-start) | collective-permute-done | bytes 8224 | tf_op jit(solution)/shard_map/ppermute | solution.py:451
  22.9 3.6 %collective-permute-done.1 = bf16[16,128]{1,0:T(8,128)(2,1)S(1)} collective-permute-done((bf16[16,128]{1,0:T(8,128)(2,1)S(1)}, bf16[16,128]{1,0:T(8,128)(2,1)S(1)}, u32[]{:S(2)}, u32[]{:S(2)}) %collective-permute-start.1) | collective-permute-done | bytes 4128 | tf_op jit(solution)/shard_map/ppermute | solution.py:451
  26.6 4.8 %collective-permute-done.3 = bf16[32,128]{1,0:T(8,128)(2,1)S(1)} collective-permute-done((bf16[32,128]{1,0:T(8,128)(2,1)S(1)}, bf16[32,128]{1,0:T(8,128)(2,1)S(1)}, u32[]{:S(2)}, u32[]{:S(2)}) %collective-permute-start.3) | collective-permute-done | bytes 8224 | tf_op jit(solution)/shard_map/ppermute | solution.py:451
  31.4 3.7 %collective-permute-done.4 = bf16[64,128]{1,0:T(8,128)(2,1)S(1)} collective-permute-done((bf16[64,128]{1,0:T(8,128)(2,1)S(1)}, bf16[64,128]{1,0:T(8,128)(2,1)S(1)}, u32[]{:S(2)}, u32[]{:S(2)}) %collective-permute-start.4) | collective-permute-done | bytes 16416 | tf_op jit(solution)/shard_map/ppermute | solution.py:451
  35.3 5.0 %collective-permute-done.5 = bf16[128,128]{1,0:T(8,128)(2,1)S(1)} collective-permute-done((bf16[128,128]{1,0:T(8,128)(2,1)S(1)}, bf16[128,128]{1,0:T(8,128)(2,1)S(1)}, u32[]{:S(2)}, u32[]{:S(2)}) %collective-permute-start.5) | collective-permute-done | bytes 32800 | tf_op jit(solution)/shard_map/ppermute | solution.py:451
  40.8 3.7 %collective-permute-done.6 = bf16[256,128]{1,0:T(8,128)(2,1)S(1)} collective-permute-done((bf16[256,128]{1,0:T(8,128)(2,1)S(1)}, bf16[256,128]{1,0:T(8,128)(2,1)S(1)}, u32[]{:S(2)}, u32[]{:S(2)}) %collective-permute-start.6) | collective-permute-done | bytes 65568 | tf_op jit(solution)/shard_map/ppermute | solution.py:451
  44.7 6.2 %collective-permute-done.7 = bf16[512,128]{1,0:T(8,128)(2,1)S(1)} collective-permute-done((bf16[512,128]{1,0:T(8,128)(2,1)S(1)}, bf16[512,128]{1,0:T(8,128)(2,1)S(1)}, u32[]{:S(2)}, u32[]{:S(2)}) %collective-permute-start.7) | collective-permute-done | bytes 131104 | tf_op jit(solution)/shard_map/ppermute | solution.py:451
  51.6 1.9 %collective-permute-start.9 = (bf16[8192,128]{1,0:T(8,128)(2,1)}, bf16[8192,128]{1,0:T(8,128)(2,1)}, u32[]{:S(2)}, u32[]{:S(2)}) collective-permute-start(bf16[8192,128]{1,0:T(8,128)(2,1)} %get-tuple-element.24.refs_1_), channel_id=1, source_target_pairs={{1,2},{3,4},{5,6},{7,8},{9,10},{11,12},{13,14},{15,16},{17,18},{19... | collective-permute-start | bytes 6291464 | tf_op jit(solution)/shard_map/ppermute | solution.py:451
  53.6 7.9 %collective-permute-start.12 = (bf16[4608,128]{1,0:T(8,128)(2,1)}, bf16[4608,128]{1,0:T(8,128)(2,1)}, u32[]{:S(2)}, u32[]{:S(2)}) collective-permute-start(bf16[4608,128]{1,0:T(8,128)(2,1)} %get-tuple-element.30), channel_id=1, source_target_pairs={{1,2},{3,4},{5,6},{7,8},{9,10},{11,12},{13,14},{15,16},{17,18},{19... | collective-permute-start | bytes 3538952 | tf_op jit(solution)/shard_map/ppermute | solution.py:451
  62.3 1.0 collective-permute-done.10.mate_in
  63.3 1.6 %copy-done.3 = bf16[128,8,32,32]{0,3,2,1:T(8,128)(2,1)S(1)} copy-done((bf16[128,8,32,32]{0,3,2,1:T(8,128)(2,1)S(1)}, bf16[128,8,32,32]{0,3,2,1:T(8,128)(2,1)}, u32[]{:S(2)}) %copy-start.3) | copy-done | bytes 2097176
  64.9 0.9 copy-done.9
  66.8 4.2 %top.1.refs_4_ = bf16[32,128]{1,0:T(8,128)(2,1)S(1)} custom-call(s32[1]{0:T(128)} %bitcast.2.me.where_am_i, s32[8,128]{1,0:T(8,128)S(1)} %bitcast.22, bf16[1024,128]{1,0:T(8,128)(2,1)S(1)} %copy-done.9, bf16[1024,128]{1,0:T(8,128)(2,1)S(1)} %collective-permute-done.10.mate_in, bf16[32,32,128]{2,1,0:T(8,128)(2,1)S(1)} %bitcast.21, ...), custom_call_target="tpu_custom_call" | custom-call | bytes 160000 | tf_op jit(solution)/shard_map/top/pallas_call | solution.py:249
  71.0 2.2 %copy-done.2 = bf16[255,8,32,32]{0,3,2,1:T(8,128)(2,1)S(1)} copy-done((bf16[255,8,32,32]{0,3,2,1:T(8,128)(2,1)S(1)}, bf16[255,8,32,32]{0,3,2,1:T(8,128)(2,1)}, u32[]{:S(2)}) %copy-start.2) | copy-done | bytes 4177944
  73.2 6.2 %coupling_turn.1.refs_5_ = bf16[256,32,288]{2,1,0:T(8,128)(2,1)S(1)} custom-call(bf16[8,32,32,255]{3,2,1,0:T(8,128)(2,1)S(1)} %bitcast.15, bf16[32,32,255]{2,1,0:T(8,128)(2,1)S(1)} %bitcast.18), custom_call_target="tpu_custom_call" | custom-call | bytes 320000 | tf_op jit(solution)/shard_map/coupling_turn/pallas_call | solution.py:91
  79.4 7.9 %near_turn.1.refs_2_ = bf16[128,64,416]{2,1,0:T(8,128)(2,1)S(1)} custom-call(bf16[6,64,64,128]{3,2,1,0:T(8,128)(2,1)S(1)} %bitcast.14, bf16[64,32,128]{2,1,0:T(8,128)(2,1)S(1)} %bitcast.20), custom_call_target="tpu_custom_call" | custom-call | bytes 320000 | tf_op jit(solution)/shard_map/near_turn/pallas_call | solution.py:91
  87.4 9.6 %downward.1.refs_1_ = bf16[4096,128]{1,0:T(8,128)(2,1)S(1)} custom-call(s32[8,255]{1,0:T(8,128)S(1)} %select_bitcast_fusion.refs_0_, bf16[8192,128]{1,0:T(8,128)(2,1)} %get-tuple-element.24.refs_1_, bf16[8192,128]{1,0:T(8,128)(2,1)} %collective-permute-done.8.refs_2_, bf16[8192,128]{1,0:T(8,128)(2,1)} %collective-permute-done.9.refs_3_, ...), custom_call_target="tpu_custom_call" | custom-call | bytes 360000 | tf_op jit(solution)/shard_map/downward/pallas_call | solution.py:327
  97.0 7.8 %leaf_rows.1 = bf16[8192,128]{1,0:T(8,128)(2,1)} custom-call(s32[6,128]{1,0:T(8,128)S(1)} %select_bitcast_fusion.1.refs_0_, bf16[4096,128]{1,0:T(8,128)(2,1)S(1)} %downward.1.refs_1_, bf16[128,64,416]{2,1,0:T(8,128)(2,1)S(1)} %near_turn.1.refs_2_, bf16[8192,128]{1,0:T(8,128)(2,1)S(1)} %copy-done.1, bf16[8192,128]{1,0:T(8,128)(2,1)} %collective-permute-done.11.refs_4_, ...), custom_call_target="tpu_custom_call" | custom-call | bytes 240000 | tf_op jit(solution)/shard_map/leaf_rows/pallas_call | solution.py:377
  (55 shorter events, 3.6 us)
Async XLA Ops:
  0.0 1.6 %copy-start = (bf16[8192,128]{1,0:T(8,128)(2,1)S(1)}, bf16[8192,128]{1,0:T(8,128)(2,1)}, u32[]{:S(2)}) copy-start(bf16[8192,128]{1,0:T(8,128)(2,1)} %refs_3_.1) | copy-start | bytes 6291460
  1.6 10.8 %copy-start.1 = (bf16[8192,128]{1,0:T(8,128)(2,1)S(1)}, bf16[8192,128]{1,0:T(8,128)(2,1)}, u32[]{:S(2)}) copy-start(bf16[8192,128]{1,0:T(8,128)(2,1)} %refs_3_.1) | copy-start | bytes 6291460
  4.2 57.4 %copy-start.12 = (s32[255,8]{0,1:T(8,128)S(1)}, s32[255,8]{0,1:T(8,128)}, u32[]{:S(2)}) copy-start(s32[255,8]{0,1:T(8,128)} %param.17) | copy-start | bytes 24484
  4.2 59.1 %copy-start.11 = (s32[128,8]{0,1:T(8,128)S(1)}, s32[128,8]{0,1:T(8,128)}, u32[]{:S(2)}) copy-start(s32[128,8]{0,1:T(8,128)} %param.19) | copy-start | bytes 12292
  4.2 22.3 %collective-permute-start.2 = (bf16[3584,128]{1,0:T(8,128)(2,1)}, bf16[3584,128]{1,0:T(8,128)(2,1)S(1)}, u32[]{:S(2)}, u32[]{:S(2)}) collective-permute-start(bf16[3584,128]{1,0:T(8,128)(2,1)} %get-tuple-element.18), channel_id=1, source_target_pairs={{1,2},{3,4},{5,6},{7,8},{9,10},{11,12},{13,14},{15,16},{17,18},{19... | collective-permute-start | bytes 2752520 | tf_op jit(solution)/shard_map/ppermute | solution.py:451
  14.4 47.1 %copy-start.13 = (s32[128,6]{0,1:T(8,128)S(1)}, s32[128,6]{0,1:T(8,128)}, u32[]{:S(2)}) copy-start(s32[128,6]{0,1:T(8,128)} %param.21) | copy-start | bytes 9220
  21.6 49.3 %copy-start.5 = (bf16[255,32,32]{0,2,1:T(8,128)(2,1)S(1)}, bf16[255,32,32]{0,2,1:T(8,128)(2,1)}, u32[]{:S(2)}) copy-start(bf16[255,32,32]{0,2,1:T(8,128)(2,1)} %param.14) | copy-start | bytes 1566724
  21.7 1.3 %collective-permute-start = (f32[16,128]{1,0:T(8,128)S(1)}, f32[16,128]{1,0:T(8,128)S(1)}, u32[]{:S(2)}, u32[]{:S(2)}) collective-permute-start(f32[16,128]{1,0:T(8,128)S(1)} %get-tuple-element.22), channel_id=1, source_target_pairs={{0,1},{1,0},{2,3},{3,2},{4,5},{5,4},{6,7},{7,6},{8,9},{9,8},{10,11... | collective-permute-start | bytes 24584 | tf_op jit(solution)/shard_map/ppermute | solution.py:451
  22.9 3.6 %collective-permute-start.1 = (bf16[16,128]{1,0:T(8,128)(2,1)S(1)}, bf16[16,128]{1,0:T(8,128)(2,1)S(1)}, u32[]{:S(2)}, u32[]{:S(2)}) collective-permute-start(bf16[16,128]{1,0:T(8,128)(2,1)S(1)} %add_convert_fusion), channel_id=1, source_target_pairs={{0,2},{1,3},{2,0},{3,1},{4,6},{5,7},{6,4},{7,5},{8,10},{9,11},{10,... | collective-permute-start | bytes 12296 | tf_op jit(solution)/shard_map/ppermute | solution.py:451
  26.5 4.9 %collective-permute-start.3 = (bf16[32,128]{1,0:T(8,128)(2,1)S(1)}, bf16[32,128]{1,0:T(8,128)(2,1)S(1)}, u32[]{:S(2)}, u32[]{:S(2)}) collective-permute-start(bf16[32,128]{1,0:T(8,128)(2,1)S(1)} %pad_maximum_fusion.3), channel_id=1, source_target_pairs={{0,6},{1,7},{2,4},{3,5},{4,2},{5,3},{6,0},{7,1},{8,14},{9,15},{10,... | collective-permute-start | bytes 24584 | tf_op jit(solution)/shard_map/ppermute | solution.py:451
  31.4 3.7 %collective-permute-start.4 = (bf16[64,128]{1,0:T(8,128)(2,1)S(1)}, bf16[64,128]{1,0:T(8,128)(2,1)S(1)}, u32[]{:S(2)}, u32[]{:S(2)}) collective-permute-start(bf16[64,128]{1,0:T(8,128)(2,1)S(1)} %pad_maximum_fusion.2), channel_id=1, source_target_pairs={{0,8},{1,9},{2,10},{3,11},{4,12},{5,13},{6,14},{7,15},{8,0},{9,1},... | collective-permute-start | bytes 49160 | tf_op jit(solution)/shard_map/ppermute | solution.py:451
  35.1 5.1 %collective-permute-start.5 = (bf16[128,128]{1,0:T(8,128)(2,1)S(1)}, bf16[128,128]{1,0:T(8,128)(2,1)S(1)}, u32[]{:S(2)}, u32[]{:S(2)}) collective-permute-start(bf16[128,128]{1,0:T(8,128)(2,1)S(1)} %pad_maximum_fusion.1), channel_id=1, source_target_pairs={{0,24},{1,25},{2,26},{3,27},{4,28},{5,29},{6,30},{7,31},{8,16},{9,... | collective-permute-start | bytes 98312 | tf_op jit(solution)/shard_map/ppermute | solution.py:451
  40.3 4.3 %collective-permute-start.6 = (bf16[256,128]{1,0:T(8,128)(2,1)S(1)}, bf16[256,128]{1,0:T(8,128)(2,1)S(1)}, u32[]{:S(2)}, u32[]{:S(2)}) collective-permute-start(bf16[256,128]{1,0:T(8,128)(2,1)S(1)} %pad_maximum_fusion), channel_id=1, source_target_pairs={{0,32},{1,33},{2,34},{3,35},{4,36},{5,37},{6,38},{7,39},{8,40},{9,... | collective-permute-start | bytes 196616 | tf_op jit(solution)/shard_map/ppermute | solution.py:451
  44.6 6.3 %collective-permute-start.7 = (bf16[512,128]{1,0:T(8,128)(2,1)S(1)}, bf16[512,128]{1,0:T(8,128)(2,1)S(1)}, u32[]{:S(2)}, u32[]{:S(2)}) collective-permute-start(bf16[512,128]{1,0:T(8,128)(2,1)S(1)} %get-tuple-element.31), channel_id=1, source_target_pairs={{0,96},{1,97},{2,98},{3,99},{4,100},{5,101},{6,102},{7,103},{8,104... | collective-permute-start | bytes 393224 | tf_op jit(solution)/shard_map/ppermute | solution.py:451
  50.9 36.5 %collective-permute-start.8 = (bf16[8192,128]{1,0:T(8,128)(2,1)}, bf16[8192,128]{1,0:T(8,128)(2,1)}, u32[]{:S(2)}, u32[]{:S(2)}) collective-permute-start(bf16[8192,128]{1,0:T(8,128)(2,1)} %get-tuple-element.24.refs_1_), channel_id=1, source_target_pairs={{0,1},{1,0},{2,3},{3,2},{4,5},{5,4},{6,7},{7,6},{8,9},{9,8},{10,11... | collective-permute-start | bytes 6291464 | tf_op jit(solution)/shard_map/ppermute | solution.py:451
  51.6 35.8 %collective-permute-start.9 = (bf16[8192,128]{1,0:T(8,128)(2,1)}, bf16[8192,128]{1,0:T(8,128)(2,1)}, u32[]{:S(2)}, u32[]{:S(2)}) collective-permute-start(bf16[8192,128]{1,0:T(8,128)(2,1)} %get-tuple-element.24.refs_1_), channel_id=1, source_target_pairs={{1,2},{3,4},{5,6},{7,8},{9,10},{11,12},{13,14},{15,16},{17,18},{19... | collective-permute-start | bytes 6291464 | tf_op jit(solution)/shard_map/ppermute | solution.py:451
  53.5 43.5 %collective-permute-start.11 = (bf16[8192,128]{1,0:T(8,128)(2,1)S(1)}, bf16[8192,128]{1,0:T(8,128)(2,1)}, u32[]{:S(2)}, u32[]{:S(2)}) collective-permute-start(bf16[8192,128]{1,0:T(8,128)(2,1)S(1)} %copy-done.1), channel_id=1, source_target_pairs={{0,1},{1,0},{2,3},{3,2},{4,5},{5,4},{6,7},{7,6},{8,9},{9,8},{10,11... | collective-permute-start | bytes 6291464 | tf_op jit(solution)/shard_map/ppermute | solution.py:451
  53.6 43.4 %collective-permute-start.12 = (bf16[4608,128]{1,0:T(8,128)(2,1)}, bf16[4608,128]{1,0:T(8,128)(2,1)}, u32[]{:S(2)}, u32[]{:S(2)}) collective-permute-start(bf16[4608,128]{1,0:T(8,128)(2,1)} %get-tuple-element.30), channel_id=1, source_target_pairs={{1,2},{3,4},{5,6},{7,8},{9,10},{11,12},{13,14},{15,16},{17,18},{19... | collective-permute-start | bytes 3538952 | tf_op jit(solution)/shard_map/ppermute | solution.py:451
  61.5 1.8 %collective-permute-start.10 = (bf16[1024,128]{1,0:T(8,128)(2,1)}, bf16[1024,128]{1,0:T(8,128)(2,1)S(1)}, u32[]{:S(2)}, u32[]{:S(2)}) collective-permute-start(bf16[1024,128]{1,0:T(8,128)(2,1)} %copy-done.8), channel_id=1, source_target_pairs={{0,1},{1,0},{2,3},{3,2},{4,5},{5,4},{6,7},{7,6},{8,9},{9,8},{10,11... | collective-permute-start | bytes 786440 | tf_op jit(solution)/shard_map/ppermute | solution.py:451
  63.3 1.6 %copy-start.3 = (bf16[128,8,32,32]{0,3,2,1:T(8,128)(2,1)S(1)}, bf16[128,8,32,32]{0,3,2,1:T(8,128)(2,1)}, u32[]{:S(2)}) copy-start(bf16[128,8,32,32]{0,3,2,1:T(8,128)(2,1)} %param.18) | copy-start | bytes 6291460
  66.8 12.6 %slice-start = ((s8[6291456]{0:T(1024)(128)(4,1)}), s8[4194304]{0:T(1024)(128)(4,1)S(1)}, s32[]{:S(2)}) async-start(s8[6291456]{0:T(1024)(128)(4,1)} %bitcast.12), calls=%async_computation | async-start | bytes 8388608
  71.0 2.2 %copy-start.2 = (bf16[255,8,32,32]{0,3,2,1:T(8,128)(2,1)S(1)}, bf16[255,8,32,32]{0,3,2,1:T(8,128)(2,1)}, u32[]{:S(2)}) copy-start(bf16[255,8,32,32]{0,3,2,1:T(8,128)(2,1)} %param.16) | copy-start | bytes 12533764
  73.2 6.2 %slice-start.1 = ((s8[6291456]{0:T(1024)(128)(4,1)}), s8[2097152]{0:T(1024)(128)(4,1)S(1)}, s32[]{:S(2)}) async-start(s8[6291456]{0:T(1024)(128)(4,1)} %bitcast.12), calls=%async_computation.1 | async-start | bytes 4194304
  73.2 6.2 %copy-start.7 = (bf16[128,64,32]{0,2,1:T(8,128)(2,1)S(1)}, bf16[128,64,32]{0,2,1:T(8,128)(2,1)}, u32[]{:S(2)}) copy-start(bf16[128,64,32]{0,2,1:T(8,128)(2,1)} %param.13) | copy-start | bytes 1572868
  (5 other events, 4.7 us)

commit v3 on v2

--- a/solution.py
+++ b/solution.py
@@ -15,6 +15,7 @@
 FIRST = 7
 SCALE = 40000
 VMEM = 28 << 20
+MOST = 50 << 20
 ANY = pl.BlockSpec(memory_space=pl.ANY)
 
 
@@ -102,7 +103,7 @@
     )(blocks_t, extra_t)
 
 
-def upward_kernel(me, points_in, basis_in, transfer_in, coeff, keep, give, points, basis, transfer, wide_b, wide_e, sems):
+def upward_kernel(me, points_in, basis_in, transfer_in, coeff, keep, give, late, points, basis, transfer, wide_b, wide_e, sems):
     size, rank, leaves = basis.shape
     copies = [pltpu.make_async_copy(src, dst, sems.at[n])
               for n, (src, dst) in enumerate(((basis_in, basis), (transfer_in, transfer), (points_in, points)))]
@@ -120,6 +121,8 @@
     batch(rank, 16, lambda r: (transfer[r],), lambda b: dot(ident_e, b, NT), lambda r, v: put(wide_e, r * step_e, v))
 
     copies[2].wait()
+    send = pltpu.make_async_copy(points.at[pl.ds(points.shape[0] - late.shape[0], late.shape[0])], late, sems.at[3])
+    send.start()
 
     def store_leaf(leaf, got):
         coeff[rows_at(leaves - 1 + leaf, rank), :] = got
@@ -151,10 +154,11 @@
     odd = (me[0] & 1) == 1
     keep[...] = jnp.where(odd, high, low)
     give[...] = jnp.where(odd, low, high)
+    send.wait()
     coeff[pl.ds(nodes * rank, rank), :] = jnp.zeros((rank, coeff.shape[1]), BF)
 
 
-def upward(me, points, basis_t, transfer_t):
+def upward(me, points, basis_t, transfer_t, cut):
     size, rank, leaves = basis_t.shape
     padded = transfer_t.shape[2] + 1
     vecs = points.shape[1]
@@ -162,11 +166,13 @@
         upward_kernel,
         in_specs=[pl.BlockSpec(memory_space=pltpu.SMEM)] + [pl.BlockSpec(memory_space=pltpu.HBM)] * 3,
         out_shape=(jax.ShapeDtypeStruct((padded * rank, vecs), BF),)
-        + (jax.ShapeDtypeStruct((rank // 2, vecs), F32),) * 2,
+        + (jax.ShapeDtypeStruct((rank // 2, vecs), F32),) * 2
+        + (jax.ShapeDtypeStruct((points.shape[0] - cut, vecs), BF),),
+        out_specs=[pl.BlockSpec(memory_space=pltpu.VMEM)] * 3 + [pl.BlockSpec(memory_space=pltpu.HBM)],
         scratch_shapes=[pltpu.VMEM(points.shape, BF), pltpu.VMEM(basis_t.shape, BF), pltpu.VMEM(transfer_t.shape, BF),
                         pltpu.VMEM((1, size * (leaves + PAD), 128), F32),
-                        pltpu.VMEM((1, rank * (padded + PAD), 128), F32), pltpu.SemaphoreType.DMA((3,))],
-        compiler_params=pltpu.CompilerParams(vmem_limit_bytes=VMEM),
+                        pltpu.VMEM((1, rank * (padded + PAD), 128), F32), pltpu.SemaphoreType.DMA((4,))],
+        compiler_params=pltpu.CompilerParams(vmem_limit_bytes=MOST),
         cost_estimate=cost(7),
         name="upward",
     )(me, points, basis_t, transfer_t)
@@ -259,29 +265,32 @@
     )(me, lists_t, mine, mate, transfer_t, coupling_t)
 
 
-def down_kernel(parts, pos, own, mate, other, above, *refs):
-    lhs_in, (out, *lhs), (window, down, sems) = refs[:parts], refs[parts:2 * parts + 1], refs[2 * parts + 1:]
-    nodes, _, width = lhs[0].shape
-    rank = above.shape[0]
-
-    def lhs_of(node):
-        return jnp.concatenate([a[node] for a in lhs], axis=0)
-
-    nodes = nodes - 1
+def down_kernel(pos, blocks_in, transfer_in, own, mate, other, above, out, blocks, transfer, window, wide, down, sems):
+    slots, rank, _, nodes = blocks.shape
     leaves = (nodes + 1) // 2
-    slots = width // rank - 1
     rows = (nodes - FIRST) * rank
-    half = nodes // 2
-    lhs_copies = [[pltpu.make_async_copy(src.at[pl.ds(at, size)], dst.at[pl.ds(at, size)], sems.at[3 + 2 * n + k])
-                   for n, (src, dst) in enumerate(zip(lhs_in, lhs))]
-                  for k, (at, size) in enumerate(((0, half), (half, nodes + 1 - half)))]
-    copies = [pltpu.make_async_copy(src.at[pl.ds(FIRST * rank, rows)], window.at[pl.ds(n * rows, rows)], sems.at[n])
-              for n, src in enumerate((own, mate, other))]
-    for c in lhs_copies[0] + copies + lhs_copies[1]:
+    part = rank // PARTS
+    step = nodes + 1 + PAD
+    width = (slots + 1) * rank
+    chunks = wide.shape[0]
+    ident = eye(nodes + 1, nodes)
+
+    load_transfer = pltpu.make_async_copy(transfer_in, transfer, sems.at[0])
+    load_blocks = [pltpu.make_async_copy(blocks_in.at[:, pl.ds(p * part, part)], blocks.at[:, pl.ds(p * part, part)],
+                                         sems.at[1 + p]) for p in range(PARTS)]
+    load_window = [pltpu.make_async_copy(src.at[pl.ds(FIRST * rank, rows)], window.at[pl.ds(n * rows, rows)],
+                                         sems.at[1 + PARTS + n]) for n, src in enumerate((own, mate, other))]
+    for c in [load_transfer] + load_blocks + load_window:
         c.start()
     window[3 * rows:3 * rows + rank, :] = jnp.zeros((rank, window.shape[1]), BF)
-    for c in lhs_copies[0]:
-        c.wait()
+    load_transfer.wait()
+    for p in range(PARTS):
+        load_blocks[p].wait()
+        batch(part, 8,
+              lambda r, p=p: (jnp.concatenate(
+                  [blocks[:, p * part + r].reshape(slots * rank, nodes), transfer[p * part + r]], axis=0),),
+              lambda both: dot(ident, both, NT),
+              lambda r, turned, p=p: put(wide, (p * part + r) * step, turned))
 
     def parent_of(node):
         if isinstance(node, int):
@@ -289,16 +298,22 @@
         return down[rows_at(lax.shift_right_logical(node - 1, 1), rank), :]
 
     for node in range(FIRST):
-        down[rows_at(node, rank), :] = dot(lhs_of(node)[:, slots * rank:], parent_of(node)).astype(BF)
-    for c in copies:
+        mine = wide[chunks - 1, pl.ds(node, rank, stride=step), :].astype(BF)[:, 0:rank]
+        down[rows_at(node, rank), :] = dot(mine, parent_of(node)).astype(BF)
+    for c in load_window:
         c.wait()
+
+    def work(mine, rhs):
+        lhs = jnp.concatenate([m.astype(BF) for m in mine], axis=1)[:, 0:width]
+        return dot(lhs, rhs).astype(BF)
 
     count = FIRST + 1
     while count <= leaves:
         def load(p, count=count):
             node = count - 1 + p
-            return lhs_of(node), jnp.concatenate(
-                [window[rows_at(pos[s, node], rank), :] for s in range(slots)] + [parent_of(node)], axis=0)
+            return ([wide[j, pl.ds(node, rank, stride=step), :] for j in range(chunks)],
+                    jnp.concatenate([window[rows_at(pos[s, node], rank), :] for s in range(slots)]
+                                    + [parent_of(node)], axis=0))
 
         def store(p, got, count=count):
             if count == leaves:
@@ -306,35 +321,32 @@
             else:
                 down[rows_at(count - 1 + p, rank), :] = got
 
-        if count == leaves:
-            for c in lhs_copies[1]:
-                c.wait()
-        batch(count, DB, load, lambda a, b: dot(a, b).astype(BF), store)
+        batch(count, 32, load, work, store)
         count *= 2
 
 
-DB = 32
-
-
-def downward(pos, lhs, own, mate, other, above):
-    nodes = lhs[0].shape[0]
-    rank = above.shape[0]
-    leaves = nodes // 2
+PARTS = 4
+
+
+def downward(pos, blocks_t, transfer_t, own, mate, other, above):
+    slots, rank, _, nodes = blocks_t.shape
+    leaves = (nodes + 1) // 2
     vecs = own.shape[1]
-    any_ = pl.BlockSpec(memory_space=pltpu.HBM)
-    vm = pl.BlockSpec(memory_space=pltpu.VMEM)
-    rows = (nodes - 1 - FIRST) * rank
+    rows = (nodes - FIRST) * rank
+    chunks = ((slots + 1) * rank + 127) // 128
+    hbm = pl.BlockSpec(memory_space=pltpu.HBM)
     return pl.pallas_call(
-        lambda *refs: down_kernel(len(lhs), *refs),
-        in_specs=[pl.BlockSpec(memory_space=pltpu.SMEM), any_, any_, any_, vm] + [any_] * len(lhs),
+        down_kernel,
+        in_specs=[pl.BlockSpec(memory_space=pltpu.SMEM)] + [hbm] * 5 + [pl.BlockSpec(memory_space=pltpu.VMEM)],
         out_shape=jax.ShapeDtypeStruct((leaves * rank, vecs), BF),
-        scratch_shapes=[pltpu.VMEM(a.shape, BF) for a in lhs]
-        + [pltpu.VMEM((3 * rows + rank, vecs), BF), pltpu.VMEM((leaves * rank, vecs), BF),
-           pltpu.SemaphoreType.DMA((3 + 2 * len(lhs),))],
-        compiler_params=pltpu.CompilerParams(vmem_limit_bytes=VMEM),
-        cost_estimate=cost(9),
+        scratch_shapes=[pltpu.VMEM(blocks_t.shape, BF), pltpu.VMEM(transfer_t.shape, BF),
+                        pltpu.VMEM((3 * rows + rank, vecs), BF),
+                        pltpu.VMEM((chunks, rank * (nodes + 1 + PAD), 128), F32),
+                        pltpu.VMEM((leaves * rank, vecs), BF), pltpu.SemaphoreType.DMA((4 + PARTS,))],
+        compiler_params=pltpu.CompilerParams(vmem_limit_bytes=40 << 20),
+        cost_estimate=cost(11),
         name="downward",
-    )(pos, own, mate, other, above, *lhs)
+    )(pos, blocks_t, transfer_t, own, mate, other, above)
 
 
 def rows_kernel(parts, count, pos, down, *refs):
@@ -391,17 +403,12 @@
     )(pos, down, *lhs, *pieces)
 
 
-def split_kernel(src, early, late, held, sems):
-    jobs, at = [], 0
-    for dst in (early, late):
-        for start in range(0, dst.shape[0], 1536):
-            size = min(1536, dst.shape[0] - start)
-            jobs.append((at + start, size, dst, start))
-        at += dst.shape[0]
-    into = [pltpu.make_async_copy(src.at[pl.ds(a, size)], held.at[pl.ds(a, size)], sems.at[0, n])
-            for n, (a, size, _, _) in enumerate(jobs)]
-    back = [pltpu.make_async_copy(held.at[pl.ds(a, size)], dst.at[pl.ds(b, size)], sems.at[1, n])
-            for n, (a, size, dst, b) in enumerate(jobs)]
+def head_kernel(src, dst, held, sems):
+    rows = dst.shape[0]
+    part = rows // 4
+    at = [pl.ds(n * part, part) for n in range(4)]
+    into = [pltpu.make_async_copy(src.at[a], held.at[a], sems.at[0, n]) for n, a in enumerate(at)]
+    back = [pltpu.make_async_copy(held.at[a], dst.at[a], sems.at[1, n]) for n, a in enumerate(at)]
     for c in into:
         c.start()
     for c, d in zip(into, back):
@@ -411,18 +418,18 @@
         d.wait()
 
 
-def split(value, cut):
-    rows, vecs = value.shape
+def head(value, rows):
+    vecs = value.shape[1]
     hbm = pl.BlockSpec(memory_space=pltpu.HBM)
     return pl.pallas_call(
-        split_kernel,
+        head_kernel,
         in_specs=[hbm],
-        out_specs=[hbm, hbm],
-        out_shape=[jax.ShapeDtypeStruct((cut, vecs), BF), jax.ShapeDtypeStruct((rows - cut, vecs), BF)],
-        scratch_shapes=[pltpu.VMEM((rows, vecs), BF), pltpu.SemaphoreType.DMA((2, rows // 1536 + 3))],
-        compiler_params=pltpu.CompilerParams(vmem_limit_bytes=VMEM),
+        out_specs=hbm,
+        out_shape=jax.ShapeDtypeStruct((rows, vecs), BF),
+        scratch_shapes=[pltpu.VMEM((rows, vecs), BF), pltpu.SemaphoreType.DMA((2, 4))],
+        compiler_params=pltpu.CompilerParams(vmem_limit_bytes=MOST),
         cost_estimate=cost(2),
-        name="split",
+        name="head",
     )(value)
 
 
@@ -459,37 +466,36 @@
     coup_t = jnp.transpose(local_coupling, (1, 2, 3, 0))
     near_t = jnp.transpose(near_blocks, (1, 2, 3, 0))
     coup_t = jnp.transpose(local_coupling, (1, 2, 3, 0))
-    early, late = split(points, CUT * leaf_size)
+    cut = CUT * leaf_size
+    early = head(points, cut)
     early_other = swap(early, others)
-    coeff, keep, give = upward(own[None], after(points, early), basis_t, transfer_t)
+    coeff, keep, give, late = upward(own[None], after(points, early), basis_t, transfer_t, cut)
     gathered = (keep + swap(give, mates)).astype(BF)
-    step = 2
-    while step < count:
-        gathered = jnp.concatenate([gathered, by_xor(gathered, step)], axis=0)
-        if step == 2:
-            gathered = after(gathered, early_other)
-        gathered = jnp.concatenate([gathered, by_xor(gathered, 3 * step)], axis=0)
-        step *= 4
-    gathered_mate = swap(gathered, mates)
-    coeff_other = swap(after(coeff, gathered), others)
-    coeff_mate = swap(after(coeff, gathered), mates)
-    late = after(late, gathered)
-    above = top(own[None], top_lists.T, gathered, gathered_mate, jnp.transpose(top_transfer, (1, 2, 0)),
-                jnp.transpose(top_coupling, (1, 2, 3, 0)))
-    late_other = swap(late, others)
-    points_mate = swap(after(points, gathered), mates)
-    lhs_coup = [turn(after(coup_t, above), transfer_t, "coupling_turn", 0, rank)]
-    lhs_near = [turn(after(near_t, lhs_coup[0]), basis_t, "near_turn", 0, leaf_size)]
-    above = after(above, lhs_near[0])
     leaf_log = leaf_dev.bit_length() - 1
     near_pos = slots_of(near_lists.T, jnp.full((1, leaf_dev), leaf_log, jnp.int32), own, 0, leaf_dev)
     level = np.array([[(n + 1).bit_length() - 1 for n in range(nodes)]], np.int32)
     coup_pos = slots_of(local_lists.T, jnp.asarray(level), own, jnp.asarray(2 ** level - 1 - FIRST), nodes - FIRST)
-    down = downward(coup_pos, lhs_coup, coeff, coeff_mate, coeff_other, above)
+    step = 2
+    while step < count:
+        came = [by_xor(gathered, way * step) for way in (1, 3, 2)]
+        gathered = jnp.concatenate([gathered] + came, axis=0)
+        if step == 2:
+            gathered = after(gathered, early_other, near_pos, coup_pos)
+        step *= 4
+    gathered_mate = swap(gathered, mates)
+    coeff_other = swap(after(coeff, came[0]), others)
+    above = top(own[None], top_lists.T, gathered, gathered_mate, jnp.transpose(top_transfer, (1, 2, 0)),
+                jnp.transpose(top_coupling, (1, 2, 3, 0)))
+    late_other = swap(after(late, above), others)
+    coeff_mate = swap(after(coeff, above), mates)
+    points_mate = swap(after(points, above), mates)
+    lhs_near = [turn(after(near_t, above), basis_t, "near_turn", 0, leaf_size)]
+    above = after(above, lhs_near[0])
+    down = downward(coup_pos, coup_t, transfer_t, coeff, coeff_mate, coeff_other, above)
     return leaf_rows(near_pos, lhs_near, down, points, points_mate, early_other, late_other)
 
 
-CUT = 56
+CUT = 72
 
 
 def solution(mesh):

time: 106 us -> 94.3 us (0.89)
  waiting for transfers between devices: 29.2 us -> 13.6 us
  starting transfers between devices: 19 us -> 31.2 us
  Pallas kernels: 45.5 us -> 38.6 us
    ppermute x13 -> x16, waiting for transfers between devices: 29.2 us -> 13.6 us  [swap(): return lax.ppermute(value, 'leaf', pairs)]
    ppermute x13 -> x16, starting transfers between devices: 19 us -> 31.2 us  [swap(): return lax.ppermute(value, 'leaf', pairs)]
    pallas_call x2 -> x1, Pallas kernels: 14.1 us -> 7.87 us  [turn(): pl.pallas_call(turn_kernel, grid=(rows // part,), in_specs=[pl.BlockSpec(...]
    pallas_call x1, Pallas kernels: 7.19 us -> 6.1 us  [upward(): pl.pallas_call(upward_kernel, in_specs=[pl.BlockSpec(memory_space=pltpu.S...]
    unnamed x36 -> x43, local copies, waits for them, and re-layouts: 10 us -> 9.37 us
  transfers between devices with their start and end apart: 13 -> 16, of which waited for: 8 -> 9; matrix products, arithmetic and copies ran while one was open for 1% -> 0% of each run, Pallas kernels for 33% -> 32%
where the time goes in v3:
time: 94.3 us; the launch traced here: 93.2 us
  Pallas kernels  38.6 us (41%)
  starting transfers between devices  31.2 us (33%)
  waiting for transfers between devices  13.6 us (14%)
  local copies, waits for them, and re-layouts  9.4 us (10%)
    ppermute x16, starting transfers between devices, swap(): return lax.ppermute(value, 'leaf', pairs)  31.2 us
    ppermute x16, waiting for transfers between devices, swap(): return lax.ppermute(value, 'leaf', pairs)  13.6 us
    pallas_call x1, Pallas kernels, downward(): pl.pallas_call(down_kernel, in_specs=[pl.BlockSpec(memory_space=pltpu.SME...  11.5 us
    unnamed x43, local copies, waits for them, and re-layouts  9.37 us
    pallas_call x1, Pallas kernels, turn(): pl.pallas_call(turn_kernel, grid=(rows // part,), in_specs=[pl.BlockSpec(...  7.87 us
    pallas_call x1, Pallas kernels, leaf_rows(): pl.pallas_call(lambda *refs: rows_kernel(len(lhs), len(pieces), *refs), g...  7.52 us
    pallas_call x1, Pallas kernels, upward(): pl.pallas_call(upward_kernel, in_specs=[pl.BlockSpec(memory_space=pltpu.S...  6.1 us
    pallas_call x1, Pallas kernels, top(): pl.pallas_call(top_kernel, in_specs=[sm, sm, ANY, ANY, hbm, hbm], out_sha...  4.19 us
  transfers between devices with their start and end apart: 16, of which 9 were waited for; matrix products, arithmetic and copies ran while one was open for 0% of the time, Pallas kernels for 32%

profile of v3, /device:TPU:6, one launch (start us, length us, event | category | flops | bytes accessed | tf_op | source)
XLA Modules:
  0.0 93.2 jit_solution(11704669447351066706)
XLA Ops:
  0.0 1.6 %copy-done = bf16[8192,128]{1,0:T(8,128)(2,1)S(1)} copy-done((bf16[8192,128]{1,0:T(8,128)(2,1)S(1)}, bf16[8192,128]{1,0:T(8,128)(2,1)}, u32[]{:S(2)}) %copy-start) | copy-done | bytes 2097176
  1.6 1.4 %head.1 = bf16[4608,128]{1,0:T(8,128)(2,1)} custom-call(bf16[8192,128]{1,0:T(8,128)(2,1)S(1)} %copy-done), custom_call_target="tpu_custom_call" | custom-call | bytes 80000 | tf_op jit(solution)/shard_map/head/pallas_call | solution.py:424
  3.0 8.2 %collective-permute-start.4 = (bf16[4608,128]{1,0:T(8,128)(2,1)}, bf16[4608,128]{1,0:T(8,128)(2,1)}, u32[]{:S(2)}, u32[]{:S(2)}) collective-permute-start(bf16[4608,128]{1,0:T(8,128)(2,1)} %head.1), channel_id=1, source_target_pairs={{1,2},{3,4},{5,6},{7,8},{9,10},{11,12},{13,14},{15,16},{17,18},{19... | collective-permute-start | bytes 3538952 | tf_op jit(solution)/shard_map/ppermute | solution.py:458
  11.3 6.1 %upward.1 = (bf16[8192,128]{1,0:T(8,128)(2,1)S(1)}, f32[16,128]{1,0:T(8,128)S(1)}, f32[16,128]{1,0:T(8,128)S(1)}, bf16[3584,128]{1,0:T(8,128)(2,1)S(1)}) custom-call(s32[1]{0:T(128)} %bitcast.4.me.where_am_i, bf16[8192,128]{1,0:T(8,128)(2,1)} %refs_3_.1, bf16[64,32,128]{2,1,0:T(8,128)(2,1)S(1)} %bitcast.17, bf16[32,32,255]{2,1,0:T(8,128)(2,1)S(1)} %bitcast.15), custom_call_target="tpu_custom_call" | custom-call | bytes 280000 | tf_op jit(solution)/shard_map/upward/pallas_call | solution.py:165
  17.4 1.3 %copy-done.6 = bf16[8192,128]{1,0:T(8,128)(2,1)} copy-done((bf16[8192,128]{1,0:T(8,128)(2,1)}, bf16[8192,128]{1,0:T(8,128)(2,1)S(1)}, u32[]{:S(2)}) %copy-start.6) | copy-done | bytes 2097176
  19.7 1.1 %collective-permute-done = f32[16,128]{1,0:T(8,128)S(1)} collective-permute-done((f32[16,128]{1,0:T(8,128)S(1)}, f32[16,128]{1,0:T(8,128)S(1)}, u32[]{:S(2)}, u32[]{:S(2)}) %collective-permute-start) | collective-permute-done | bytes 8224 | tf_op jit(solution)/shard_map/ppermute | solution.py:458
  21.0 4.0 %collective-permute-start.3 = (bf16[16,128]{1,0:T(8,128)(2,1)S(1)}, bf16[16,128]{1,0:T(8,128)(2,1)S(1)}, u32[]{:S(2)}, u32[]{:S(2)}) collective-permute-start(bf16[16,128]{1,0:T(8,128)(2,1)S(1)} %add_convert_fusion), channel_id=1, source_target_pairs={{0,4},{1,5},{2,6},{3,7},{4,0},{5,1},{6,2},{7,3},{8,12},{9,13},{10,... | collective-permute-start | bytes 12296 | tf_op jit(solution)/shard_map/ppermute | solution.py:458
  26.6 2.5 %collective-permute-start.6 = (bf16[64,128]{1,0:T(8,128)(2,1)S(1)}, bf16[64,128]{1,0:T(8,128)(2,1)S(1)}, u32[]{:S(2)}, u32[]{:S(2)}) collective-permute-start(bf16[64,128]{1,0:T(8,128)(2,1)S(1)} %pad_maximum_fusion), channel_id=1, source_target_pairs={{0,24},{1,25},{2,26},{3,27},{4,28},{5,29},{6,30},{7,31},{8,16},{9,... | collective-permute-start | bytes 49160 | tf_op jit(solution)/shard_map/ppermute | solution.py:458
  29.0 1.6 %collective-permute-start.7 = (bf16[64,128]{1,0:T(8,128)(2,1)S(1)}, bf16[64,128]{1,0:T(8,128)(2,1)S(1)}, u32[]{:S(2)}, u32[]{:S(2)}) collective-permute-start(bf16[64,128]{1,0:T(8,128)(2,1)S(1)} %pad_maximum_fusion), channel_id=1, source_target_pairs={{0,16},{1,17},{2,18},{3,19},{4,20},{5,21},{6,22},{7,23},{8,24},{9,... | collective-permute-start | bytes 49160 | tf_op jit(solution)/shard_map/ppermute | solution.py:458
  30.7 1.1 %collective-permute-done.6 = bf16[64,128]{1,0:T(8,128)(2,1)S(1)} collective-permute-done((bf16[64,128]{1,0:T(8,128)(2,1)S(1)}, bf16[64,128]{1,0:T(8,128)(2,1)S(1)}, u32[]{:S(2)}, u32[]{:S(2)}) %collective-permute-start.6) | collective-permute-done | bytes 16416 | tf_op jit(solution)/shard_map/ppermute | solution.py:458
  31.7 2.5 %collective-permute-done.7 = bf16[64,128]{1,0:T(8,128)(2,1)S(1)} collective-permute-done((bf16[64,128]{1,0:T(8,128)(2,1)S(1)}, bf16[64,128]{1,0:T(8,128)(2,1)S(1)}, u32[]{:S(2)}, u32[]{:S(2)}) %collective-permute-start.7) | collective-permute-done | bytes 16416 | tf_op jit(solution)/shard_map/ppermute | solution.py:458
  35.2 1.1 %collective-permute-start.9 = (bf16[256,128]{1,0:T(8,128)(2,1)S(1)}, bf16[256,128]{1,0:T(8,128)(2,1)S(1)}, u32[]{:S(2)}, u32[]{:S(2)}) collective-permute-start(bf16[256,128]{1,0:T(8,128)(2,1)S(1)} %get-tuple-element.29), channel_id=1, source_target_pairs={{0,96},{1,97},{2,98},{3,99},{4,100},{5,101},{6,102},{7,103},{8,104... | collective-permute-start | bytes 196616 | tf_op jit(solution)/shard_map/ppermute | solution.py:458
  36.3 2.1 %collective-permute-start.10 = (bf16[256,128]{1,0:T(8,128)(2,1)S(1)}, bf16[256,128]{1,0:T(8,128)(2,1)S(1)}, u32[]{:S(2)}, u32[]{:S(2)}) collective-permute-start(bf16[256,128]{1,0:T(8,128)(2,1)S(1)} %get-tuple-element.29), channel_id=1, source_target_pairs={{0,64},{1,65},{2,66},{3,67},{4,68},{5,69},{6,70},{7,71},{8,72},{9,... | collective-permute-start | bytes 196616 | tf_op jit(solution)/shard_map/ppermute | solution.py:458
  38.6 2.0 %collective-permute-done.9 = bf16[256,128]{1,0:T(8,128)(2,1)S(1)} collective-permute-done((bf16[256,128]{1,0:T(8,128)(2,1)S(1)}, bf16[256,128]{1,0:T(8,128)(2,1)S(1)}, u32[]{:S(2)}, u32[]{:S(2)}) %collective-permute-start.9) | collective-permute-done | bytes 65568 | tf_op jit(solution)/shard_map/ppermute | solution.py:458
  40.7 1.4 %collective-permute-done.10 = bf16[256,128]{1,0:T(8,128)(2,1)S(1)} collective-permute-done((bf16[256,128]{1,0:T(8,128)(2,1)S(1)}, bf16[256,128]{1,0:T(8,128)(2,1)S(1)}, u32[]{:S(2)}, u32[]{:S(2)}) %collective-permute-start.10) | collective-permute-done | bytes 65568 | tf_op jit(solution)/shard_map/ppermute | solution.py:458
  42.2 4.5 %collective-permute-start.13 = (bf16[8192,128]{1,0:T(8,128)(2,1)}, bf16[8192,128]{1,0:T(8,128)(2,1)S(1)}, u32[]{:S(2)}, u32[]{:S(2)}) collective-permute-start(bf16[8192,128]{1,0:T(8,128)(2,1)} %copy-done.6), channel_id=1, source_target_pairs={{1,2},{3,4},{5,6},{7,8},{9,10},{11,12},{13,14},{15,16},{17,18},{19... | collective-permute-start | bytes 6291464 | tf_op jit(solution)/shard_map/ppermute | solution.py:458
  46.8 1.6 %copy-done.4 = bf16[128,8,32,32]{0,3,2,1:T(8,128)(2,1)S(1)} copy-done((bf16[128,8,32,32]{0,3,2,1:T(8,128)(2,1)S(1)}, bf16[128,8,32,32]{0,3,2,1:T(8,128)(2,1)}, u32[]{:S(2)}) %copy-start.4) | copy-done | bytes 2097176
  48.4 4.2 %top.1.above = bf16[32,128]{1,0:T(8,128)(2,1)S(1)} custom-call(s32[1]{0:T(128)} %bitcast.4.me.where_am_i, s32[8,128]{1,0:T(8,128)S(1)} %bitcast.20, bf16[1024,128]{1,0:T(8,128)(2,1)S(1)} %constant_dynamic-update-slice_fusion.4.mine_in, bf16[1024,128]{1,0:T(8,128)(2,1)S(1)} %collective-permute-done.11.mate_in, bf16[32,32,128]{2,1,0:T(8,128)(2,1)S(1)} %bitcast.19, ...), custom_call_target="tpu_custom_call" | custom-call | bytes 160000 | tf_op jit(solution)/shard_map/top/pallas_call | solution.py:255
  53.2 5.4 %collective-permute-start.15 = (bf16[3584,128]{1,0:T(8,128)(2,1)S(1)}, bf16[3584,128]{1,0:T(8,128)(2,1)S(1)}, u32[]{:S(2)}, u32[]{:S(2)}) collective-permute-start(bf16[3584,128]{1,0:T(8,128)(2,1)S(1)} %copy-done.13), channel_id=1, source_target_pairs={{1,2},{3,4},{5,6},{7,8},{9,10},{11,12},{13,14},{15,16},{17,18},{19... | collective-permute-start | bytes 2752520 | tf_op jit(solution)/shard_map/ppermute | solution.py:458
  58.6 2.8 %copy-done.2 = bf16[128,6,64,64]{0,3,2,1:T(8,128)(2,1)S(1)} copy-done((bf16[128,6,64,64]{0,3,2,1:T(8,128)(2,1)S(1)}, bf16[128,6,64,64]{0,3,2,1:T(8,128)(2,1)}, u32[]{:S(2)}) %copy-start.2) | copy-done | bytes 6291480
  62.4 7.9 %near_turn.1.refs_2_ = bf16[128,64,416]{2,1,0:T(8,128)(2,1)S(1)} custom-call(bf16[6,64,64,128]{3,2,1,0:T(8,128)(2,1)S(1)} %bitcast.12, bf16[64,32,128]{2,1,0:T(8,128)(2,1)S(1)} %bitcast.18), custom_call_target="tpu_custom_call" | custom-call | bytes 320000 | tf_op jit(solution)/shard_map/near_turn/pallas_call | solution.py:92
  70.3 3.7 %collective-permute-done.13.other = bf16[8192,128]{1,0:T(8,128)(2,1)S(1)} collective-permute-done((bf16[8192,128]{1,0:T(8,128)(2,1)}, bf16[8192,128]{1,0:T(8,128)(2,1)S(1)}, u32[]{:S(2)}, u32[]{:S(2)}) %collective-permute-start.13) | collective-permute-done | bytes 2097184 | tf_op jit(solution)/shard_map/ppermute | solution.py:458
  74.0 11.5 %downward.1.refs_1_ = bf16[4096,128]{1,0:T(8,128)(2,1)S(1)} custom-call(s32[8,255]{1,0:T(8,128)S(1)} %select_bitcast_fusion.pos, bf16[8,32,32,255]{3,2,1,0:T(8,128)(2,1)S(1)} %bitcast.13, bf16[32,32,255]{2,1,0:T(8,128)(2,1)S(1)} %bitcast.16, bf16[8192,128]{1,0:T(8,128)(2,1)S(1)} %copy-done.7, bf16[8192,128]{1,0:T(8,128)(2,1)S(1)} %collective-permute-done.12.mate, ...), custom_call_target="tpu_custom_call" | custom-call | bytes 440000 | tf_op jit(solution)/shard_map/downward/pallas_call | solution.py:338
  85.5 7.5 %leaf_rows.1 = bf16[8192,128]{1,0:T(8,128)(2,1)} custom-call(s32[6,128]{1,0:T(8,128)S(1)} %select_bitcast_fusion.1.refs_0_, bf16[4096,128]{1,0:T(8,128)(2,1)S(1)} %downward.1.refs_1_, bf16[128,64,416]{2,1,0:T(8,128)(2,1)S(1)} %near_turn.1.refs_2_, bf16[8192,128]{1,0:T(8,128)(2,1)S(1)} %copy-done.1, bf16[8192,128]{1,0:T(8,128)(2,1)} %collective-permute-done.14.refs_4_, ...), custom_call_target="tpu_custom_call" | custom-call | bytes 240000 | tf_op jit(solution)/shard_map/leaf_rows/pallas_call | solution.py:389
  (63 shorter events, 5.6 us)
Async XLA Ops:
  3.0 16.7 %copy-start.14 = (s32[255,8]{0,1:T(8,128)S(1)}, s32[255,8]{0,1:T(8,128)}, u32[]{:S(2)}) copy-start(s32[255,8]{0,1:T(8,128)} %param.17) | copy-start | bytes 24484
  3.0 16.7 %copy-start.16 = (s32[255]{0:T(256)S(1)}, s32[255]{0:T(256)}, u32[]{:S(2)}) copy-start(s32[255]{0:T(256)} %constant.40) | copy-start | bytes 3064
  3.0 16.7 %copy-start.17 = (s32[255]{0:T(256)S(1)}, s32[255]{0:T(256)}, u32[]{:S(2)}) copy-start(s32[255]{0:T(256)} %constant.41) | copy-start | bytes 3064
  3.0 16.7 %copy-start.18 = (s32[255]{0:T(256)S(1)}, s32[255]{0:T(256)}, u32[]{:S(2)}) copy-start(s32[255]{0:T(256)} %constant.44) | copy-start | bytes 3064
  3.0 22.0 %copy-start.15 = (s32[128,6]{0,1:T(8,128)S(1)}, s32[128,6]{0,1:T(8,128)}, u32[]{:S(2)}) copy-start(s32[128,6]{0,1:T(8,128)} %param.21) | copy-start | bytes 9220
  3.0 43.7 %copy-start.10 = (bf16[128,32,32]{0,2,1:T(8,128)(2,1)S(1)}, bf16[128,32,32]{0,2,1:T(8,128)(2,1)}, u32[]{:S(2)}) copy-start(bf16[128,32,32]{0,2,1:T(8,128)(2,1)} %param.15) | copy-start | bytes 786436
  3.0 43.7 %copy-start.11 = (s32[128,8]{0,1:T(8,128)S(1)}, s32[128,8]{0,1:T(8,128)}, u32[]{:S(2)}) copy-start(s32[128,8]{0,1:T(8,128)} %param.19) | copy-start | bytes 12292
  3.0 23.5 %collective-permute-start.4 = (bf16[4608,128]{1,0:T(8,128)(2,1)}, bf16[4608,128]{1,0:T(8,128)(2,1)}, u32[]{:S(2)}, u32[]{:S(2)}) collective-permute-start(bf16[4608,128]{1,0:T(8,128)(2,1)} %head.1), channel_id=1, source_target_pairs={{1,2},{3,4},{5,6},{7,8},{9,10},{11,12},{13,14},{15,16},{17,18},{19... | collective-permute-start | bytes 3538952 | tf_op jit(solution)/shard_map/ppermute | solution.py:458
  19.7 33.0 %copy-start.1 = (bf16[8192,128]{1,0:T(8,128)(2,1)S(1)}, bf16[8192,128]{1,0:T(8,128)(2,1)}, u32[]{:S(2)}) copy-start(bf16[8192,128]{1,0:T(8,128)(2,1)} %refs_3_.1) | copy-start | bytes 6291460
  19.7 1.2 %collective-permute-start = (f32[16,128]{1,0:T(8,128)S(1)}, f32[16,128]{1,0:T(8,128)S(1)}, u32[]{:S(2)}, u32[]{:S(2)}) collective-permute-start(f32[16,128]{1,0:T(8,128)S(1)} %get-tuple-element.20), channel_id=1, source_target_pairs={{0,1},{1,0},{2,3},{3,2},{4,5},{5,4},{6,7},{7,6},{8,9},{9,8},{10,11... | collective-permute-start | bytes 24584 | tf_op jit(solution)/shard_map/ppermute | solution.py:458
  20.9 4.1 %collective-permute-start.1 = (bf16[16,128]{1,0:T(8,128)(2,1)S(1)}, bf16[16,128]{1,0:T(8,128)(2,1)S(1)}, u32[]{:S(2)}, u32[]{:S(2)}) collective-permute-start(bf16[16,128]{1,0:T(8,128)(2,1)S(1)} %add_convert_fusion), channel_id=1, source_target_pairs={{0,2},{1,3},{2,0},{3,1},{4,6},{5,7},{6,4},{7,5},{8,10},{9,11},{10,... | collective-permute-start | bytes 12296 | tf_op jit(solution)/shard_map/ppermute | solution.py:458
  20.9 4.9 %collective-permute-start.2 = (bf16[16,128]{1,0:T(8,128)(2,1)S(1)}, bf16[16,128]{1,0:T(8,128)(2,1)S(1)}, u32[]{:S(2)}, u32[]{:S(2)}) collective-permute-start(bf16[16,128]{1,0:T(8,128)(2,1)S(1)} %add_convert_fusion), channel_id=1, source_target_pairs={{0,6},{1,7},{2,4},{3,5},{4,2},{5,3},{6,0},{7,1},{8,14},{9,15},{10,... | collective-permute-start | bytes 12296 | tf_op jit(solution)/shard_map/ppermute | solution.py:458
  21.0 5.6 %collective-permute-start.3 = (bf16[16,128]{1,0:T(8,128)(2,1)S(1)}, bf16[16,128]{1,0:T(8,128)(2,1)S(1)}, u32[]{:S(2)}, u32[]{:S(2)}) collective-permute-start(bf16[16,128]{1,0:T(8,128)(2,1)S(1)} %add_convert_fusion), channel_id=1, source_target_pairs={{0,4},{1,5},{2,6},{3,7},{4,0},{5,1},{6,2},{7,3},{8,12},{9,13},{10,... | collective-permute-start | bytes 12296 | tf_op jit(solution)/shard_map/ppermute | solution.py:458
  26.5 4.1 %collective-permute-start.5 = (bf16[64,128]{1,0:T(8,128)(2,1)S(1)}, bf16[64,128]{1,0:T(8,128)(2,1)S(1)}, u32[]{:S(2)}, u32[]{:S(2)}) collective-permute-start(bf16[64,128]{1,0:T(8,128)(2,1)S(1)} %pad_maximum_fusion), channel_id=1, source_target_pairs={{0,8},{1,9},{2,10},{3,11},{4,12},{5,13},{6,14},{7,15},{8,0},{9,1},... | collective-permute-start | bytes 49160 | tf_op jit(solution)/shard_map/ppermute | solution.py:458
  26.6 5.2 %collective-permute-start.6 = (bf16[64,128]{1,0:T(8,128)(2,1)S(1)}, bf16[64,128]{1,0:T(8,128)(2,1)S(1)}, u32[]{:S(2)}, u32[]{:S(2)}) collective-permute-start(bf16[64,128]{1,0:T(8,128)(2,1)S(1)} %pad_maximum_fusion), channel_id=1, source_target_pairs={{0,24},{1,25},{2,26},{3,27},{4,28},{5,29},{6,30},{7,31},{8,16},{9,... | collective-permute-start | bytes 49160 | tf_op jit(solution)/shard_map/ppermute | solution.py:458
  29.0 5.2 %collective-permute-start.7 = (bf16[64,128]{1,0:T(8,128)(2,1)S(1)}, bf16[64,128]{1,0:T(8,128)(2,1)S(1)}, u32[]{:S(2)}, u32[]{:S(2)}) collective-permute-start(bf16[64,128]{1,0:T(8,128)(2,1)S(1)} %pad_maximum_fusion), channel_id=1, source_target_pairs={{0,16},{1,17},{2,18},{3,19},{4,20},{5,21},{6,22},{7,23},{8,24},{9,... | collective-permute-start | bytes 49160 | tf_op jit(solution)/shard_map/ppermute | solution.py:458
  34.3 4.3 %collective-permute-start.8 = (bf16[256,128]{1,0:T(8,128)(2,1)S(1)}, bf16[256,128]{1,0:T(8,128)(2,1)S(1)}, u32[]{:S(2)}, u32[]{:S(2)}) collective-permute-start(bf16[256,128]{1,0:T(8,128)(2,1)S(1)} %get-tuple-element.29), channel_id=1, source_target_pairs={{0,32},{1,33},{2,34},{3,35},{4,36},{5,37},{6,38},{7,39},{8,40},{9,... | collective-permute-start | bytes 196616 | tf_op jit(solution)/shard_map/ppermute | solution.py:458
  35.2 5.5 %collective-permute-start.9 = (bf16[256,128]{1,0:T(8,128)(2,1)S(1)}, bf16[256,128]{1,0:T(8,128)(2,1)S(1)}, u32[]{:S(2)}, u32[]{:S(2)}) collective-permute-start(bf16[256,128]{1,0:T(8,128)(2,1)S(1)} %get-tuple-element.29), channel_id=1, source_target_pairs={{0,96},{1,97},{2,98},{3,99},{4,100},{5,101},{6,102},{7,103},{8,104... | collective-permute-start | bytes 196616 | tf_op jit(solution)/shard_map/ppermute | solution.py:458
  36.3 5.8 %collective-permute-start.10 = (bf16[256,128]{1,0:T(8,128)(2,1)S(1)}, bf16[256,128]{1,0:T(8,128)(2,1)S(1)}, u32[]{:S(2)}, u32[]{:S(2)}) collective-permute-start(bf16[256,128]{1,0:T(8,128)(2,1)S(1)} %get-tuple-element.29), channel_id=1, source_target_pairs={{0,64},{1,65},{2,66},{3,67},{4,68},{5,69},{6,70},{7,71},{8,72},{9,... | collective-permute-start | bytes 196616 | tf_op jit(solution)/shard_map/ppermute | solution.py:458
  42.1 4.6 %collective-permute-start.11 = (bf16[1024,128]{1,0:T(8,128)(2,1)S(1)}, bf16[1024,128]{1,0:T(8,128)(2,1)S(1)}, u32[]{:S(2)}, u32[]{:S(2)}) collective-permute-start(bf16[1024,128]{1,0:T(8,128)(2,1)S(1)} %constant_dynamic-update-slice_fusion.4.mine_in), channel_id=1, source_target_pairs={{0,1},{1,0},{2,3},{3,2},{4,5},{5,4},{6,7},{7,6},{8,9},{9,8},{10,11... | collective-permute-start | bytes 786440 | tf_op jit(solution)/shard_map/ppermute | solution.py:458
  42.2 31.8 %collective-permute-start.13 = (bf16[8192,128]{1,0:T(8,128)(2,1)}, bf16[8192,128]{1,0:T(8,128)(2,1)S(1)}, u32[]{:S(2)}, u32[]{:S(2)}) collective-permute-start(bf16[8192,128]{1,0:T(8,128)(2,1)} %copy-done.6), channel_id=1, source_target_pairs={{1,2},{3,4},{5,6},{7,8},{9,10},{11,12},{13,14},{15,16},{17,18},{19... | collective-permute-start | bytes 6291464 | tf_op jit(solution)/shard_map/ppermute | solution.py:458
  52.6 21.4 %collective-permute-start.12 = (bf16[8192,128]{1,0:T(8,128)(2,1)}, bf16[8192,128]{1,0:T(8,128)(2,1)S(1)}, u32[]{:S(2)}, u32[]{:S(2)}) collective-permute-start(bf16[8192,128]{1,0:T(8,128)(2,1)} %copy-done.6), channel_id=1, source_target_pairs={{0,1},{1,0},{2,3},{3,2},{4,5},{5,4},{6,7},{7,6},{8,9},{9,8},{10,11... | collective-permute-start | bytes 6291464 | tf_op jit(solution)/shard_map/ppermute | solution.py:458
  52.7 32.9 %collective-permute-start.14 = (bf16[8192,128]{1,0:T(8,128)(2,1)S(1)}, bf16[8192,128]{1,0:T(8,128)(2,1)}, u32[]{:S(2)}, u32[]{:S(2)}) collective-permute-start(bf16[8192,128]{1,0:T(8,128)(2,1)S(1)} %copy-done.1), channel_id=1, source_target_pairs={{0,1},{1,0},{2,3},{3,2},{4,5},{5,4},{6,7},{7,6},{8,9},{9,8},{10,11... | collective-permute-start | bytes 6291464 | tf_op jit(solution)/shard_map/ppermute | solution.py:458
  53.2 32.4 %collective-permute-start.15 = (bf16[3584,128]{1,0:T(8,128)(2,1)S(1)}, bf16[3584,128]{1,0:T(8,128)(2,1)S(1)}, u32[]{:S(2)}, u32[]{:S(2)}) collective-permute-start(bf16[3584,128]{1,0:T(8,128)(2,1)S(1)} %copy-done.13), channel_id=1, source_target_pairs={{1,2},{3,4},{5,6},{7,8},{9,10},{11,12},{13,14},{15,16},{17,18},{19... | collective-permute-start | bytes 2752520 | tf_op jit(solution)/shard_map/ppermute | solution.py:458
  (11 other events, 56.7 us)

commit v4 on v3

--- a/solution.py
+++ b/solution.py
@@ -321,7 +321,7 @@
             else:
                 down[rows_at(count - 1 + p, rank), :] = got
 
-        batch(count, 32, load, work, store)
+        batch(count, 64, load, work, store)
         count *= 2
 
 
@@ -337,7 +337,7 @@
     hbm = pl.BlockSpec(memory_space=pltpu.HBM)
     return pl.pallas_call(
         down_kernel,
-        in_specs=[pl.BlockSpec(memory_space=pltpu.SMEM)] + [hbm] * 5 + [pl.BlockSpec(memory_space=pltpu.VMEM)],
+        in_specs=[pl.BlockSpec(memory_space=pltpu.SMEM)] + [hbm] * 2 + [ANY] * 3 + [pl.BlockSpec(memory_space=pltpu.VMEM)],
         out_shape=jax.ShapeDtypeStruct((leaves * rank, vecs), BF),
         scratch_shapes=[pltpu.VMEM(blocks_t.shape, BF), pltpu.VMEM(transfer_t.shape, BF),
                         pltpu.VMEM((3 * rows + rank, vecs), BF),
@@ -385,7 +385,7 @@
     rows, vecs = pieces[0].shape
     rank = down.shape[0] // leaves
     part = 32
-    any_ = pl.BlockSpec(memory_space=pltpu.HBM)
+    any_ = pl.BlockSpec(memory_space=pl.ANY)
     return pl.pallas_call(
         lambda *refs: rows_kernel(len(lhs), len(pieces), *refs),
         grid_spec=pltpu.PrefetchScalarGridSpec(

time: 94.3 us -> 93.7 us (level)
  transfers between devices with their start and end apart: 16 -> 16, of which waited for: 9 -> 9; matrix products, arithmetic and copies ran while one was open for 0% -> 0% of each run, Pallas kernels for 32% -> 31%
where the time goes in v4:
time: 93.7 us; the launch traced here: 92.7 us
  Pallas kernels  38 us (41%)
  starting transfers between devices  31.2 us (33%)
  waiting for transfers between devices  13.6 us (15%)
  local copies, waits for them, and re-layouts  9.4 us (10%)
    ppermute x16, starting transfers between devices, swap(): return lax.ppermute(value, 'leaf', pairs)  31.2 us
    ppermute x16, waiting for transfers between devices, swap(): return lax.ppermute(value, 'leaf', pairs)  13.6 us
    pallas_call x1, Pallas kernels, downward(): pl.pallas_call(down_kernel, in_specs=[pl.BlockSpec(memory_space=pltpu.SME...  11 us
    unnamed x43, local copies, waits for them, and re-layouts  9.37 us
    pallas_call x1, Pallas kernels, turn(): pl.pallas_call(turn_kernel, grid=(rows // part,), in_specs=[pl.BlockSpec(...  7.87 us
    pallas_call x1, Pallas kernels, leaf_rows(): pl.pallas_call(lambda *refs: rows_kernel(len(lhs), len(pieces), *refs), g...  7.52 us
    pallas_call x1, Pallas kernels, upward(): pl.pallas_call(upward_kernel, in_specs=[pl.BlockSpec(memory_space=pltpu.S...  6.1 us
    pallas_call x1, Pallas kernels, top(): pl.pallas_call(top_kernel, in_specs=[sm, sm, ANY, ANY, hbm, hbm], out_sha...  4.19 us
  transfers between devices with their start and end apart: 16, of which 9 were waited for; matrix products, arithmetic and copies ran while one was open for 0% of the time, Pallas kernels for 31%

profile of v4, /device:TPU:6, one launch (start us, length us, event | category | flops | bytes accessed | tf_op | source)
XLA Modules:
  0.0 92.7 jit_solution(16685595437545960896)
XLA Ops:
  0.0 1.6 %copy-done = bf16[8192,128]{1,0:T(8,128)(2,1)S(1)} copy-done((bf16[8192,128]{1,0:T(8,128)(2,1)S(1)}, bf16[8192,128]{1,0:T(8,128)(2,1)}, u32[]{:S(2)}) %copy-start) | copy-done | bytes 2097176
  1.6 1.4 %head.1 = bf16[4608,128]{1,0:T(8,128)(2,1)} custom-call(bf16[8192,128]{1,0:T(8,128)(2,1)S(1)} %copy-done), custom_call_target="tpu_custom_call" | custom-call | bytes 80000 | tf_op jit(solution)/shard_map/head/pallas_call | solution.py:424
  3.0 8.2 %collective-permute-start.4 = (bf16[4608,128]{1,0:T(8,128)(2,1)}, bf16[4608,128]{1,0:T(8,128)(2,1)}, u32[]{:S(2)}, u32[]{:S(2)}) collective-permute-start(bf16[4608,128]{1,0:T(8,128)(2,1)} %head.1), channel_id=1, source_target_pairs={{1,2},{3,4},{5,6},{7,8},{9,10},{11,12},{13,14},{15,16},{17,18},{19... | collective-permute-start | bytes 3538952 | tf_op jit(solution)/shard_map/ppermute | solution.py:458
  11.3 6.1 %upward.1 = (bf16[8192,128]{1,0:T(8,128)(2,1)S(1)}, f32[16,128]{1,0:T(8,128)S(1)}, f32[16,128]{1,0:T(8,128)S(1)}, bf16[3584,128]{1,0:T(8,128)(2,1)S(1)}) custom-call(s32[1]{0:T(128)} %bitcast.4.me.where_am_i, bf16[8192,128]{1,0:T(8,128)(2,1)} %refs_3_.1, bf16[64,32,128]{2,1,0:T(8,128)(2,1)S(1)} %bitcast.17, bf16[32,32,255]{2,1,0:T(8,128)(2,1)S(1)} %bitcast.15), custom_call_target="tpu_custom_call" | custom-call | bytes 280000 | tf_op jit(solution)/shard_map/upward/pallas_call | solution.py:165
  17.4 1.3 %copy-done.6 = bf16[8192,128]{1,0:T(8,128)(2,1)} copy-done((bf16[8192,128]{1,0:T(8,128)(2,1)}, bf16[8192,128]{1,0:T(8,128)(2,1)S(1)}, u32[]{:S(2)}) %copy-start.6) | copy-done | bytes 2097176
  19.7 1.1 %collective-permute-done = f32[16,128]{1,0:T(8,128)S(1)} collective-permute-done((f32[16,128]{1,0:T(8,128)S(1)}, f32[16,128]{1,0:T(8,128)S(1)}, u32[]{:S(2)}, u32[]{:S(2)}) %collective-permute-start) | collective-permute-done | bytes 8224 | tf_op jit(solution)/shard_map/ppermute | solution.py:458
  21.0 4.0 %collective-permute-start.3 = (bf16[16,128]{1,0:T(8,128)(2,1)S(1)}, bf16[16,128]{1,0:T(8,128)(2,1)S(1)}, u32[]{:S(2)}, u32[]{:S(2)}) collective-permute-start(bf16[16,128]{1,0:T(8,128)(2,1)S(1)} %add_convert_fusion), channel_id=1, source_target_pairs={{0,4},{1,5},{2,6},{3,7},{4,0},{5,1},{6,2},{7,3},{8,12},{9,13},{10,... | collective-permute-start | bytes 12296 | tf_op jit(solution)/shard_map/ppermute | solution.py:458
  26.6 2.5 %collective-permute-start.6 = (bf16[64,128]{1,0:T(8,128)(2,1)S(1)}, bf16[64,128]{1,0:T(8,128)(2,1)S(1)}, u32[]{:S(2)}, u32[]{:S(2)}) collective-permute-start(bf16[64,128]{1,0:T(8,128)(2,1)S(1)} %pad_maximum_fusion), channel_id=1, source_target_pairs={{0,24},{1,25},{2,26},{3,27},{4,28},{5,29},{6,30},{7,31},{8,16},{9,... | collective-permute-start | bytes 49160 | tf_op jit(solution)/shard_map/ppermute | solution.py:458
  29.0 1.6 %collective-permute-start.7 = (bf16[64,128]{1,0:T(8,128)(2,1)S(1)}, bf16[64,128]{1,0:T(8,128)(2,1)S(1)}, u32[]{:S(2)}, u32[]{:S(2)}) collective-permute-start(bf16[64,128]{1,0:T(8,128)(2,1)S(1)} %pad_maximum_fusion), channel_id=1, source_target_pairs={{0,16},{1,17},{2,18},{3,19},{4,20},{5,21},{6,22},{7,23},{8,24},{9,... | collective-permute-start | bytes 49160 | tf_op jit(solution)/shard_map/ppermute | solution.py:458
  30.7 1.1 %collective-permute-done.6 = bf16[64,128]{1,0:T(8,128)(2,1)S(1)} collective-permute-done((bf16[64,128]{1,0:T(8,128)(2,1)S(1)}, bf16[64,128]{1,0:T(8,128)(2,1)S(1)}, u32[]{:S(2)}, u32[]{:S(2)}) %collective-permute-start.6) | collective-permute-done | bytes 16416 | tf_op jit(solution)/shard_map/ppermute | solution.py:458
  31.7 2.5 %collective-permute-done.7 = bf16[64,128]{1,0:T(8,128)(2,1)S(1)} collective-permute-done((bf16[64,128]{1,0:T(8,128)(2,1)S(1)}, bf16[64,128]{1,0:T(8,128)(2,1)S(1)}, u32[]{:S(2)}, u32[]{:S(2)}) %collective-permute-start.7) | collective-permute-done | bytes 16416 | tf_op jit(solution)/shard_map/ppermute | solution.py:458
  35.2 1.1 %collective-permute-start.9 = (bf16[256,128]{1,0:T(8,128)(2,1)S(1)}, bf16[256,128]{1,0:T(8,128)(2,1)S(1)}, u32[]{:S(2)}, u32[]{:S(2)}) collective-permute-start(bf16[256,128]{1,0:T(8,128)(2,1)S(1)} %get-tuple-element.29), channel_id=1, source_target_pairs={{0,96},{1,97},{2,98},{3,99},{4,100},{5,101},{6,102},{7,103},{8,104... | collective-permute-start | bytes 196616 | tf_op jit(solution)/shard_map/ppermute | solution.py:458
  36.3 2.1 %collective-permute-start.10 = (bf16[256,128]{1,0:T(8,128)(2,1)S(1)}, bf16[256,128]{1,0:T(8,128)(2,1)S(1)}, u32[]{:S(2)}, u32[]{:S(2)}) collective-permute-start(bf16[256,128]{1,0:T(8,128)(2,1)S(1)} %get-tuple-element.29), channel_id=1, source_target_pairs={{0,64},{1,65},{2,66},{3,67},{4,68},{5,69},{6,70},{7,71},{8,72},{9,... | collective-permute-start | bytes 196616 | tf_op jit(solution)/shard_map/ppermute | solution.py:458
  38.6 2.0 %collective-permute-done.9 = bf16[256,128]{1,0:T(8,128)(2,1)S(1)} collective-permute-done((bf16[256,128]{1,0:T(8,128)(2,1)S(1)}, bf16[256,128]{1,0:T(8,128)(2,1)S(1)}, u32[]{:S(2)}, u32[]{:S(2)}) %collective-permute-start.9) | collective-permute-done | bytes 65568 | tf_op jit(solution)/shard_map/ppermute | solution.py:458
  40.7 1.4 %collective-permute-done.10 = bf16[256,128]{1,0:T(8,128)(2,1)S(1)} collective-permute-done((bf16[256,128]{1,0:T(8,128)(2,1)S(1)}, bf16[256,128]{1,0:T(8,128)(2,1)S(1)}, u32[]{:S(2)}, u32[]{:S(2)}) %collective-permute-start.10) | collective-permute-done | bytes 65568 | tf_op jit(solution)/shard_map/ppermute | solution.py:458
  42.2 4.5 %collective-permute-start.13 = (bf16[8192,128]{1,0:T(8,128)(2,1)}, bf16[8192,128]{1,0:T(8,128)(2,1)S(1)}, u32[]{:S(2)}, u32[]{:S(2)}) collective-permute-start(bf16[8192,128]{1,0:T(8,128)(2,1)} %copy-done.6), channel_id=1, source_target_pairs={{1,2},{3,4},{5,6},{7,8},{9,10},{11,12},{13,14},{15,16},{17,18},{19... | collective-permute-start | bytes 6291464 | tf_op jit(solution)/shard_map/ppermute | solution.py:458
  46.8 1.6 %copy-done.4 = bf16[128,8,32,32]{0,3,2,1:T(8,128)(2,1)S(1)} copy-done((bf16[128,8,32,32]{0,3,2,1:T(8,128)(2,1)S(1)}, bf16[128,8,32,32]{0,3,2,1:T(8,128)(2,1)}, u32[]{:S(2)}) %copy-start.4) | copy-done | bytes 2097176
  48.4 4.2 %top.1.above = bf16[32,128]{1,0:T(8,128)(2,1)S(1)} custom-call(s32[1]{0:T(128)} %bitcast.4.me.where_am_i, s32[8,128]{1,0:T(8,128)S(1)} %bitcast.20, bf16[1024,128]{1,0:T(8,128)(2,1)S(1)} %constant_dynamic-update-slice_fusion.4.mine_in, bf16[1024,128]{1,0:T(8,128)(2,1)S(1)} %collective-permute-done.11.mate_in, bf16[32,32,128]{2,1,0:T(8,128)(2,1)S(1)} %bitcast.19, ...), custom_call_target="tpu_custom_call" | custom-call | bytes 160000 | tf_op jit(solution)/shard_map/top/pallas_call | solution.py:255
  53.2 5.4 %collective-permute-start.15 = (bf16[3584,128]{1,0:T(8,128)(2,1)S(1)}, bf16[3584,128]{1,0:T(8,128)(2,1)S(1)}, u32[]{:S(2)}, u32[]{:S(2)}) collective-permute-start(bf16[3584,128]{1,0:T(8,128)(2,1)S(1)} %copy-done.13), channel_id=1, source_target_pairs={{1,2},{3,4},{5,6},{7,8},{9,10},{11,12},{13,14},{15,16},{17,18},{19... | collective-permute-start | bytes 2752520 | tf_op jit(solution)/shard_map/ppermute | solution.py:458
  58.6 2.8 %copy-done.2 = bf16[128,6,64,64]{0,3,2,1:T(8,128)(2,1)S(1)} copy-done((bf16[128,6,64,64]{0,3,2,1:T(8,128)(2,1)S(1)}, bf16[128,6,64,64]{0,3,2,1:T(8,128)(2,1)}, u32[]{:S(2)}) %copy-start.2) | copy-done | bytes 6291480
  62.4 7.9 %near_turn.1.refs_2_ = bf16[128,64,416]{2,1,0:T(8,128)(2,1)S(1)} custom-call(bf16[6,64,64,128]{3,2,1,0:T(8,128)(2,1)S(1)} %bitcast.12, bf16[64,32,128]{2,1,0:T(8,128)(2,1)S(1)} %bitcast.18), custom_call_target="tpu_custom_call" | custom-call | bytes 320000 | tf_op jit(solution)/shard_map/near_turn/pallas_call | solution.py:92
  70.3 3.7 %collective-permute-done.13.other = bf16[8192,128]{1,0:T(8,128)(2,1)S(1)} collective-permute-done((bf16[8192,128]{1,0:T(8,128)(2,1)}, bf16[8192,128]{1,0:T(8,128)(2,1)S(1)}, u32[]{:S(2)}, u32[]{:S(2)}) %collective-permute-start.13) | collective-permute-done | bytes 2097184 | tf_op jit(solution)/shard_map/ppermute | solution.py:458
  74.0 11.0 %downward.1.refs_1_ = bf16[4096,128]{1,0:T(8,128)(2,1)S(1)} custom-call(s32[8,255]{1,0:T(8,128)S(1)} %select_bitcast_fusion.pos, bf16[8,32,32,255]{3,2,1,0:T(8,128)(2,1)S(1)} %bitcast.13, bf16[32,32,255]{2,1,0:T(8,128)(2,1)S(1)} %bitcast.16, bf16[8192,128]{1,0:T(8,128)(2,1)S(1)} %copy-done.7, bf16[8192,128]{1,0:T(8,128)(2,1)S(1)} %collective-permute-done.12.mate, ...), custom_call_target="tpu_custom_call" | custom-call | bytes 440000 | tf_op jit(solution)/shard_map/downward/pallas_call | solution.py:338
  85.0 7.5 %leaf_rows.1 = bf16[8192,128]{1,0:T(8,128)(2,1)} custom-call(s32[6,128]{1,0:T(8,128)S(1)} %select_bitcast_fusion.1.refs_0_, bf16[4096,128]{1,0:T(8,128)(2,1)S(1)} %downward.1.refs_1_, bf16[128,64,416]{2,1,0:T(8,128)(2,1)S(1)} %near_turn.1.refs_2_, bf16[8192,128]{1,0:T(8,128)(2,1)S(1)} %copy-done.1, bf16[8192,128]{1,0:T(8,128)(2,1)} %collective-permute-done.14.refs_4_, ...), custom_call_target="tpu_custom_call" | custom-call | bytes 240000 | tf_op jit(solution)/shard_map/leaf_rows/pallas_call | solution.py:389
  (63 shorter events, 5.6 us)
Async XLA Ops:
  3.0 16.7 %copy-start.14 = (s32[255,8]{0,1:T(8,128)S(1)}, s32[255,8]{0,1:T(8,128)}, u32[]{:S(2)}) copy-start(s32[255,8]{0,1:T(8,128)} %param.17) | copy-start | bytes 24484
  3.0 16.7 %copy-start.16 = (s32[255]{0:T(256)S(1)}, s32[255]{0:T(256)}, u32[]{:S(2)}) copy-start(s32[255]{0:T(256)} %constant.40) | copy-start | bytes 3064
  3.0 16.7 %copy-start.17 = (s32[255]{0:T(256)S(1)}, s32[255]{0:T(256)}, u32[]{:S(2)}) copy-start(s32[255]{0:T(256)} %constant.41) | copy-start | bytes 3064
  3.0 16.7 %copy-start.18 = (s32[255]{0:T(256)S(1)}, s32[255]{0:T(256)}, u32[]{:S(2)}) copy-start(s32[255]{0:T(256)} %constant.44) | copy-start | bytes 3064
  3.0 22.0 %copy-start.15 = (s32[128,6]{0,1:T(8,128)S(1)}, s32[128,6]{0,1:T(8,128)}, u32[]{:S(2)}) copy-start(s32[128,6]{0,1:T(8,128)} %param.21) | copy-start | bytes 9220
  3.0 43.7 %copy-start.10 = (bf16[128,32,32]{0,2,1:T(8,128)(2,1)S(1)}, bf16[128,32,32]{0,2,1:T(8,128)(2,1)}, u32[]{:S(2)}) copy-start(bf16[128,32,32]{0,2,1:T(8,128)(2,1)} %param.15) | copy-start | bytes 786436
  3.0 43.7 %copy-start.11 = (s32[128,8]{0,1:T(8,128)S(1)}, s32[128,8]{0,1:T(8,128)}, u32[]{:S(2)}) copy-start(s32[128,8]{0,1:T(8,128)} %param.19) | copy-start | bytes 12292
  3.0 23.5 %collective-permute-start.4 = (bf16[4608,128]{1,0:T(8,128)(2,1)}, bf16[4608,128]{1,0:T(8,128)(2,1)}, u32[]{:S(2)}, u32[]{:S(2)}) collective-permute-start(bf16[4608,128]{1,0:T(8,128)(2,1)} %head.1), channel_id=1, source_target_pairs={{1,2},{3,4},{5,6},{7,8},{9,10},{11,12},{13,14},{15,16},{17,18},{19... | collective-permute-start | bytes 3538952 | tf_op jit(solution)/shard_map/ppermute | solution.py:458
  19.7 33.0 %copy-start.1 = (bf16[8192,128]{1,0:T(8,128)(2,1)S(1)}, bf16[8192,128]{1,0:T(8,128)(2,1)}, u32[]{:S(2)}) copy-start(bf16[8192,128]{1,0:T(8,128)(2,1)} %refs_3_.1) | copy-start | bytes 6291460
  19.7 1.2 %collective-permute-start = (f32[16,128]{1,0:T(8,128)S(1)}, f32[16,128]{1,0:T(8,128)S(1)}, u32[]{:S(2)}, u32[]{:S(2)}) collective-permute-start(f32[16,128]{1,0:T(8,128)S(1)} %get-tuple-element.20), channel_id=1, source_target_pairs={{0,1},{1,0},{2,3},{3,2},{4,5},{5,4},{6,7},{7,6},{8,9},{9,8},{10,11... | collective-permute-start | bytes 24584 | tf_op jit(solution)/shard_map/ppermute | solution.py:458
  20.9 4.1 %collective-permute-start.1 = (bf16[16,128]{1,0:T(8,128)(2,1)S(1)}, bf16[16,128]{1,0:T(8,128)(2,1)S(1)}, u32[]{:S(2)}, u32[]{:S(2)}) collective-permute-start(bf16[16,128]{1,0:T(8,128)(2,1)S(1)} %add_convert_fusion), channel_id=1, source_target_pairs={{0,2},{1,3},{2,0},{3,1},{4,6},{5,7},{6,4},{7,5},{8,10},{9,11},{10,... | collective-permute-start | bytes 12296 | tf_op jit(solution)/shard_map/ppermute | solution.py:458
  20.9 4.9 %collective-permute-start.2 = (bf16[16,128]{1,0:T(8,128)(2,1)S(1)}, bf16[16,128]{1,0:T(8,128)(2,1)S(1)}, u32[]{:S(2)}, u32[]{:S(2)}) collective-permute-start(bf16[16,128]{1,0:T(8,128)(2,1)S(1)} %add_convert_fusion), channel_id=1, source_target_pairs={{0,6},{1,7},{2,4},{3,5},{4,2},{5,3},{6,0},{7,1},{8,14},{9,15},{10,... | collective-permute-start | bytes 12296 | tf_op jit(solution)/shard_map/ppermute | solution.py:458
  21.0 5.6 %collective-permute-start.3 = (bf16[16,128]{1,0:T(8,128)(2,1)S(1)}, bf16[16,128]{1,0:T(8,128)(2,1)S(1)}, u32[]{:S(2)}, u32[]{:S(2)}) collective-permute-start(bf16[16,128]{1,0:T(8,128)(2,1)S(1)} %add_convert_fusion), channel_id=1, source_target_pairs={{0,4},{1,5},{2,6},{3,7},{4,0},{5,1},{6,2},{7,3},{8,12},{9,13},{10,... | collective-permute-start | bytes 12296 | tf_op jit(solution)/shard_map/ppermute | solution.py:458
  26.5 4.1 %collective-permute-start.5 = (bf16[64,128]{1,0:T(8,128)(2,1)S(1)}, bf16[64,128]{1,0:T(8,128)(2,1)S(1)}, u32[]{:S(2)}, u32[]{:S(2)}) collective-permute-start(bf16[64,128]{1,0:T(8,128)(2,1)S(1)} %pad_maximum_fusion), channel_id=1, source_target_pairs={{0,8},{1,9},{2,10},{3,11},{4,12},{5,13},{6,14},{7,15},{8,0},{9,1},... | collective-permute-start | bytes 49160 | tf_op jit(solution)/shard_map/ppermute | solution.py:458
  26.6 5.2 %collective-permute-start.6 = (bf16[64,128]{1,0:T(8,128)(2,1)S(1)}, bf16[64,128]{1,0:T(8,128)(2,1)S(1)}, u32[]{:S(2)}, u32[]{:S(2)}) collective-permute-start(bf16[64,128]{1,0:T(8,128)(2,1)S(1)} %pad_maximum_fusion), channel_id=1, source_target_pairs={{0,24},{1,25},{2,26},{3,27},{4,28},{5,29},{6,30},{7,31},{8,16},{9,... | collective-permute-start | bytes 49160 | tf_op jit(solution)/shard_map/ppermute | solution.py:458
  29.0 5.2 %collective-permute-start.7 = (bf16[64,128]{1,0:T(8,128)(2,1)S(1)}, bf16[64,128]{1,0:T(8,128)(2,1)S(1)}, u32[]{:S(2)}, u32[]{:S(2)}) collective-permute-start(bf16[64,128]{1,0:T(8,128)(2,1)S(1)} %pad_maximum_fusion), channel_id=1, source_target_pairs={{0,16},{1,17},{2,18},{3,19},{4,20},{5,21},{6,22},{7,23},{8,24},{9,... | collective-permute-start | bytes 49160 | tf_op jit(solution)/shard_map/ppermute | solution.py:458
  34.3 4.3 %collective-permute-start.8 = (bf16[256,128]{1,0:T(8,128)(2,1)S(1)}, bf16[256,128]{1,0:T(8,128)(2,1)S(1)}, u32[]{:S(2)}, u32[]{:S(2)}) collective-permute-start(bf16[256,128]{1,0:T(8,128)(2,1)S(1)} %get-tuple-element.29), channel_id=1, source_target_pairs={{0,32},{1,33},{2,34},{3,35},{4,36},{5,37},{6,38},{7,39},{8,40},{9,... | collective-permute-start | bytes 196616 | tf_op jit(solution)/shard_map/ppermute | solution.py:458
  35.2 5.5 %collective-permute-start.9 = (bf16[256,128]{1,0:T(8,128)(2,1)S(1)}, bf16[256,128]{1,0:T(8,128)(2,1)S(1)}, u32[]{:S(2)}, u32[]{:S(2)}) collective-permute-start(bf16[256,128]{1,0:T(8,128)(2,1)S(1)} %get-tuple-element.29), channel_id=1, source_target_pairs={{0,96},{1,97},{2,98},{3,99},{4,100},{5,101},{6,102},{7,103},{8,104... | collective-permute-start | bytes 196616 | tf_op jit(solution)/shard_map/ppermute | solution.py:458
  36.3 5.8 %collective-permute-start.10 = (bf16[256,128]{1,0:T(8,128)(2,1)S(1)}, bf16[256,128]{1,0:T(8,128)(2,1)S(1)}, u32[]{:S(2)}, u32[]{:S(2)}) collective-permute-start(bf16[256,128]{1,0:T(8,128)(2,1)S(1)} %get-tuple-element.29), channel_id=1, source_target_pairs={{0,64},{1,65},{2,66},{3,67},{4,68},{5,69},{6,70},{7,71},{8,72},{9,... | collective-permute-start | bytes 196616 | tf_op jit(solution)/shard_map/ppermute | solution.py:458
  42.1 4.6 %collective-permute-start.11 = (bf16[1024,128]{1,0:T(8,128)(2,1)S(1)}, bf16[1024,128]{1,0:T(8,128)(2,1)S(1)}, u32[]{:S(2)}, u32[]{:S(2)}) collective-permute-start(bf16[1024,128]{1,0:T(8,128)(2,1)S(1)} %constant_dynamic-update-slice_fusion.4.mine_in), channel_id=1, source_target_pairs={{0,1},{1,0},{2,3},{3,2},{4,5},{5,4},{6,7},{7,6},{8,9},{9,8},{10,11... | collective-permute-start | bytes 786440 | tf_op jit(solution)/shard_map/ppermute | solution.py:458
  42.2 31.8 %collective-permute-start.13 = (bf16[8192,128]{1,0:T(8,128)(2,1)}, bf16[8192,128]{1,0:T(8,128)(2,1)S(1)}, u32[]{:S(2)}, u32[]{:S(2)}) collective-permute-start(bf16[8192,128]{1,0:T(8,128)(2,1)} %copy-done.6), channel_id=1, source_target_pairs={{1,2},{3,4},{5,6},{7,8},{9,10},{11,12},{13,14},{15,16},{17,18},{19... | collective-permute-start | bytes 6291464 | tf_op jit(solution)/shard_map/ppermute | solution.py:458
  52.6 21.4 %collective-permute-start.12 = (bf16[8192,128]{1,0:T(8,128)(2,1)}, bf16[8192,128]{1,0:T(8,128)(2,1)S(1)}, u32[]{:S(2)}, u32[]{:S(2)}) collective-permute-start(bf16[8192,128]{1,0:T(8,128)(2,1)} %copy-done.6), channel_id=1, source_target_pairs={{0,1},{1,0},{2,3},{3,2},{4,5},{5,4},{6,7},{7,6},{8,9},{9,8},{10,11... | collective-permute-start | bytes 6291464 | tf_op jit(solution)/shard_map/ppermute | solution.py:458
  52.7 32.3 %collective-permute-start.14 = (bf16[8192,128]{1,0:T(8,128)(2,1)S(1)}, bf16[8192,128]{1,0:T(8,128)(2,1)}, u32[]{:S(2)}, u32[]{:S(2)}) collective-permute-start(bf16[8192,128]{1,0:T(8,128)(2,1)S(1)} %copy-done.1), channel_id=1, source_target_pairs={{0,1},{1,0},{2,3},{3,2},{4,5},{5,4},{6,7},{7,6},{8,9},{9,8},{10,11... | collective-permute-start | bytes 6291464 | tf_op jit(solution)/shard_map/ppermute | solution.py:458
  53.2 31.8 %collective-permute-start.15 = (bf16[3584,128]{1,0:T(8,128)(2,1)S(1)}, bf16[3584,128]{1,0:T(8,128)(2,1)S(1)}, u32[]{:S(2)}, u32[]{:S(2)}) collective-permute-start(bf16[3584,128]{1,0:T(8,128)(2,1)S(1)} %copy-done.13), channel_id=1, source_target_pairs={{1,2},{3,4},{5,6},{7,8},{9,10},{11,12},{13,14},{15,16},{17,18},{19... | collective-permute-start | bytes 2752520 | tf_op jit(solution)/shard_map/ppermute | solution.py:458
  (11 other events, 56.7 us)

commit v5 on v4

--- a/solution.py
+++ b/solution.py
@@ -384,7 +384,7 @@
     size = sum(a.shape[1] for a in lhs)
     rows, vecs = pieces[0].shape
     rank = down.shape[0] // leaves
-    part = 32
+    part = 64
     any_ = pl.BlockSpec(memory_space=pl.ANY)
     return pl.pallas_call(
         lambda *refs: rows_kernel(len(lhs), len(pieces), *refs),

time: 93.7 us -> 93.9 us (level)
  no operation moved by 1% of the time
where the time goes in v5:
time: 93.9 us; the launch traced here: 92.8 us
  Pallas kernels  38.2 us (41%)
  starting transfers between devices  31.2 us (33%)
  waiting for transfers between devices  13.6 us (14%)
  local copies, waits for them, and re-layouts  9.4 us (10%)
    ppermute x16, starting transfers between devices, swap(): return lax.ppermute(value, 'leaf', pairs)  31.2 us
    ppermute x16, waiting for transfers between devices, swap(): return lax.ppermute(value, 'leaf', pairs)  13.6 us
    pallas_call x1, Pallas kernels, downward(): pl.pallas_call(down_kernel, in_specs=[pl.BlockSpec(memory_space=pltpu.SME...  11 us
    unnamed x43, local copies, waits for them, and re-layouts  9.37 us
    pallas_call x1, Pallas kernels, turn(): pl.pallas_call(turn_kernel, grid=(rows // part,), in_specs=[pl.BlockSpec(...  7.87 us
    pallas_call x1, Pallas kernels, leaf_rows(): pl.pallas_call(lambda *refs: rows_kernel(len(lhs), len(pieces), *refs), g...  7.65 us
    pallas_call x1, Pallas kernels, upward(): pl.pallas_call(upward_kernel, in_specs=[pl.BlockSpec(memory_space=pltpu.S...  6.1 us
    pallas_call x1, Pallas kernels, top(): pl.pallas_call(top_kernel, in_specs=[sm, sm, ANY, ANY, hbm, hbm], out_sha...  4.19 us
  transfers between devices with their start and end apart: 16, of which 9 were waited for; matrix products, arithmetic and copies ran while one was open for 0% of the time, Pallas kernels for 31%

profile of v5, /device:TPU:6, one launch (start us, length us, event | category | flops | bytes accessed | tf_op | source)
XLA Modules:
  0.0 92.8 jit_solution(13910109875559974423)
XLA Ops:
  0.0 1.6 %copy-done = bf16[8192,128]{1,0:T(8,128)(2,1)S(1)} copy-done((bf16[8192,128]{1,0:T(8,128)(2,1)S(1)}, bf16[8192,128]{1,0:T(8,128)(2,1)}, u32[]{:S(2)}) %copy-start) | copy-done | bytes 2097176
  1.6 1.4 %head.1 = bf16[4608,128]{1,0:T(8,128)(2,1)} custom-call(bf16[8192,128]{1,0:T(8,128)(2,1)S(1)} %copy-done), custom_call_target="tpu_custom_call" | custom-call | bytes 80000 | tf_op jit(solution)/shard_map/head/pallas_call | solution.py:424
  3.0 8.2 %collective-permute-start.4 = (bf16[4608,128]{1,0:T(8,128)(2,1)}, bf16[4608,128]{1,0:T(8,128)(2,1)}, u32[]{:S(2)}, u32[]{:S(2)}) collective-permute-start(bf16[4608,128]{1,0:T(8,128)(2,1)} %head.1), channel_id=1, source_target_pairs={{1,2},{3,4},{5,6},{7,8},{9,10},{11,12},{13,14},{15,16},{17,18},{19... | collective-permute-start | bytes 3538952 | tf_op jit(solution)/shard_map/ppermute | solution.py:458
  11.3 6.1 %upward.1 = (bf16[8192,128]{1,0:T(8,128)(2,1)S(1)}, f32[16,128]{1,0:T(8,128)S(1)}, f32[16,128]{1,0:T(8,128)S(1)}, bf16[3584,128]{1,0:T(8,128)(2,1)S(1)}) custom-call(s32[1]{0:T(128)} %bitcast.4.me.where_am_i, bf16[8192,128]{1,0:T(8,128)(2,1)} %refs_3_.1, bf16[64,32,128]{2,1,0:T(8,128)(2,1)S(1)} %bitcast.17, bf16[32,32,255]{2,1,0:T(8,128)(2,1)S(1)} %bitcast.15), custom_call_target="tpu_custom_call" | custom-call | bytes 280000 | tf_op jit(solution)/shard_map/upward/pallas_call | solution.py:165
  17.4 1.3 %copy-done.6 = bf16[8192,128]{1,0:T(8,128)(2,1)} copy-done((bf16[8192,128]{1,0:T(8,128)(2,1)}, bf16[8192,128]{1,0:T(8,128)(2,1)S(1)}, u32[]{:S(2)}) %copy-start.6) | copy-done | bytes 2097176
  19.7 1.1 %collective-permute-done = f32[16,128]{1,0:T(8,128)S(1)} collective-permute-done((f32[16,128]{1,0:T(8,128)S(1)}, f32[16,128]{1,0:T(8,128)S(1)}, u32[]{:S(2)}, u32[]{:S(2)}) %collective-permute-start) | collective-permute-done | bytes 8224 | tf_op jit(solution)/shard_map/ppermute | solution.py:458
  21.0 4.0 %collective-permute-start.3 = (bf16[16,128]{1,0:T(8,128)(2,1)S(1)}, bf16[16,128]{1,0:T(8,128)(2,1)S(1)}, u32[]{:S(2)}, u32[]{:S(2)}) collective-permute-start(bf16[16,128]{1,0:T(8,128)(2,1)S(1)} %add_convert_fusion), channel_id=1, source_target_pairs={{0,4},{1,5},{2,6},{3,7},{4,0},{5,1},{6,2},{7,3},{8,12},{9,13},{10,... | collective-permute-start | bytes 12296 | tf_op jit(solution)/shard_map/ppermute | solution.py:458
  26.6 2.5 %collective-permute-start.6 = (bf16[64,128]{1,0:T(8,128)(2,1)S(1)}, bf16[64,128]{1,0:T(8,128)(2,1)S(1)}, u32[]{:S(2)}, u32[]{:S(2)}) collective-permute-start(bf16[64,128]{1,0:T(8,128)(2,1)S(1)} %pad_maximum_fusion), channel_id=1, source_target_pairs={{0,24},{1,25},{2,26},{3,27},{4,28},{5,29},{6,30},{7,31},{8,16},{9,... | collective-permute-start | bytes 49160 | tf_op jit(solution)/shard_map/ppermute | solution.py:458
  29.0 1.6 %collective-permute-start.7 = (bf16[64,128]{1,0:T(8,128)(2,1)S(1)}, bf16[64,128]{1,0:T(8,128)(2,1)S(1)}, u32[]{:S(2)}, u32[]{:S(2)}) collective-permute-start(bf16[64,128]{1,0:T(8,128)(2,1)S(1)} %pad_maximum_fusion), channel_id=1, source_target_pairs={{0,16},{1,17},{2,18},{3,19},{4,20},{5,21},{6,22},{7,23},{8,24},{9,... | collective-permute-start | bytes 49160 | tf_op jit(solution)/shard_map/ppermute | solution.py:458
  30.7 1.1 %collective-permute-done.6 = bf16[64,128]{1,0:T(8,128)(2,1)S(1)} collective-permute-done((bf16[64,128]{1,0:T(8,128)(2,1)S(1)}, bf16[64,128]{1,0:T(8,128)(2,1)S(1)}, u32[]{:S(2)}, u32[]{:S(2)}) %collective-permute-start.6) | collective-permute-done | bytes 16416 | tf_op jit(solution)/shard_map/ppermute | solution.py:458
  31.7 2.5 %collective-permute-done.7 = bf16[64,128]{1,0:T(8,128)(2,1)S(1)} collective-permute-done((bf16[64,128]{1,0:T(8,128)(2,1)S(1)}, bf16[64,128]{1,0:T(8,128)(2,1)S(1)}, u32[]{:S(2)}, u32[]{:S(2)}) %collective-permute-start.7) | collective-permute-done | bytes 16416 | tf_op jit(solution)/shard_map/ppermute | solution.py:458
  35.2 1.1 %collective-permute-start.9 = (bf16[256,128]{1,0:T(8,128)(2,1)S(1)}, bf16[256,128]{1,0:T(8,128)(2,1)S(1)}, u32[]{:S(2)}, u32[]{:S(2)}) collective-permute-start(bf16[256,128]{1,0:T(8,128)(2,1)S(1)} %get-tuple-element.29), channel_id=1, source_target_pairs={{0,96},{1,97},{2,98},{3,99},{4,100},{5,101},{6,102},{7,103},{8,104... | collective-permute-start | bytes 196616 | tf_op jit(solution)/shard_map/ppermute | solution.py:458
  36.3 2.1 %collective-permute-start.10 = (bf16[256,128]{1,0:T(8,128)(2,1)S(1)}, bf16[256,128]{1,0:T(8,128)(2,1)S(1)}, u32[]{:S(2)}, u32[]{:S(2)}) collective-permute-start(bf16[256,128]{1,0:T(8,128)(2,1)S(1)} %get-tuple-element.29), channel_id=1, source_target_pairs={{0,64},{1,65},{2,66},{3,67},{4,68},{5,69},{6,70},{7,71},{8,72},{9,... | collective-permute-start | bytes 196616 | tf_op jit(solution)/shard_map/ppermute | solution.py:458
  38.6 2.0 %collective-permute-done.9 = bf16[256,128]{1,0:T(8,128)(2,1)S(1)} collective-permute-done((bf16[256,128]{1,0:T(8,128)(2,1)S(1)}, bf16[256,128]{1,0:T(8,128)(2,1)S(1)}, u32[]{:S(2)}, u32[]{:S(2)}) %collective-permute-start.9) | collective-permute-done | bytes 65568 | tf_op jit(solution)/shard_map/ppermute | solution.py:458
  40.7 1.4 %collective-permute-done.10 = bf16[256,128]{1,0:T(8,128)(2,1)S(1)} collective-permute-done((bf16[256,128]{1,0:T(8,128)(2,1)S(1)}, bf16[256,128]{1,0:T(8,128)(2,1)S(1)}, u32[]{:S(2)}, u32[]{:S(2)}) %collective-permute-start.10) | collective-permute-done | bytes 65568 | tf_op jit(solution)/shard_map/ppermute | solution.py:458
  42.2 4.5 %collective-permute-start.13 = (bf16[8192,128]{1,0:T(8,128)(2,1)}, bf16[8192,128]{1,0:T(8,128)(2,1)S(1)}, u32[]{:S(2)}, u32[]{:S(2)}) collective-permute-start(bf16[8192,128]{1,0:T(8,128)(2,1)} %copy-done.6), channel_id=1, source_target_pairs={{1,2},{3,4},{5,6},{7,8},{9,10},{11,12},{13,14},{15,16},{17,18},{19... | collective-permute-start | bytes 6291464 | tf_op jit(solution)/shard_map/ppermute | solution.py:458
  46.8 1.6 %copy-done.4 = bf16[128,8,32,32]{0,3,2,1:T(8,128)(2,1)S(1)} copy-done((bf16[128,8,32,32]{0,3,2,1:T(8,128)(2,1)S(1)}, bf16[128,8,32,32]{0,3,2,1:T(8,128)(2,1)}, u32[]{:S(2)}) %copy-start.4) | copy-done | bytes 2097176
  48.4 4.2 %top.1.above = bf16[32,128]{1,0:T(8,128)(2,1)S(1)} custom-call(s32[1]{0:T(128)} %bitcast.4.me.where_am_i, s32[8,128]{1,0:T(8,128)S(1)} %bitcast.20, bf16[1024,128]{1,0:T(8,128)(2,1)S(1)} %constant_dynamic-update-slice_fusion.4.mine_in, bf16[1024,128]{1,0:T(8,128)(2,1)S(1)} %collective-permute-done.11.mate_in, bf16[32,32,128]{2,1,0:T(8,128)(2,1)S(1)} %bitcast.19, ...), custom_call_target="tpu_custom_call" | custom-call | bytes 160000 | tf_op jit(solution)/shard_map/top/pallas_call | solution.py:255
  53.2 5.4 %collective-permute-start.15 = (bf16[3584,128]{1,0:T(8,128)(2,1)S(1)}, bf16[3584,128]{1,0:T(8,128)(2,1)S(1)}, u32[]{:S(2)}, u32[]{:S(2)}) collective-permute-start(bf16[3584,128]{1,0:T(8,128)(2,1)S(1)} %copy-done.13), channel_id=1, source_target_pairs={{1,2},{3,4},{5,6},{7,8},{9,10},{11,12},{13,14},{15,16},{17,18},{19... | collective-permute-start | bytes 2752520 | tf_op jit(solution)/shard_map/ppermute | solution.py:458
  58.6 2.8 %copy-done.2 = bf16[128,6,64,64]{0,3,2,1:T(8,128)(2,1)S(1)} copy-done((bf16[128,6,64,64]{0,3,2,1:T(8,128)(2,1)S(1)}, bf16[128,6,64,64]{0,3,2,1:T(8,128)(2,1)}, u32[]{:S(2)}) %copy-start.2) | copy-done | bytes 6291480
  62.4 7.9 %near_turn.1.refs_2_ = bf16[128,64,416]{2,1,0:T(8,128)(2,1)S(1)} custom-call(bf16[6,64,64,128]{3,2,1,0:T(8,128)(2,1)S(1)} %bitcast.12, bf16[64,32,128]{2,1,0:T(8,128)(2,1)S(1)} %bitcast.18), custom_call_target="tpu_custom_call" | custom-call | bytes 320000 | tf_op jit(solution)/shard_map/near_turn/pallas_call | solution.py:92
  70.3 3.7 %collective-permute-done.13.other = bf16[8192,128]{1,0:T(8,128)(2,1)S(1)} collective-permute-done((bf16[8192,128]{1,0:T(8,128)(2,1)}, bf16[8192,128]{1,0:T(8,128)(2,1)S(1)}, u32[]{:S(2)}, u32[]{:S(2)}) %collective-permute-start.13) | collective-permute-done | bytes 2097184 | tf_op jit(solution)/shard_map/ppermute | solution.py:458
  74.0 11.0 %downward.1.refs_1_ = bf16[4096,128]{1,0:T(8,128)(2,1)S(1)} custom-call(s32[8,255]{1,0:T(8,128)S(1)} %select_bitcast_fusion.pos, bf16[8,32,32,255]{3,2,1,0:T(8,128)(2,1)S(1)} %bitcast.13, bf16[32,32,255]{2,1,0:T(8,128)(2,1)S(1)} %bitcast.16, bf16[8192,128]{1,0:T(8,128)(2,1)S(1)} %copy-done.7, bf16[8192,128]{1,0:T(8,128)(2,1)S(1)} %collective-permute-done.12.mate, ...), custom_call_target="tpu_custom_call" | custom-call | bytes 440000 | tf_op jit(solution)/shard_map/downward/pallas_call | solution.py:338
  85.0 7.6 %leaf_rows.1 = bf16[8192,128]{1,0:T(8,128)(2,1)} custom-call(s32[6,128]{1,0:T(8,128)S(1)} %select_bitcast_fusion.1.refs_0_, bf16[4096,128]{1,0:T(8,128)(2,1)S(1)} %downward.1.refs_1_, bf16[128,64,416]{2,1,0:T(8,128)(2,1)S(1)} %near_turn.1.refs_2_, bf16[8192,128]{1,0:T(8,128)(2,1)S(1)} %copy-done.1, bf16[8192,128]{1,0:T(8,128)(2,1)} %collective-permute-done.14.refs_4_, ...), custom_call_target="tpu_custom_call" | custom-call | bytes 240000 | tf_op jit(solution)/shard_map/leaf_rows/pallas_call | solution.py:389
  (63 shorter events, 5.6 us)
Async XLA Ops:
  3.0 16.7 %copy-start.14 = (s32[255,8]{0,1:T(8,128)S(1)}, s32[255,8]{0,1:T(8,128)}, u32[]{:S(2)}) copy-start(s32[255,8]{0,1:T(8,128)} %param.17) | copy-start | bytes 24484
  3.0 16.7 %copy-start.16 = (s32[255]{0:T(256)S(1)}, s32[255]{0:T(256)}, u32[]{:S(2)}) copy-start(s32[255]{0:T(256)} %constant.40) | copy-start | bytes 3064
  3.0 16.7 %copy-start.17 = (s32[255]{0:T(256)S(1)}, s32[255]{0:T(256)}, u32[]{:S(2)}) copy-start(s32[255]{0:T(256)} %constant.41) | copy-start | bytes 3064
  3.0 16.7 %copy-start.18 = (s32[255]{0:T(256)S(1)}, s32[255]{0:T(256)}, u32[]{:S(2)}) copy-start(s32[255]{0:T(256)} %constant.44) | copy-start | bytes 3064
  3.0 22.0 %copy-start.15 = (s32[128,6]{0,1:T(8,128)S(1)}, s32[128,6]{0,1:T(8,128)}, u32[]{:S(2)}) copy-start(s32[128,6]{0,1:T(8,128)} %param.21) | copy-start | bytes 9220
  3.0 43.7 %copy-start.10 = (bf16[128,32,32]{0,2,1:T(8,128)(2,1)S(1)}, bf16[128,32,32]{0,2,1:T(8,128)(2,1)}, u32[]{:S(2)}) copy-start(bf16[128,32,32]{0,2,1:T(8,128)(2,1)} %param.15) | copy-start | bytes 786436
  3.0 43.7 %copy-start.11 = (s32[128,8]{0,1:T(8,128)S(1)}, s32[128,8]{0,1:T(8,128)}, u32[]{:S(2)}) copy-start(s32[128,8]{0,1:T(8,128)} %param.19) | copy-start | bytes 12292
  3.0 23.5 %collective-permute-start.4 = (bf16[4608,128]{1,0:T(8,128)(2,1)}, bf16[4608,128]{1,0:T(8,128)(2,1)}, u32[]{:S(2)}, u32[]{:S(2)}) collective-permute-start(bf16[4608,128]{1,0:T(8,128)(2,1)} %head.1), channel_id=1, source_target_pairs={{1,2},{3,4},{5,6},{7,8},{9,10},{11,12},{13,14},{15,16},{17,18},{19... | collective-permute-start | bytes 3538952 | tf_op jit(solution)/shard_map/ppermute | solution.py:458
  19.7 33.0 %copy-start.1 = (bf16[8192,128]{1,0:T(8,128)(2,1)S(1)}, bf16[8192,128]{1,0:T(8,128)(2,1)}, u32[]{:S(2)}) copy-start(bf16[8192,128]{1,0:T(8,128)(2,1)} %refs_3_.1) | copy-start | bytes 6291460
  19.7 1.2 %collective-permute-start = (f32[16,128]{1,0:T(8,128)S(1)}, f32[16,128]{1,0:T(8,128)S(1)}, u32[]{:S(2)}, u32[]{:S(2)}) collective-permute-start(f32[16,128]{1,0:T(8,128)S(1)} %get-tuple-element.20), channel_id=1, source_target_pairs={{0,1},{1,0},{2,3},{3,2},{4,5},{5,4},{6,7},{7,6},{8,9},{9,8},{10,11... | collective-permute-start | bytes 24584 | tf_op jit(solution)/shard_map/ppermute | solution.py:458
  20.9 4.1 %collective-permute-start.1 = (bf16[16,128]{1,0:T(8,128)(2,1)S(1)}, bf16[16,128]{1,0:T(8,128)(2,1)S(1)}, u32[]{:S(2)}, u32[]{:S(2)}) collective-permute-start(bf16[16,128]{1,0:T(8,128)(2,1)S(1)} %add_convert_fusion), channel_id=1, source_target_pairs={{0,2},{1,3},{2,0},{3,1},{4,6},{5,7},{6,4},{7,5},{8,10},{9,11},{10,... | collective-permute-start | bytes 12296 | tf_op jit(solution)/shard_map/ppermute | solution.py:458
  20.9 4.9 %collective-permute-start.2 = (bf16[16,128]{1,0:T(8,128)(2,1)S(1)}, bf16[16,128]{1,0:T(8,128)(2,1)S(1)}, u32[]{:S(2)}, u32[]{:S(2)}) collective-permute-start(bf16[16,128]{1,0:T(8,128)(2,1)S(1)} %add_convert_fusion), channel_id=1, source_target_pairs={{0,6},{1,7},{2,4},{3,5},{4,2},{5,3},{6,0},{7,1},{8,14},{9,15},{10,... | collective-permute-start | bytes 12296 | tf_op jit(solution)/shard_map/ppermute | solution.py:458
  21.0 5.6 %collective-permute-start.3 = (bf16[16,128]{1,0:T(8,128)(2,1)S(1)}, bf16[16,128]{1,0:T(8,128)(2,1)S(1)}, u32[]{:S(2)}, u32[]{:S(2)}) collective-permute-start(bf16[16,128]{1,0:T(8,128)(2,1)S(1)} %add_convert_fusion), channel_id=1, source_target_pairs={{0,4},{1,5},{2,6},{3,7},{4,0},{5,1},{6,2},{7,3},{8,12},{9,13},{10,... | collective-permute-start | bytes 12296 | tf_op jit(solution)/shard_map/ppermute | solution.py:458
  26.5 4.1 %collective-permute-start.5 = (bf16[64,128]{1,0:T(8,128)(2,1)S(1)}, bf16[64,128]{1,0:T(8,128)(2,1)S(1)}, u32[]{:S(2)}, u32[]{:S(2)}) collective-permute-start(bf16[64,128]{1,0:T(8,128)(2,1)S(1)} %pad_maximum_fusion), channel_id=1, source_target_pairs={{0,8},{1,9},{2,10},{3,11},{4,12},{5,13},{6,14},{7,15},{8,0},{9,1},... | collective-permute-start | bytes 49160 | tf_op jit(solution)/shard_map/ppermute | solution.py:458
  26.6 5.2 %collective-permute-start.6 = (bf16[64,128]{1,0:T(8,128)(2,1)S(1)}, bf16[64,128]{1,0:T(8,128)(2,1)S(1)}, u32[]{:S(2)}, u32[]{:S(2)}) collective-permute-start(bf16[64,128]{1,0:T(8,128)(2,1)S(1)} %pad_maximum_fusion), channel_id=1, source_target_pairs={{0,24},{1,25},{2,26},{3,27},{4,28},{5,29},{6,30},{7,31},{8,16},{9,... | collective-permute-start | bytes 49160 | tf_op jit(solution)/shard_map/ppermute | solution.py:458
  29.0 5.2 %collective-permute-start.7 = (bf16[64,128]{1,0:T(8,128)(2,1)S(1)}, bf16[64,128]{1,0:T(8,128)(2,1)S(1)}, u32[]{:S(2)}, u32[]{:S(2)}) collective-permute-start(bf16[64,128]{1,0:T(8,128)(2,1)S(1)} %pad_maximum_fusion), channel_id=1, source_target_pairs={{0,16},{1,17},{2,18},{3,19},{4,20},{5,21},{6,22},{7,23},{8,24},{9,... | collective-permute-start | bytes 49160 | tf_op jit(solution)/shard_map/ppermute | solution.py:458
  34.3 4.3 %collective-permute-start.8 = (bf16[256,128]{1,0:T(8,128)(2,1)S(1)}, bf16[256,128]{1,0:T(8,128)(2,1)S(1)}, u32[]{:S(2)}, u32[]{:S(2)}) collective-permute-start(bf16[256,128]{1,0:T(8,128)(2,1)S(1)} %get-tuple-element.29), channel_id=1, source_target_pairs={{0,32},{1,33},{2,34},{3,35},{4,36},{5,37},{6,38},{7,39},{8,40},{9,... | collective-permute-start | bytes 196616 | tf_op jit(solution)/shard_map/ppermute | solution.py:458
  35.2 5.5 %collective-permute-start.9 = (bf16[256,128]{1,0:T(8,128)(2,1)S(1)}, bf16[256,128]{1,0:T(8,128)(2,1)S(1)}, u32[]{:S(2)}, u32[]{:S(2)}) collective-permute-start(bf16[256,128]{1,0:T(8,128)(2,1)S(1)} %get-tuple-element.29), channel_id=1, source_target_pairs={{0,96},{1,97},{2,98},{3,99},{4,100},{5,101},{6,102},{7,103},{8,104... | collective-permute-start | bytes 196616 | tf_op jit(solution)/shard_map/ppermute | solution.py:458
  36.3 5.8 %collective-permute-start.10 = (bf16[256,128]{1,0:T(8,128)(2,1)S(1)}, bf16[256,128]{1,0:T(8,128)(2,1)S(1)}, u32[]{:S(2)}, u32[]{:S(2)}) collective-permute-start(bf16[256,128]{1,0:T(8,128)(2,1)S(1)} %get-tuple-element.29), channel_id=1, source_target_pairs={{0,64},{1,65},{2,66},{3,67},{4,68},{5,69},{6,70},{7,71},{8,72},{9,... | collective-permute-start | bytes 196616 | tf_op jit(solution)/shard_map/ppermute | solution.py:458
  42.1 4.6 %collective-permute-start.11 = (bf16[1024,128]{1,0:T(8,128)(2,1)S(1)}, bf16[1024,128]{1,0:T(8,128)(2,1)S(1)}, u32[]{:S(2)}, u32[]{:S(2)}) collective-permute-start(bf16[1024,128]{1,0:T(8,128)(2,1)S(1)} %constant_dynamic-update-slice_fusion.4.mine_in), channel_id=1, source_target_pairs={{0,1},{1,0},{2,3},{3,2},{4,5},{5,4},{6,7},{7,6},{8,9},{9,8},{10,11... | collective-permute-start | bytes 786440 | tf_op jit(solution)/shard_map/ppermute | solution.py:458
  42.2 31.8 %collective-permute-start.13 = (bf16[8192,128]{1,0:T(8,128)(2,1)}, bf16[8192,128]{1,0:T(8,128)(2,1)S(1)}, u32[]{:S(2)}, u32[]{:S(2)}) collective-permute-start(bf16[8192,128]{1,0:T(8,128)(2,1)} %copy-done.6), channel_id=1, source_target_pairs={{1,2},{3,4},{5,6},{7,8},{9,10},{11,12},{13,14},{15,16},{17,18},{19... | collective-permute-start | bytes 6291464 | tf_op jit(solution)/shard_map/ppermute | solution.py:458
  52.6 21.4 %collective-permute-start.12 = (bf16[8192,128]{1,0:T(8,128)(2,1)}, bf16[8192,128]{1,0:T(8,128)(2,1)S(1)}, u32[]{:S(2)}, u32[]{:S(2)}) collective-permute-start(bf16[8192,128]{1,0:T(8,128)(2,1)} %copy-done.6), channel_id=1, source_target_pairs={{0,1},{1,0},{2,3},{3,2},{4,5},{5,4},{6,7},{7,6},{8,9},{9,8},{10,11... | collective-permute-start | bytes 6291464 | tf_op jit(solution)/shard_map/ppermute | solution.py:458
  52.7 32.3 %collective-permute-start.14 = (bf16[8192,128]{1,0:T(8,128)(2,1)S(1)}, bf16[8192,128]{1,0:T(8,128)(2,1)}, u32[]{:S(2)}, u32[]{:S(2)}) collective-permute-start(bf16[8192,128]{1,0:T(8,128)(2,1)S(1)} %copy-done.1), channel_id=1, source_target_pairs={{0,1},{1,0},{2,3},{3,2},{4,5},{5,4},{6,7},{7,6},{8,9},{9,8},{10,11... | collective-permute-start | bytes 6291464 | tf_op jit(solution)/shard_map/ppermute | solution.py:458
  53.2 31.8 %collective-permute-start.15 = (bf16[3584,128]{1,0:T(8,128)(2,1)S(1)}, bf16[3584,128]{1,0:T(8,128)(2,1)S(1)}, u32[]{:S(2)}, u32[]{:S(2)}) collective-permute-start(bf16[3584,128]{1,0:T(8,128)(2,1)S(1)} %copy-done.13), channel_id=1, source_target_pairs={{1,2},{3,4},{5,6},{7,8},{9,10},{11,12},{13,14},{15,16},{17,18},{19... | collective-permute-start | bytes 2752520 | tf_op jit(solution)/shard_map/ppermute | solution.py:458
  (11 other events, 56.7 us)
